TPU v7x, 512 devices: a whole 4x8x8 slice. The times are simulated.
512 devices in a mesh: row: 64 (over y, z), col: 8 (over x, core).
Axes of the slice: x: 4, y: 8, z: 8, core: 2. Of those that a mesh axis runs over, the one named last changes fastest.
Arguments:
- features: bfloat16 [65536, 512], P(('row', 'col')), may hold values from -6 to 6
- weight: bfloat16 [512, 512], replicated, may hold values from -0.25 to 0.25
- bias_vec: float32 [512], replicated, may hold values from -3 to 3
- tile_vals: bfloat16 [64, 8, 16, 128, 128], P('row', 'col'), may hold values from -0.1875 to 0.1875
- tile_coords: int32 [64, 8, 16, 2], P('row', 'col'), may hold values from 0 to 63, as said below
- tile_count: int32 [64, 8], P('row', 'col'), may hold values from 2 to 16, as said below
- cotangent: bfloat16 [65536, 512], P(('row', 'col')), may hold values from -6 to 6
Outputs:
- layer_out: bfloat16 [65536, 512], P(('row', 'col'))
- grad_weight: float32 [512, 512], replicated
- grad_bias: float32 [512], replicated
- grad_features: bfloat16 [65536, 512], P(('row', 'col'))
Inputs may be any that keep to these rules, and one draw needn't show every extreme that they name: tile_coords[r, c, s, 0] is below 8; tile_coords[r, c, s, 1] lies in the row bands r - 3 to r + 3 that exist. `tile_count`: some device has all 16 slots live.
All inputs are finite; a program needn't handle non-finite values.
Results may differ from a plain program's by a relative error of at most 0.019.
Values may be sent and summed in bfloat16 or wider, within the bound.
No kernel may reach another device: no remote copies, remote signals or barrier semaphores. Data moves between devices by JAX's collectives and lax.ppermute only.
A program may use at most 64 MiB of HBM per device.

v0:
```python
import jax
import jax.numpy as jnp
from jax import lax
from jax.sharding import PartitionSpec as P

REACH = 3


def passed_along(block, axis, distance):
    devices = range(lax.axis_size(axis))
    route = [(i - distance, i) for i in devices if i - distance in devices]
    return lax.ppermute(block, axis, route)


def gelu_tanh(values):
    return jax.nn.gelu(values, approximate=True)


def body(features, weight, bias_vec, tile_vals, tile_coords, tile_count, cotangent):
    col_count = lax.axis_size("col")
    own_row = lax.axis_index("row")
    tiles_here = tile_vals[0, 0]
    coords_here = tile_coords[0, 0]
    live_count = tile_count[0, 0]
    slot_count = tiles_here.shape[0]
    tile_size = features.shape[0]
    feat_width = features.shape[1]
    window = 2 * REACH + 1
    per_step = 8
    row_local = coords_here[:, 0]
    col_local = coords_here[:, 1]
    alive_mask = (jnp.arange(slot_count, dtype=jnp.int32) < live_count).astype(jnp.float32)
    window_index = col_local - own_row + REACH
    nearby = []
    for shift_by in range(-REACH, REACH + 1):
        if shift_by == 0:
            nearby.append(features)
        else:
            nearby.append(passed_along(features, "row", -shift_by))
    panels = jnp.stack(nearby)
    step_total = slot_count // per_step

    def slot_slices(group_idx):
        first_slot = group_idx * per_step
        tiles_now = lax.dynamic_slice_in_dim(tiles_here, first_slot, per_step, 0)
        alive_now = lax.dynamic_slice_in_dim(alive_mask, first_slot, per_step, 0)
        return (first_slot, tiles_now, alive_now)

    def forward_group(group_idx, totals):
        first_slot, tiles_now, alive_now = slot_slices(group_idx)
        col_pick = lax.dynamic_slice_in_dim(window_index, first_slot, per_step, 0)
        row_pick = lax.dynamic_slice_in_dim(row_local, first_slot, per_step, 0)
        picked = panels[col_pick]
        product = jnp.einsum("gij,gjf->gif", tiles_now, picked, preferred_element_type=jnp.float32)
        onehot = (row_pick[:, None] == jnp.arange(col_count, dtype=jnp.int32)[None, :]).astype(
            jnp.float32
        )
        onehot = onehot * alive_now[:, None]
        return totals + jnp.einsum("gb,gif->bif", onehot, product)

    partial_value = lax.fori_loop(
        0, step_total, forward_group, jnp.zeros((col_count, tile_size, feat_width), jnp.float32)
    )
    aggregate = lax.psum_scatter(
        partial_value.reshape(col_count * tile_size, feat_width),
        "col",
        scatter_dimension=0,
        tiled=True,
    )
    aggregate_b = aggregate.astype(jnp.bfloat16)
    pre_act = jnp.dot(aggregate_b, weight, preferred_element_type=jnp.float32) + bias_vec
    layer_out = gelu_tanh(pre_act).astype(jnp.bfloat16)
    unused_out, pullback = jax.vjp(gelu_tanh, pre_act)
    grad_pre = pullback(cotangent.astype(jnp.float32))[0].astype(jnp.bfloat16)
    weight_term = jnp.einsum("nf,ng->fg", aggregate_b, grad_pre, preferred_element_type=jnp.float32)
    bias_term = jnp.sum(grad_pre.astype(jnp.float32), axis=0)
    grad_weight, grad_bias = lax.psum((weight_term, bias_term), ("row", "col"))
    grad_mid = jnp.einsum("ng,fg->nf", grad_pre, weight, preferred_element_type=jnp.float32).astype(
        jnp.bfloat16
    )
    band_panels = lax.all_gather(grad_mid, "col", axis=0, tiled=True).reshape(
        col_count, tile_size, feat_width
    )

    def backward_group(group_idx, totals):
        first_slot, tiles_now, alive_now = slot_slices(group_idx)
        row_pick = lax.dynamic_slice_in_dim(row_local, first_slot, per_step, 0)
        win_pick = lax.dynamic_slice_in_dim(window_index, first_slot, per_step, 0)
        picked = band_panels[row_pick]
        product = jnp.einsum("gji,gjf->gif", tiles_now, picked, preferred_element_type=jnp.float32)
        onehot = (win_pick[:, None] == jnp.arange(window, dtype=jnp.int32)[None, :]).astype(
            jnp.float32
        )
        onehot = onehot * alive_now[:, None]
        return totals + jnp.einsum("gb,gif->bif", onehot, product)

    grad_acc = lax.fori_loop(
        0, step_total, backward_group, jnp.zeros((window, tile_size, feat_width), jnp.float32)
    )
    result_sum = grad_acc[REACH]
    for shift_by in range(-REACH, REACH + 1):
        if shift_by != 0:
            result_sum = result_sum + passed_along(grad_acc[shift_by + REACH], "row", shift_by)
    grad_features = result_sum.astype(jnp.bfloat16)
    return (layer_out, grad_weight, grad_bias, grad_features)


def solution(mesh):
    return jax.shard_map(
        body,
        mesh=mesh,
        in_specs=(
            P(("row", "col"), None),
            P(),
            P(),
            P("row", "col", None, None, None),
            P("row", "col", None, None),
            P("row", "col"),
            P(("row", "col"), None),
        ),
        out_specs=(P(("row", "col"), None), P(), P(), P(("row", "col"), None)),
        check_vma=False,
    )
```

profile of v0, /device:TPU:1, one launch (start us, length us, event | category | flops | bytes accessed | tf_op | source)
XLA Modules:
  0.0 473.2 jit_solution(12974934062237815644)
XLA Ops:
  7.2 8.6 %collective-permute-start = (bf16[128,512]{1,0:T(8,128)(2,1)}, bf16[128,512]{1,0:T(8,128)(2,1)S(1)}, u32[]{:S(2)}, u32[]{:S(2)}) collective-permute-start(bf16[128,512]{1,0:T(8,128)(2,1)} %param.11), channel_id=1, source_target_pairs={{0,24},{8,32},{16,40},{24,48},{32,56},{40,64},{48,72},{56,80},{64,... | collective-permute-start | bytes 393224 | tf_op jit(solution)/shard_map/ppermute | solution.py:12
  15.8 6.1 %collective-permute-start.1 = (bf16[128,512]{1,0:T(8,128)(2,1)}, bf16[128,512]{1,0:T(8,128)(2,1)S(1)}, u32[]{:S(2)}, u32[]{:S(2)}) collective-permute-start(bf16[128,512]{1,0:T(8,128)(2,1)} %param.11), channel_id=1, source_target_pairs={{0,16},{8,24},{16,32},{24,40},{32,48},{40,56},{48,64},{56,72},{64,... | collective-permute-start | bytes 393224 | tf_op jit(solution)/shard_map/ppermute | solution.py:12
  22.0 3.1 collective-permute-start.2
  25.1 1.3 collective-permute-start.3
  26.4 1.3 collective-permute-start.4
  29.1 1.3 collective-permute-start.5
  31.4 6.2 %collective-permute-done.4 = bf16[128,512]{1,0:T(8,128)(2,1)S(1)} collective-permute-done((bf16[128,512]{1,0:T(8,128)(2,1)}, bf16[128,512]{1,0:T(8,128)(2,1)S(1)}, u32[]{:S(2)}, u32[]{:S(2)}) %collective-permute-start.4) | collective-permute-done | bytes 131104 | tf_op jit(solution)/shard_map/ppermute | solution.py:12
  37.6 13.1 %collective-permute-done.5 = bf16[128,512]{1,0:T(8,128)(2,1)S(1)} collective-permute-done((bf16[128,512]{1,0:T(8,128)(2,1)}, bf16[128,512]{1,0:T(8,128)(2,1)S(1)}, u32[]{:S(2)}, u32[]{:S(2)}) %collective-permute-start.5) | collective-permute-done | bytes 131104 | tf_op jit(solution)/shard_map/ppermute | solution.py:12
  50.7 10.3 %while.28 = (s32[]{:T(128)}, f32[8,128,512]{2,0,1:T(8,128)}, s32[16]{0:T(128)S(1)}, bf16[16]{0:T(256)(128)(2,1)S(1)}, bf16[16,128,128]{2,1,0:T(8,128)(2,1)}, /*i...) while((s32[]{:T(128)}, f32[8,128,512]{2,0,1:T(8,128)}, ...), condition=%wide.region_1.0_spmd.clone, body=%wide.region_0.0_spmd.clone.sunk | while | flops 143656096 | bytes 9703877 | solution.py:61
  51.4 1.4 fusion.67
  53.0 2.1 select_add_fusion.4
  55.7 1.4 fusion.67
  57.3 3.7 select_add_fusion.4
  61.0 4.1 copy.18
  65.2 34.3 %reduce-scatter.2.cloned.1.call-done = f32[128,512]{1,0:T(8,128)} async-done(((f32[1024,512]{1,0:T(8,128)}), f32[128,512]{1,0:T(8,128)}) %reduce-scatter.2.cloned.1.call-update) | async-done | bytes 262160 | tf_op jit(solution)/shard_map/reduce_scatter | solution.py:64
  99.5 2.0 convert_reduce_fusion
  102.5 29.9 %all-gather.2.cloned.1.call-done = bf16[1024,512]{1,0:T(8,128)(2,1)} async-done(((bf16[128,512]{1,0:T(8,128)(2,1)}), bf16[1024,512]{1,0:T(8,128)(2,1)}) %all-gather.2.cloned.1.call-update) | async-done | bytes 1048592 | tf_op jit(solution)/shard_map/all_gather | solution.py:81
  132.5 11.0 %while.29 = (s32[]{:T(128)}, f32[7,128,512]{2,0,1:T(8,128)}, s32[16]{0:T(128)S(1)}, bf16[16]{0:T(256)(128)(2,1)S(1)}, bf16[16,128,128]{2,1,0:T(8,128)(2,1)S(1)},...) while((s32[]{:T(128)}, f32[7,128,512]{2,0,1:T(8,128)}, ...), condition=%wide.region_7.0_spmd.clone, body=%wide.region_6.0_spmd.clone.sunk | while | flops 142476432 | bytes 9179589 | solution.py:97
  132.6 1.8 gather_fusion.1
  135.1 2.1 select_add_fusion.5
  137.3 1.8 gather_fusion.1
  139.8 3.7 select_add_fusion.5
  143.5 2.7 copy.19
  147.1 4.2 collective-permute-start.10
  151.3 5.7 %collective-permute-start.11 = (f32[128,512]{1,0:T(8,128)}, f32[128,512]{1,0:T(8,128)S(1)}, u32[]{:S(2)}, u32[]{:S(2)}) collective-permute-start(f32[128,512]{1,0:T(8,128)} %get-tuple-element.333), channel_id=1, source_target_pairs={{0,24},{8,32},{16,40},{24,48},{32,56},{40,64},{48,72},{56,80},{64,... | collective-permute-start | bytes 786440 | tf_op jit(solution)/shard_map/ppermute | solution.py:12
  157.1 1.3 collective-permute-start.6
  161.0 11.4 %collective-permute-start.9 = (f32[128,512]{1,0:T(8,128)S(1)}, f32[128,512]{1,0:T(8,128)}, u32[]{:S(2)}, u32[]{:S(2)}) collective-permute-start(f32[128,512]{1,0:T(8,128)S(1)} %get-tuple-element.335), channel_id=1, source_target_pairs={{0,8},{8,16},{16,24},{24,32},{32,40},{40,48},{48,56},{56,64},{64,7... | collective-permute-start | bytes 786440 | tf_op jit(solution)/shard_map/ppermute | solution.py:12
  172.5 1.3 fusion.43
  173.8 122.9 %psum.15 = f32[512]{0:T(512)} all-reduce(f32[512]{0:T(512)S(1)} %get-tuple-element.330), channel_id=1, replica_groups=mesh['row'=64,'col'=8] {'row','col'}, use_global_device_ids=true, to_apply=%region_5.0 | all-reduce | flops 512 | bytes 4096 | tf_op jit(solution)/shard_map/psum | solution.py:77
  296.7 2.0 fusion.42
  298.7 165.7 %all-reduce.2.cloned.1.call-done = f32[512,512]{1,0:T(8,128)} async-done(((f32[512,512]{1,0:T(8,128)}), f32[512,512]{1,0:T(8,128)}) %all-reduce.2.cloned.1.call-update) | async-done | bytes 1048592 | tf_op jit(solution)/shard_map/psum | solution.py:77
  464.4 2.3 copy.60
  (61 shorter events, 9.6 us)
Async XLA Ops:
  7.2 92.3 %copy-start = (bf16[512,512]{1,0:T(8,128)(2,1)S(1)}, bf16[512,512]{1,0:T(8,128)(2,1)}, u32[]{:S(2)}) copy-start(bf16[512,512]{1,0:T(8,128)(2,1)} %param.12) | copy-start | bytes 1572868
  7.2 92.3 %reduce-scatter.2.cloned.1.call-start = ((), (), s32[]{:S(2)}) async-start(), calls=%async_computation.1 | async-start | bytes 2359296 | tf_op jit(solution)/shard_map/reduce_scatter | solution.py:64
  7.2 21.9 %collective-permute-start = (bf16[128,512]{1,0:T(8,128)(2,1)}, bf16[128,512]{1,0:T(8,128)(2,1)S(1)}, u32[]{:S(2)}, u32[]{:S(2)}) collective-permute-start(bf16[128,512]{1,0:T(8,128)(2,1)} %param.11), channel_id=1, source_target_pairs={{0,24},{8,32},{16,40},{24,48},{32,56},{40,64},{48,72},{56,80},{64,... | collective-permute-start | bytes 393224 | tf_op jit(solution)/shard_map/ppermute | solution.py:12
  15.8 14.6 %collective-permute-start.1 = (bf16[128,512]{1,0:T(8,128)(2,1)}, bf16[128,512]{1,0:T(8,128)(2,1)S(1)}, u32[]{:S(2)}, u32[]{:S(2)}) collective-permute-start(bf16[128,512]{1,0:T(8,128)(2,1)} %param.11), channel_id=1, source_target_pairs={{0,16},{8,24},{16,32},{24,40},{32,48},{40,56},{48,64},{56,72},{64,... | collective-permute-start | bytes 393224 | tf_op jit(solution)/shard_map/ppermute | solution.py:12
  22.0 8.5 %collective-permute-start.2 = (bf16[128,512]{1,0:T(8,128)(2,1)}, bf16[128,512]{1,0:T(8,128)(2,1)S(1)}, u32[]{:S(2)}, u32[]{:S(2)}) collective-permute-start(bf16[128,512]{1,0:T(8,128)(2,1)} %param.11), channel_id=1, source_target_pairs={{0,8},{8,16},{16,24},{24,32},{32,40},{40,48},{48,56},{56,64},{64,7... | collective-permute-start | bytes 393224 | tf_op jit(solution)/shard_map/ppermute | solution.py:12
  25.1 6.3 %collective-permute-start.3 = (bf16[128,512]{1,0:T(8,128)(2,1)}, bf16[128,512]{1,0:T(8,128)(2,1)S(1)}, u32[]{:S(2)}, u32[]{:S(2)}) collective-permute-start(bf16[128,512]{1,0:T(8,128)(2,1)} %param.11), channel_id=1, source_target_pairs={{8,0},{16,8},{24,16},{32,24},{40,32},{48,40},{56,48},{64,56},{72,6... | collective-permute-start | bytes 393224 | tf_op jit(solution)/shard_map/ppermute | solution.py:12
  26.4 11.2 %collective-permute-start.4 = (bf16[128,512]{1,0:T(8,128)(2,1)}, bf16[128,512]{1,0:T(8,128)(2,1)S(1)}, u32[]{:S(2)}, u32[]{:S(2)}) collective-permute-start(bf16[128,512]{1,0:T(8,128)(2,1)} %param.11), channel_id=1, source_target_pairs={{16,0},{24,8},{32,16},{40,24},{48,32},{56,40},{64,48},{72,56},{80,... | collective-permute-start | bytes 393224 | tf_op jit(solution)/shard_map/ppermute | solution.py:12
  29.1 21.6 %collective-permute-start.5 = (bf16[128,512]{1,0:T(8,128)(2,1)}, bf16[128,512]{1,0:T(8,128)(2,1)S(1)}, u32[]{:S(2)}, u32[]{:S(2)}) collective-permute-start(bf16[128,512]{1,0:T(8,128)(2,1)} %param.11), channel_id=1, source_target_pairs={{24,0},{32,8},{40,16},{48,24},{56,32},{64,40},{72,48},{80,56},{88,... | collective-permute-start | bytes 393224 | tf_op jit(solution)/shard_map/ppermute | solution.py:12
  65.1 34.4 %copy-start.3 = (bf16[128,512]{1,0:T(8,128)(2,1)S(1)}, bf16[128,512]{1,0:T(8,128)(2,1)}, u32[]{:S(2)}) copy-start(bf16[128,512]{1,0:T(8,128)(2,1)} %param.17) | copy-start | bytes 393220
  65.1 34.4 %copy-start.4 = (f32[512]{0:T(512)S(1)}, f32[512]{0:T(512)}, u32[]{:S(2)}) copy-start(f32[512]{0:T(512)} %param.13) | copy-start | bytes 6148
  65.1 67.4 %copy-start.1 = (bf16[16,128,128]{2,1,0:T(8,128)(2,1)S(1)}, bf16[16,128,128]{2,1,0:T(8,128)(2,1)}, u32[]{:S(2)}) copy-start(bf16[16,128,128]{2,1,0:T(8,128)(2,1)} %get-tuple-element.501) | copy-start | bytes 1572868
  65.1 67.4 %all-gather.2.cloned.1.call-start = ((), (), s32[]{:S(2)}) async-start(), calls=%async_computation.3 | async-start | bytes 1179648 | tf_op jit(solution)/shard_map/all_gather | solution.py:81
  102.5 361.9 %all-reduce.2.cloned.1.call-start = ((), (), s32[]{:S(2)}) async-start(), calls=%async_computation.2 | async-start | bytes 2097152 | tf_op jit(solution)/shard_map/psum | solution.py:77
  146.2 26.3 %copy-start.2 = (f32[128,512]{1,0:T(8,128)S(1)}, f32[128,512]{1,0:T(8,128)}, u32[]{:S(2)}) copy-start(f32[128,512]{1,0:T(8,128)} %reduce-scatter.2.cloned.1.call-done) | copy-start | bytes 786436
  147.1 13.9 %collective-permute-start.10 = (f32[128,512]{1,0:T(8,128)S(1)}, f32[128,512]{1,0:T(8,128)S(1)}, u32[]{:S(2)}, u32[]{:S(2)}) collective-permute-start(f32[128,512]{1,0:T(8,128)S(1)} %get-tuple-element.334), channel_id=1, source_target_pairs={{0,16},{8,24},{16,32},{24,40},{32,48},{40,56},{48,64},{56,72},{64,... | collective-permute-start | bytes 786440 | tf_op jit(solution)/shard_map/ppermute | solution.py:12
  151.3 145.3 %collective-permute-start.11 = (f32[128,512]{1,0:T(8,128)}, f32[128,512]{1,0:T(8,128)S(1)}, u32[]{:S(2)}, u32[]{:S(2)}) collective-permute-start(f32[128,512]{1,0:T(8,128)} %get-tuple-element.333), channel_id=1, source_target_pairs={{0,24},{8,32},{16,40},{24,48},{32,56},{40,64},{48,72},{56,80},{64,... | collective-permute-start | bytes 786440 | tf_op jit(solution)/shard_map/ppermute | solution.py:12
  157.1 139.5 %collective-permute-start.6 = (f32[128,512]{1,0:T(8,128)}, f32[128,512]{1,0:T(8,128)}, u32[]{:S(2)}, u32[]{:S(2)}) collective-permute-start(f32[128,512]{1,0:T(8,128)} %get-tuple-element.332), channel_id=1, source_target_pairs={{24,0},{32,8},{40,16},{48,24},{56,32},{64,40},{72,48},{80,56},{88,... | collective-permute-start | bytes 786440 | tf_op jit(solution)/shard_map/ppermute | solution.py:12
  158.4 138.2 %collective-permute-start.7 = (f32[128,512]{1,0:T(8,128)}, f32[128,512]{1,0:T(8,128)}, u32[]{:S(2)}, u32[]{:S(2)}) collective-permute-start(f32[128,512]{1,0:T(8,128)} %get-tuple-element.337), channel_id=1, source_target_pairs={{16,0},{24,8},{32,16},{40,24},{48,32},{56,40},{64,48},{72,56},{80,... | collective-permute-start | bytes 786440 | tf_op jit(solution)/shard_map/ppermute | solution.py:12
  159.7 136.9 %collective-permute-start.8 = (f32[128,512]{1,0:T(8,128)S(1)}, f32[128,512]{1,0:T(8,128)}, u32[]{:S(2)}, u32[]{:S(2)}) collective-permute-start(f32[128,512]{1,0:T(8,128)S(1)} %get-tuple-element.336), channel_id=1, source_target_pairs={{8,0},{16,8},{24,16},{32,24},{40,32},{48,40},{56,48},{64,56},{72,6... | collective-permute-start | bytes 786440 | tf_op jit(solution)/shard_map/ppermute | solution.py:12
  161.0 135.6 %collective-permute-start.9 = (f32[128,512]{1,0:T(8,128)S(1)}, f32[128,512]{1,0:T(8,128)}, u32[]{:S(2)}, u32[]{:S(2)}) collective-permute-start(f32[128,512]{1,0:T(8,128)S(1)} %get-tuple-element.335), channel_id=1, source_target_pairs={{0,8},{8,16},{16,24},{24,32},{32,40},{40,48},{48,56},{56,64},{64,7... | collective-permute-start | bytes 786440 | tf_op jit(solution)/shard_map/ppermute | solution.py:12
Sparse Core Ops, SparseCore 0:
  65.3 34.1 reduce-scatter.1
  102.6 29.8 all-gather.1
  173.9 290.4 all-reduce.1
where the time goes:
time: 474 us; the launch traced here: 473 us
  waiting for transfers between devices  249 us (53%)
  blocking collectives  123 us (26%)
  starting transfers between devices  47.1 us (10%)
  matrix products  19.6 us (4%)
  local copies, waits for them, and re-layouts  16.5 us (3%)
  between operations  14.6 us (3%)
    psum x1, waiting for transfers between devices, body(): grad_weight, grad_bias = lax.psum((weight_term, bias_term), ('row', 'col'))  166 us
    psum x1, blocking collectives, body(): grad_weight, grad_bias = lax.psum((weight_term, bias_term), ('row', 'col'))  123 us
    ppermute x12, starting transfers between devices, passed_along(): return lax.ppermute(block, axis, route)  46.9 us
    reduce_scatter x1, waiting for transfers between devices, body(): lax.psum_scatter(partial_value.reshape(col_count * tile_size, feat_width)...  34.3 us
    all_gather x1, waiting for transfers between devices, body(): lax.all_gather(grad_mid, 'col', axis=0, tiled=True)  29.9 us
    ppermute x12, waiting for transfers between devices, passed_along(): return lax.ppermute(block, axis, route)  19.3 us
  transfers between devices with their start and end apart: 15, of which 5 were waited for; matrix products, arithmetic and copies ran while one was open for 1% of the time, Pallas kernels for 0%

commit v1 on v0

v1 whole, which is shorter than its diff:
```python
import jax
import jax.numpy as jnp
from jax import lax
from jax.experimental import pallas as pl
from jax.experimental.pallas import tpu as pltpu
from jax.sharding import Mesh, PartitionSpec as P

REACH = 3
WINDOW = 2 * REACH + 1
TILE = 128
FEAT = 512
BANDS = 8
SLOTS = 16
ROW = ("y", "z")
COL = ("x", "core")
ALL = ("y", "z", "x", "core")
EXTRA = 128
BF16 = jnp.bfloat16
F32 = jnp.float32
SQRT_2_OVER_PI = 0.7978845608028654
VMEM_LIMIT = 48 * 1024 * 1024

SMEM_SPEC = pl.BlockSpec(memory_space=pltpu.SMEM)
VMEM_SPEC = pl.BlockSpec(memory_space=pltpu.VMEM)
ANY_SPEC = pl.BlockSpec(memory_space=pl.ANY)


def params():
    return pltpu.CompilerParams(vmem_limit_bytes=VMEM_LIMIT)


def rolled(block, axis, distance):
    size = lax.axis_size(axis)
    return lax.ppermute(block, axis, [(i, (i + distance) % size) for i in range(size)])


def exchange(chunks, axis):
    return lax.all_to_all(chunks, axis, 0, 0, tiled=True)


def copy_in(sources, targets, sems):
    copies = [
        pltpu.make_async_copy(s, t, sems.at[i]) for i, (s, t) in enumerate(zip(sources, targets))
    ]
    for c in copies:
        c.start()
    return copies


def forward_kernel(meta, tiles_hbm, *refs):
    panel_refs = refs[:WINDOW]
    out, tiles, panels, acc, sems = refs[WINDOW:]
    copies = copy_in(
        [tiles_hbm, *panel_refs], [tiles, *[panels.at[i] for i in range(WINDOW)]], sems
    )
    acc[...] = jnp.zeros_like(acc)
    for c in copies:
        c.wait()

    def slot(s, carry):
        b = meta[s]
        w = meta[SLOTS + s]
        acc[b] += jnp.dot(tiles[s], panels[w], preferred_element_type=F32)
        return carry

    lax.fori_loop(0, meta[2 * SLOTS], slot, 0)
    out[...] = acc[...].astype(BF16)


def forward(meta, tiles, panels):
    return pl.pallas_call(
        forward_kernel,
        out_shape=jax.ShapeDtypeStruct((BANDS, TILE, FEAT), BF16),
        in_specs=[SMEM_SPEC] + [ANY_SPEC] * (1 + WINDOW),
        out_specs=VMEM_SPEC,
        scratch_shapes=[
            pltpu.VMEM((SLOTS, TILE, TILE), BF16),
            pltpu.VMEM((WINDOW, TILE, FEAT), BF16),
            pltpu.VMEM((BANDS, TILE, FEAT), F32),
            pltpu.SemaphoreType.DMA((1 + WINDOW,)),
        ],
        compiler_params=params(),
        name="aggregate_tiles",
    )(meta, tiles, *panels)


def bias_rows(total):
    high = total.astype(BF16).astype(F32)
    return jnp.concatenate([high, total - high, jnp.zeros((8, 128), F32)], axis=0).astype(BF16)


def dense_kernel(parts, weight, bias, cot, layer_out, grad_mid, chunks):
    agg = parts[0].astype(F32)
    for i in range(1, BANDS):
        agg = agg + parts[i].astype(F32)
    agg_b = agg.astype(BF16)
    w = weight[...]
    v = jnp.dot(agg_b, w, preferred_element_type=F32) + bias[...]
    v2 = v * v
    t = jnp.tanh(SQRT_2_OVER_PI * (v + 0.044715 * (v2 * v)))
    half = 0.5 * (1.0 + t)
    layer_out[...] = (v * half).astype(BF16)
    slope = half + 0.5 * v * (1.0 - t * t) * (SQRT_2_OVER_PI * (1.0 + 3 * 0.044715 * v2))
    grad_pre = (cot[...].astype(F32) * slope).astype(BF16)
    grad_mid[...] = lax.dot_general(
        grad_pre, w, (((1,), (1,)), ((), ())), preferred_element_type=F32
    ).astype(BF16)
    term = lax.dot_general(agg_b, grad_pre, (((0,), (0,)), ((), ())), preferred_element_type=F32)
    count = chunks.shape[0]
    chunks[:, :, :FEAT] = term.astype(BF16).reshape(count, FEAT // count, FEAT)
    total = jnp.sum(grad_pre.astype(F32), axis=0, keepdims=True)
    total = jnp.concatenate([total[:, i * 128 : (i + 1) * 128] for i in range(4)], axis=0)
    chunks[:, :, FEAT:] = jnp.broadcast_to(bias_rows(total)[None], (count, 16, EXTRA))


def dense(parts, weight, bias, cot, groups):
    return pl.pallas_call(
        dense_kernel,
        out_shape=(
            jax.ShapeDtypeStruct((TILE, FEAT), BF16),
            jax.ShapeDtypeStruct((TILE, FEAT), BF16),
            jax.ShapeDtypeStruct((groups, FEAT // groups, FEAT + EXTRA), BF16),
        ),
        in_specs=[VMEM_SPEC] * 4,
        out_specs=(VMEM_SPEC,) * 3,
        compiler_params=params(),
        name="dense_layer",
    )(parts, weight, bias, cot)


def backward_kernel(meta, tiles_hbm, same_hbm, other_hbm, *refs):
    outs = refs[:WINDOW]
    tiles, panels, acc, sems = refs[WINDOW:]
    copies = copy_in(
        [tiles_hbm, same_hbm, other_hbm], [tiles, panels.at[0], panels.at[1]], sems
    )
    acc[...] = jnp.zeros_like(acc)
    for c in copies:
        c.wait()

    def slot(s, carry):
        b = meta[s]
        w = meta[SLOTS + s]
        side = (b + meta[2 * SLOTS + 1]) & 1
        acc[w] += lax.dot_general(
            tiles[s], panels[side, b >> 1], (((0,), (0,)), ((), ())), preferred_element_type=F32
        )
        return carry

    lax.fori_loop(0, meta[2 * SLOTS], slot, 0)
    for i in range(WINDOW):
        outs[i][...] = acc[i].astype(outs[i].dtype)


def backward(meta, tiles, same, other):
    return pl.pallas_call(
        backward_kernel,
        out_shape=tuple(
            jax.ShapeDtypeStruct((TILE, FEAT), F32 if i == REACH else BF16) for i in range(WINDOW)
        ),
        in_specs=[SMEM_SPEC] + [ANY_SPEC] * 3,
        out_specs=(VMEM_SPEC,) * WINDOW,
        scratch_shapes=[
            pltpu.VMEM((SLOTS, TILE, TILE), BF16),
            pltpu.VMEM((2, BANDS // 2, TILE, FEAT), BF16),
            pltpu.VMEM((WINDOW, TILE, FEAT), F32),
            pltpu.SemaphoreType.DMA((3,)),
        ],
        compiler_params=params(),
        name="backward_tiles",
    )(meta, tiles, same, other)


def summed(parts):
    total = parts[0].astype(F32)
    for i in range(1, parts.shape[0]):
        total = total + parts[i].astype(F32)
    return total


def middle_kernel(parts, out):
    total = summed(parts)
    out[:, :, :FEAT] = jnp.broadcast_to(total[None, :, :FEAT].astype(BF16), (out.shape[0], 16, FEAT))
    bias = total[0:4, FEAT:] + total[4:8, FEAT:]
    out[:, :, FEAT:] = jnp.broadcast_to(bias_rows(bias)[None], (out.shape[0], 16, EXTRA))


def middle_sum(parts, copies):
    return pl.pallas_call(
        middle_kernel,
        out_shape=jax.ShapeDtypeStruct((copies, 16, FEAT + EXTRA), BF16),
        in_specs=[VMEM_SPEC],
        out_specs=VMEM_SPEC,
        compiler_params=params(),
        name="group_sum",
    )(parts)


def last_kernel(parts, out, bias_out):
    total = summed(parts)
    out[...] = jnp.broadcast_to(total[None, :, :FEAT].astype(BF16), out.shape)
    bias = total[0:4, FEAT:] + total[4:8, FEAT:]
    for i in range(4):
        bias_out[:, i * 128 : (i + 1) * 128] = bias[i : i + 1]


def last_sum(parts, copies):
    return pl.pallas_call(
        last_kernel,
        out_shape=(
            jax.ShapeDtypeStruct((copies, 16, FEAT), BF16),
            jax.ShapeDtypeStruct((1, FEAT), F32),
        ),
        in_specs=[VMEM_SPEC],
        out_specs=(VMEM_SPEC,) * 2,
        compiler_params=params(),
        name="total_sum",
    )(parts)


def body(features, weight, bias_vec, tile_vals, tile_coords, tile_count, cotangent):
    own_row = lax.axis_index(ROW)
    core = lax.axis_index("core")
    tiles = tile_vals[0, 0]
    coords = tile_coords[0, 0]
    meta = jnp.concatenate(
        [
            coords[:, 0],
            coords[:, 1] - own_row + REACH,
            tile_count.reshape(1),
            core.reshape(1).astype(jnp.int32),
        ]
    )
    near = {0: features}
    for d in (1, 2, 3, -1, -2, -3):
        near[-d] = rolled(features, ROW, d)
    partial = forward(meta, tiles, [near[i - REACH] for i in range(WINDOW)])
    parts = exchange(partial, COL)
    groups = lax.axis_size("z") * lax.axis_size("x")
    copies = lax.axis_size("y") * lax.axis_size("core")
    layer_out, grad_mid, chunks = dense(parts, weight, bias_vec.reshape(1, FEAT), cotangent, groups)

    same = lax.all_gather(grad_mid, "x", axis=0, tiled=False)
    other = rolled(same, "core", 1)
    grads = backward(meta, tiles, same, other)
    result = grads[REACH]
    for d in (1, 2, 3, -1, -2, -3):
        result = result + rolled(grads[REACH + d], ROW, d).astype(F32)
    grad_features = result.astype(BF16)

    spread = middle_sum(exchange(chunks, ("z", "x")), copies)
    final, bias_total = last_sum(exchange(spread, ("y", "core")), groups)
    grad_weight = exchange(final, ("z", "x")).reshape(FEAT, FEAT).astype(F32)
    return (layer_out, grad_weight, bias_total.reshape(FEAT), grad_features)


def solution(mesh):
    split = Mesh(mesh.devices.reshape(8, 8, 4, 2), ALL)
    return jax.shard_map(
        body,
        mesh=split,
        in_specs=(
            P(ALL, None),
            P(),
            P(),
            P(ROW, COL, None, None, None),
            P(ROW, COL, None, None),
            P(ROW, COL),
            P(ALL, None),
        ),
        out_specs=(P(ALL, None), P(), P(), P(ALL, None)),
        check_vma=False,
    )
```

time: 474 us -> 176 us (0.37)
  waiting for transfers between devices: 249 us -> 30 us
  blocking collectives: 123 us -> 57.1 us
  starting transfers between devices: 47.1 us -> 75.3 us
  matrix products: 19.6 us -> 0 us
  local copies, waits for them, and re-layouts: 16.5 us -> 1.97 us
  between operations: 14.6 us -> 1.54 us
  Pallas kernels: 0 us -> 6.55 us
    psum x1 -> x0, waiting for transfers between devices: 166 us -> none  [body(): grad_weight, grad_bias = lax.psum((weight_term, bias_term), ('row', 'col'))]
    psum x1 -> x0, blocking collectives: 123 us -> none  [body(): grad_weight, grad_bias = lax.psum((weight_term, bias_term), ('row', 'col'))]
    all_to_all x0 -> x2, blocking collectives: none -> 46 us  [exchange(): return lax.all_to_all(chunks, axis, 0, 0, tiled=True)]
    reduce_scatter x1 -> x0, waiting for transfers between devices: 34.3 us -> none  [body(): lax.psum_scatter(partial_value.reshape(col_count * tile_size, feat_width)...]
    all_gather x1 -> x0, waiting for transfers between devices: 29.9 us -> none  [body(): lax.all_gather(grad_mid, 'col', axis=0, tiled=True)]
    dot_general x11 -> x0, matrix products: 19.6 us -> none  [the longest x2 5.87 us: backward_group(): return totals + jnp.einsum('gb,gif->bif', onehot, product)]
    all_to_all x0 -> x2, starting transfers between devices: none -> 16 us  [exchange(): return lax.all_to_all(chunks, axis, 0, 0, tiled=True)]
    ppermute x12 -> x13, starting transfers between devices: 46.9 us -> 59.3 us  [rolled(): lax.ppermute(block, axis, [(i, (i + distance) % size) for i in range(size)])]
  transfers between devices with their start and end apart: 15 -> 15, of which waited for: 5 -> 4; matrix products, arithmetic and copies ran while one was open for 1% -> 1% of each run, Pallas kernels for 0% -> 1%
where the time goes in v1:
time: 176 us; the launch traced here: 175 us
  starting transfers between devices  75.3 us (43%)
  blocking collectives  57.1 us (32%)
  waiting for transfers between devices  30 us (17%)
  Pallas kernels  6.55 us (4%)
  other arithmetic  2.01 us (1%)
  local copies, waits for them, and re-layouts  1.97 us (1%)
    ppermute x13, starting transfers between devices, rolled(): lax.ppermute(block, axis, [(i, (i + distance) % size) for i in range(size)])  59.3 us
    all_to_all x2, blocking collectives, exchange(): return lax.all_to_all(chunks, axis, 0, 0, tiled=True)  46 us
    ppermute x13, waiting for transfers between devices, rolled(): lax.ppermute(block, axis, [(i, (i + distance) % size) for i in range(size)])  30 us
    all_to_all x2, starting transfers between devices, exchange(): return lax.all_to_all(chunks, axis, 0, 0, tiled=True)  16 us
    all_gather x1, blocking collectives, body(): same = lax.all_gather(grad_mid, 'x', axis=0, tiled=False)  11.1 us
  transfers between devices with their start and end apart: 15, of which 4 were waited for; matrix products, arithmetic and copies ran while one was open for 1% of the time, Pallas kernels for 1%

profile of v1, /device:TPU:1, one launch (start us, length us, event | category | flops | bytes accessed | tf_op | source)
XLA Modules:
  0.0 174.6 jit_solution(15933569610988930854)
XLA Ops:
  0.6 8.4 %collective-permute-start = (bf16[128,512]{1,0:T(8,128)(2,1)}, bf16[128,512]{1,0:T(8,128)(2,1)S(1)}, u32[]{:S(2)}, u32[]{:S(2)}) collective-permute-start(bf16[128,512]{1,0:T(8,128)(2,1)} %refs_3_.1), channel_id=1, source_target_pairs={{0,24},{8,32},{16,40},{24,48},{32,56},{40,64},{48,72},{56,80},{64,... | collective-permute-start | bytes 393224 | tf_op jit(solution)/shard_map/ppermute | solution.py:34
  9.1 6.1 %collective-permute-start.1 = (bf16[128,512]{1,0:T(8,128)(2,1)}, bf16[128,512]{1,0:T(8,128)(2,1)S(1)}, u32[]{:S(2)}, u32[]{:S(2)}) collective-permute-start(bf16[128,512]{1,0:T(8,128)(2,1)} %refs_3_.1), channel_id=1, source_target_pairs={{0,16},{8,24},{16,32},{24,40},{32,48},{40,56},{48,64},{56,72},{64,... | collective-permute-start | bytes 393224 | tf_op jit(solution)/shard_map/ppermute | solution.py:34
  15.2 3.1 %collective-permute-start.2 = (bf16[128,512]{1,0:T(8,128)(2,1)}, bf16[128,512]{1,0:T(8,128)(2,1)S(1)}, u32[]{:S(2)}, u32[]{:S(2)}) collective-permute-start(bf16[128,512]{1,0:T(8,128)(2,1)} %refs_3_.1), channel_id=1, source_target_pairs={{0,8},{8,16},{16,24},{24,32},{32,40},{40,48},{48,56},{56,64},{64,7... | collective-permute-start | bytes 393224 | tf_op jit(solution)/shard_map/ppermute | solution.py:34
  18.3 5.5 %collective-permute-start.3 = (bf16[128,512]{1,0:T(8,128)(2,1)}, bf16[128,512]{1,0:T(8,128)(2,1)S(1)}, u32[]{:S(2)}, u32[]{:S(2)}) collective-permute-start(bf16[128,512]{1,0:T(8,128)(2,1)} %refs_3_.1), channel_id=1, source_target_pairs={{0,504},{8,0},{16,8},{24,16},{32,24},{40,32},{48,40},{56,48},{64,5... | collective-permute-start | bytes 393224 | tf_op jit(solution)/shard_map/ppermute | solution.py:34
  23.8 1.9 %collective-permute-start.4 = (bf16[128,512]{1,0:T(8,128)(2,1)}, bf16[128,512]{1,0:T(8,128)(2,1)S(1)}, u32[]{:S(2)}, u32[]{:S(2)}) collective-permute-start(bf16[128,512]{1,0:T(8,128)(2,1)} %refs_3_.1), channel_id=1, source_target_pairs={{0,496},{8,504},{16,0},{24,8},{32,16},{40,24},{48,32},{56,40},{64,... | collective-permute-start | bytes 393224 | tf_op jit(solution)/shard_map/ppermute | solution.py:34
  25.8 5.7 %collective-permute-start.5 = (bf16[128,512]{1,0:T(8,128)(2,1)}, bf16[128,512]{1,0:T(8,128)(2,1)S(1)}, u32[]{:S(2)}, u32[]{:S(2)}) collective-permute-start(bf16[128,512]{1,0:T(8,128)(2,1)} %refs_3_.1), channel_id=1, source_target_pairs={{0,488},{8,496},{16,504},{24,0},{32,8},{40,16},{48,24},{56,32},{64... | collective-permute-start | bytes 393224 | tf_op jit(solution)/shard_map/ppermute | solution.py:34
  32.2 0.1 pad_add_fusion.meta
  32.3 0.7 collective-permute-done.4.refs_5_
  32.9 8.9 %collective-permute-done.5.refs_6_ = bf16[128,512]{1,0:T(8,128)(2,1)S(1)} collective-permute-done((bf16[128,512]{1,0:T(8,128)(2,1)}, bf16[128,512]{1,0:T(8,128)(2,1)S(1)}, u32[]{:S(2)}, u32[]{:S(2)}) %collective-permute-start.5) | collective-permute-done | bytes 131104 | tf_op jit(solution)/shard_map/ppermute | solution.py:34
  41.8 1.0 copy-done
  42.9 0.9 copy-done.4
  43.8 2.4 %aggregate_tiles.1 = bf16[8,128,512]{2,1,0:T(8,128)(2,1)S(1)} custom-call(s32[34]{0:T(128)S(1)} %pad_add_fusion.meta, bf16[16,128,128]{2,1,0:T(8,128)(2,1)S(1)} %bitcast.17, bf16[128,512]{1,0:T(8,128)(2,1)S(1)} %collective-permute-done.refs_0_, bf16[128,512]{1,0:T(8,128)(2,1)S(1)} %collective-permute-done.1.refs_1_, ...), custom_call_target="tpu_custom_call" | custom-call | tf_op jit(solution)/shard_map/aggregate_tiles/pallas_call | solution.py:71
  46.2 24.5 %all_to_all.20.parts = bf16[8,128,512]{2,1,0:T(8,128)(2,1)S(1)} all-to-all(bf16[8,128,512]{2,1,0:T(8,128)(2,1)S(1)} %aggregate_tiles.1), channel_id=1, replica_groups=mesh['y'=8,'z'=8,'x'=4,'core'=2] {'x','core'}, dimensions={0} | all-to-all | bytes 2097152 | tf_op jit(solution)/shard_map/all_to_all | solution.py:38
  70.7 1.1 dense_layer.1
  71.8 21.5 %all_to_all.21.parts = bf16[32,16,640]{2,1,0:T(8,128)(2,1)S(1)} all-to-all(bf16[32,16,640]{2,1,0:T(8,128)(2,1)S(1)} %get-tuple-element.17), channel_id=1, replica_groups=mesh['y'=8,'z'=8,'x'=4,'core'=2] {'z','x'}, dimensions={0} | all-to-all | bytes 1310720 | tf_op jit(solution)/shard_map/all_to_all | solution.py:38
  93.3 0.8 group_sum.1
  94.2 10.9 %all-to-all-start.2 = ((bf16[16,16,640]{2,1,0:T(8,128)(2,1)}), bf16[16,16,640]{2,1,0:T(8,128)(2,1)S(1)}, u32[]{:S(2)}, u32[]{:S(2)}) async-start(bf16[16,16,640]{2,1,0:T(8,128)(2,1)} %group_sum.1), calls=%async_computation.2 | async-start | bytes 655360 | tf_op jit(solution)/shard_map/all_to_all | solution.py:38
  105.1 11.1 %all-gather = bf16[512,512]{1,0:T(8,128)(2,1)S(1)} all-gather(bf16[128,512]{1,0:T(8,128)(2,1)S(1)} %get-tuple-element.20), channel_id=2, replica_groups=mesh['y'=8,'z'=8,'x'=4,'core'=2] {'x'}, dimensions={0}, use_global_device_ids=true | all-gather | bytes 655360 | tf_op jit(solution)/shard_map/all_gather | solution.py:243
  116.2 3.9 %collective-permute-start.6 = (bf16[4,128,512]{2,1,0:T(8,128)(2,1)S(1)}, bf16[4,128,512]{2,1,0:T(8,128)(2,1)S(1)}, u32[]{:S(2)}, u32[]{:S(2)}) collective-permute-start(bf16[4,128,512]{2,1,0:T(8,128)(2,1)S(1)} %bitcast.15), channel_id=1, source_target_pairs={{0,1},{1,0},{2,3},{3,2},{4,5},{5,4},{6,7},{7,6},{8,9},{9,8},{10,11... | collective-permute-start | bytes 1572872 | tf_op jit(solution)/shard_map/ppermute | solution.py:34
  120.2 0.9 total_sum.1
  121.1 5.1 %all-to-all-start.3 = ((bf16[32,16,512]{2,1,0:T(8,128)(2,1)}), bf16[32,16,512]{2,1,0:T(8,128)(2,1)S(1)}, u32[]{:S(2)}, u32[]{:S(2)}) async-start(bf16[32,16,512]{2,1,0:T(8,128)(2,1)} %get-tuple-element.18), calls=%async_computation.3 | async-start | bytes 1048576 | tf_op jit(solution)/shard_map/all_to_all | solution.py:38
  126.2 1.3 backward_tiles.1
  127.5 8.1 %collective-permute-start.10 = (bf16[128,512]{1,0:T(8,128)(2,1)S(1)}, bf16[128,512]{1,0:T(8,128)(2,1)S(1)}, u32[]{:S(2)}, u32[]{:S(2)}) collective-permute-start(bf16[128,512]{1,0:T(8,128)(2,1)S(1)} %get-tuple-element.25), channel_id=1, source_target_pairs={{0,504},{8,0},{16,8},{24,16},{32,24},{40,32},{48,40},{56,48},{64,5... | collective-permute-start | bytes 393224 | tf_op jit(solution)/shard_map/ppermute | solution.py:34
  135.6 3.9 %collective-permute-start.11 = (bf16[128,512]{1,0:T(8,128)(2,1)S(1)}, bf16[128,512]{1,0:T(8,128)(2,1)S(1)}, u32[]{:S(2)}, u32[]{:S(2)}) collective-permute-start(bf16[128,512]{1,0:T(8,128)(2,1)S(1)} %get-tuple-element.26), channel_id=1, source_target_pairs={{0,496},{8,504},{16,0},{24,8},{32,16},{40,24},{48,32},{56,40},{64,... | collective-permute-start | bytes 393224 | tf_op jit(solution)/shard_map/ppermute | solution.py:34
  139.5 4.5 %collective-permute-start.12 = (bf16[128,512]{1,0:T(8,128)(2,1)S(1)}, bf16[128,512]{1,0:T(8,128)(2,1)S(1)}, u32[]{:S(2)}, u32[]{:S(2)}) collective-permute-start(bf16[128,512]{1,0:T(8,128)(2,1)S(1)} %get-tuple-element.27), channel_id=1, source_target_pairs={{0,488},{8,496},{16,504},{24,0},{32,8},{40,16},{48,24},{56,32},{64... | collective-permute-start | bytes 393224 | tf_op jit(solution)/shard_map/ppermute | solution.py:34
  144.0 3.1 %collective-permute-start.7 = (bf16[128,512]{1,0:T(8,128)(2,1)S(1)}, bf16[128,512]{1,0:T(8,128)(2,1)S(1)}, u32[]{:S(2)}, u32[]{:S(2)}) collective-permute-start(bf16[128,512]{1,0:T(8,128)(2,1)S(1)} %get-tuple-element.22), channel_id=1, source_target_pairs={{0,8},{8,16},{16,24},{24,32},{32,40},{40,48},{48,56},{56,64},{64,7... | collective-permute-start | bytes 393224 | tf_op jit(solution)/shard_map/ppermute | solution.py:34
  147.1 3.1 %collective-permute-start.8 = (bf16[128,512]{1,0:T(8,128)(2,1)S(1)}, bf16[128,512]{1,0:T(8,128)(2,1)S(1)}, u32[]{:S(2)}, u32[]{:S(2)}) collective-permute-start(bf16[128,512]{1,0:T(8,128)(2,1)S(1)} %get-tuple-element.23), channel_id=1, source_target_pairs={{0,16},{8,24},{16,32},{24,40},{32,48},{40,56},{48,64},{56,72},{64,... | collective-permute-start | bytes 393224 | tf_op jit(solution)/shard_map/ppermute | solution.py:34
  150.2 10.5 %collective-permute-done.10 = bf16[128,512]{1,0:T(8,128)(2,1)S(1)} collective-permute-done((bf16[128,512]{1,0:T(8,128)(2,1)S(1)}, bf16[128,512]{1,0:T(8,128)(2,1)S(1)}, u32[]{:S(2)}, u32[]{:S(2)}) %collective-permute-start.10) | collective-permute-done | bytes 131104 | tf_op jit(solution)/shard_map/ppermute | solution.py:34
  160.7 1.9 %collective-permute-start.9 = (bf16[128,512]{1,0:T(8,128)(2,1)S(1)}, bf16[128,512]{1,0:T(8,128)(2,1)S(1)}, u32[]{:S(2)}, u32[]{:S(2)}) collective-permute-start(bf16[128,512]{1,0:T(8,128)(2,1)S(1)} %get-tuple-element.24), channel_id=1, source_target_pairs={{0,24},{8,32},{16,40},{24,48},{32,56},{40,64},{48,72},{56,80},{64,... | collective-permute-start | bytes 393224 | tf_op jit(solution)/shard_map/ppermute | solution.py:34
  162.7 9.9 %collective-permute-done.9 = bf16[128,512]{1,0:T(8,128)(2,1)S(1)} collective-permute-done((bf16[128,512]{1,0:T(8,128)(2,1)S(1)}, bf16[128,512]{1,0:T(8,128)(2,1)S(1)}, u32[]{:S(2)}, u32[]{:S(2)}) %collective-permute-start.9) | collective-permute-done | bytes 131104 | tf_op jit(solution)/shard_map/ppermute | solution.py:34
  172.6 0.8 add_convert_fusion
  173.4 1.1 bitcast_convert_fusion
  (24 shorter events, 0.1 us)
Async XLA Ops:
  0.6 25.2 %collective-permute-start = (bf16[128,512]{1,0:T(8,128)(2,1)}, bf16[128,512]{1,0:T(8,128)(2,1)S(1)}, u32[]{:S(2)}, u32[]{:S(2)}) collective-permute-start(bf16[128,512]{1,0:T(8,128)(2,1)} %refs_3_.1), channel_id=1, source_target_pairs={{0,24},{8,32},{16,40},{24,48},{32,56},{40,64},{48,72},{56,80},{64,... | collective-permute-start | bytes 393224 | tf_op jit(solution)/shard_map/ppermute | solution.py:34
  9.1 23.2 %collective-permute-start.1 = (bf16[128,512]{1,0:T(8,128)(2,1)}, bf16[128,512]{1,0:T(8,128)(2,1)S(1)}, u32[]{:S(2)}, u32[]{:S(2)}) collective-permute-start(bf16[128,512]{1,0:T(8,128)(2,1)} %refs_3_.1), channel_id=1, source_target_pairs={{0,16},{8,24},{16,32},{24,40},{32,48},{40,56},{48,64},{56,72},{64,... | collective-permute-start | bytes 393224 | tf_op jit(solution)/shard_map/ppermute | solution.py:34
  15.2 17.1 %collective-permute-start.2 = (bf16[128,512]{1,0:T(8,128)(2,1)}, bf16[128,512]{1,0:T(8,128)(2,1)S(1)}, u32[]{:S(2)}, u32[]{:S(2)}) collective-permute-start(bf16[128,512]{1,0:T(8,128)(2,1)} %refs_3_.1), channel_id=1, source_target_pairs={{0,8},{8,16},{16,24},{24,32},{32,40},{40,48},{48,56},{56,64},{64,7... | collective-permute-start | bytes 393224 | tf_op jit(solution)/shard_map/ppermute | solution.py:34
  18.3 13.9 %collective-permute-start.3 = (bf16[128,512]{1,0:T(8,128)(2,1)}, bf16[128,512]{1,0:T(8,128)(2,1)S(1)}, u32[]{:S(2)}, u32[]{:S(2)}) collective-permute-start(bf16[128,512]{1,0:T(8,128)(2,1)} %refs_3_.1), channel_id=1, source_target_pairs={{0,504},{8,0},{16,8},{24,16},{32,24},{40,32},{48,40},{56,48},{64,5... | collective-permute-start | bytes 393224 | tf_op jit(solution)/shard_map/ppermute | solution.py:34
  23.8 9.1 %collective-permute-start.4 = (bf16[128,512]{1,0:T(8,128)(2,1)}, bf16[128,512]{1,0:T(8,128)(2,1)S(1)}, u32[]{:S(2)}, u32[]{:S(2)}) collective-permute-start(bf16[128,512]{1,0:T(8,128)(2,1)} %refs_3_.1), channel_id=1, source_target_pairs={{0,496},{8,504},{16,0},{24,8},{32,16},{40,24},{48,32},{56,40},{64,... | collective-permute-start | bytes 393224 | tf_op jit(solution)/shard_map/ppermute | solution.py:34
  25.8 5.7 %copy-start.6 = (s32[1,1,16,2]{2,3,1,0:T(2,128)S(1)}, s32[1,1,16,2]{2,3,1,0:T(2,128)}, u32[]{:S(2)}) copy-start(s32[1,1,16,2]{2,3,1,0:T(2,128)} %param.11) | copy-start | bytes 388
  25.8 16.0 %collective-permute-start.5 = (bf16[128,512]{1,0:T(8,128)(2,1)}, bf16[128,512]{1,0:T(8,128)(2,1)S(1)}, u32[]{:S(2)}, u32[]{:S(2)}) collective-permute-start(bf16[128,512]{1,0:T(8,128)(2,1)} %refs_3_.1), channel_id=1, source_target_pairs={{0,488},{8,496},{16,504},{24,0},{32,8},{40,16},{48,24},{56,32},{64... | collective-permute-start | bytes 393224 | tf_op jit(solution)/shard_map/ppermute | solution.py:34
  41.8 1.0 copy-start
  42.9 0.9 copy-start.4
  46.2 24.5 %copy-start.2 = (bf16[512,512]{1,0:T(8,128)(2,1)S(1)}, bf16[512,512]{1,0:T(8,128)(2,1)}, u32[]{:S(2)}) copy-start(bf16[512,512]{1,0:T(8,128)(2,1)} %weight.1) | copy-start | bytes 1572868
  46.2 24.5 %copy-start.3 = (bf16[128,512]{1,0:T(8,128)(2,1)S(1)}, bf16[128,512]{1,0:T(8,128)(2,1)}, u32[]{:S(2)}) copy-start(bf16[128,512]{1,0:T(8,128)(2,1)} %cot.1) | copy-start | bytes 393220
  46.2 24.5 %copy-start.5 = (f32[512]{0:T(512)S(1)}, f32[512]{0:T(512)}, u32[]{:S(2)}) copy-start(f32[512]{0:T(512)} %param.9) | copy-start | bytes 6148
  94.2 26.0 %all-to-all-start.2 = ((bf16[16,16,640]{2,1,0:T(8,128)(2,1)}), bf16[16,16,640]{2,1,0:T(8,128)(2,1)S(1)}, u32[]{:S(2)}, u32[]{:S(2)}) async-start(bf16[16,16,640]{2,1,0:T(8,128)(2,1)} %group_sum.1), calls=%async_computation.2 | async-start | bytes 655360 | tf_op jit(solution)/shard_map/all_to_all | solution.py:38
  116.2 9.9 %collective-permute-start.6 = (bf16[4,128,512]{2,1,0:T(8,128)(2,1)S(1)}, bf16[4,128,512]{2,1,0:T(8,128)(2,1)S(1)}, u32[]{:S(2)}, u32[]{:S(2)}) collective-permute-start(bf16[4,128,512]{2,1,0:T(8,128)(2,1)S(1)} %bitcast.15), channel_id=1, source_target_pairs={{0,1},{1,0},{2,3},{3,2},{4,5},{5,4},{6,7},{7,6},{8,9},{9,8},{10,11... | collective-permute-start | bytes 1572872 | tf_op jit(solution)/shard_map/ppermute | solution.py:34
  121.1 5.1 %copy-start.1 = (bf16[1,1,16,128,128]{4,3,2,1,0:T(8,128)(2,1)S(1)}, bf16[1,1,16,128,128]{4,3,2,1,0:T(8,128)(2,1)}, u32[]{:S(2)}) copy-start(bf16[1,1,16,128,128]{4,3,2,1,0:T(8,128)(2,1)} %param.10) | copy-start | bytes 1572868
  121.1 52.4 %all-to-all-start.3 = ((bf16[32,16,512]{2,1,0:T(8,128)(2,1)}), bf16[32,16,512]{2,1,0:T(8,128)(2,1)S(1)}, u32[]{:S(2)}, u32[]{:S(2)}) async-start(bf16[32,16,512]{2,1,0:T(8,128)(2,1)} %get-tuple-element.18), calls=%async_computation.3 | async-start | bytes 1048576 | tf_op jit(solution)/shard_map/all_to_all | solution.py:38
  127.5 33.2 %collective-permute-start.10 = (bf16[128,512]{1,0:T(8,128)(2,1)S(1)}, bf16[128,512]{1,0:T(8,128)(2,1)S(1)}, u32[]{:S(2)}, u32[]{:S(2)}) collective-permute-start(bf16[128,512]{1,0:T(8,128)(2,1)S(1)} %get-tuple-element.25), channel_id=1, source_target_pairs={{0,504},{8,0},{16,8},{24,16},{32,24},{40,32},{48,40},{56,48},{64,5... | collective-permute-start | bytes 393224 | tf_op jit(solution)/shard_map/ppermute | solution.py:34
  135.6 27.1 %collective-permute-start.11 = (bf16[128,512]{1,0:T(8,128)(2,1)S(1)}, bf16[128,512]{1,0:T(8,128)(2,1)S(1)}, u32[]{:S(2)}, u32[]{:S(2)}) collective-permute-start(bf16[128,512]{1,0:T(8,128)(2,1)S(1)} %get-tuple-element.26), channel_id=1, source_target_pairs={{0,496},{8,504},{16,0},{24,8},{32,16},{40,24},{48,32},{56,40},{64,... | collective-permute-start | bytes 393224 | tf_op jit(solution)/shard_map/ppermute | solution.py:34
  139.5 23.2 %collective-permute-start.12 = (bf16[128,512]{1,0:T(8,128)(2,1)S(1)}, bf16[128,512]{1,0:T(8,128)(2,1)S(1)}, u32[]{:S(2)}, u32[]{:S(2)}) collective-permute-start(bf16[128,512]{1,0:T(8,128)(2,1)S(1)} %get-tuple-element.27), channel_id=1, source_target_pairs={{0,488},{8,496},{16,504},{24,0},{32,8},{40,16},{48,24},{56,32},{64... | collective-permute-start | bytes 393224 | tf_op jit(solution)/shard_map/ppermute | solution.py:34
  144.0 18.7 %collective-permute-start.7 = (bf16[128,512]{1,0:T(8,128)(2,1)S(1)}, bf16[128,512]{1,0:T(8,128)(2,1)S(1)}, u32[]{:S(2)}, u32[]{:S(2)}) collective-permute-start(bf16[128,512]{1,0:T(8,128)(2,1)S(1)} %get-tuple-element.22), channel_id=1, source_target_pairs={{0,8},{8,16},{16,24},{24,32},{32,40},{40,48},{48,56},{56,64},{64,7... | collective-permute-start | bytes 393224 | tf_op jit(solution)/shard_map/ppermute | solution.py:34
  147.1 15.6 %collective-permute-start.8 = (bf16[128,512]{1,0:T(8,128)(2,1)S(1)}, bf16[128,512]{1,0:T(8,128)(2,1)S(1)}, u32[]{:S(2)}, u32[]{:S(2)}) collective-permute-start(bf16[128,512]{1,0:T(8,128)(2,1)S(1)} %get-tuple-element.23), channel_id=1, source_target_pairs={{0,16},{8,24},{16,32},{24,40},{32,48},{40,56},{48,64},{56,72},{64,... | collective-permute-start | bytes 393224 | tf_op jit(solution)/shard_map/ppermute | solution.py:34
  160.7 11.9 %collective-permute-start.9 = (bf16[128,512]{1,0:T(8,128)(2,1)S(1)}, bf16[128,512]{1,0:T(8,128)(2,1)S(1)}, u32[]{:S(2)}, u32[]{:S(2)}) collective-permute-start(bf16[128,512]{1,0:T(8,128)(2,1)S(1)} %get-tuple-element.24), channel_id=1, source_target_pairs={{0,24},{8,32},{16,40},{24,48},{32,56},{40,64},{48,72},{56,80},{64,... | collective-permute-start | bytes 393224 | tf_op jit(solution)/shard_map/ppermute | solution.py:34

commit v2 on v1

v2 whole, which is shorter than its diff:
```python
import jax
import jax.numpy as jnp
from jax import lax
from jax.experimental import pallas as pl
from jax.experimental.pallas import tpu as pltpu
from jax.sharding import Mesh, PartitionSpec as P

REACH = 3
WINDOW = 2 * REACH + 1
TILE = 128
FEAT = 512
BANDS = 8
SLOTS = 16
ROW = ("y", "z", "pair")
COL = ("x", "core")
ALL = ROW + COL
PAIR = "pair"
SPREAD = ("y", "x")
REST = ("z", "pair")
EXTRA = 128
HALF = 256
BF16 = jnp.bfloat16
F32 = jnp.float32
SQRT_2_OVER_PI = 0.7978845608028654
VMEM_LIMIT = 40 * 1024 * 1024

SMEM_SPEC = pl.BlockSpec(memory_space=pltpu.SMEM)
VMEM_SPEC = pl.BlockSpec(memory_space=pltpu.VMEM)
ANY_SPEC = pl.BlockSpec(memory_space=pl.ANY)
HBM_SPEC = pl.BlockSpec(memory_space=pltpu.HBM)


def params():
    return pltpu.CompilerParams(vmem_limit_bytes=VMEM_LIMIT)


def moved(block, target):
    size = lax.axis_size(ROW)
    return lax.ppermute(block, ROW, [(i, target(i) % size) for i in range(size)])


def to_sibling(i):
    return i ^ 1


def to_odd(i):
    return i + 1 if i % 2 else i - 1


def to_skip(i):
    return i + 2 if i % 2 else i - 2


def from_skip(i):
    return i - 2 if i % 2 else i + 2


def to_far(i):
    return i + 3 if i % 2 else i - 3


def swapped(block):
    return lax.ppermute(block, "core", [(0, 1), (1, 0)])


def exchange(chunks, axis):
    return lax.all_to_all(chunks, axis, 0, 0, tiled=True)


def copy_in(sources, targets, sems):
    copies = [
        pltpu.make_async_copy(s, t, sems.at[i]) for i, (s, t) in enumerate(zip(sources, targets))
    ]
    for c in copies:
        c.start()
    return copies


def stage_kernel(source, out, sem):
    copy = pltpu.make_async_copy(source, out, sem)
    copy.start()
    copy.wait()


def stage(tiles):
    return pl.pallas_call(
        stage_kernel,
        out_shape=jax.ShapeDtypeStruct(tiles.shape, tiles.dtype),
        in_specs=[HBM_SPEC],
        out_specs=VMEM_SPEC,
        scratch_shapes=[pltpu.SemaphoreType.DMA],
        compiler_params=params(),
        name="stage_tiles",
    )(tiles)


def forward_kernel(meta, tiles, own, odd, skip, far, mine, theirs, panels, acc, sems):
    copies = copy_in(
        [own, odd, skip, far],
        [panels.at[0:2], panels.at[2:4], panels.at[4:6], panels.at[6:7]],
        sems,
    )
    acc[...] = jnp.zeros_like(acc)
    for c in copies:
        c.wait()

    def slot(s, carry):
        acc[meta[s]] += jnp.dot(tiles[s], panels[meta[SLOTS + s]], preferred_element_type=F32)
        return carry

    lax.fori_loop(0, meta[2 * SLOTS], slot, 0)
    mine[...] = acc[0:4]
    theirs[...] = acc[4:8].astype(BF16)


def forward(meta, tiles, own, odd, skip, far):
    return pl.pallas_call(
        forward_kernel,
        out_shape=(
            jax.ShapeDtypeStruct((BANDS // 2, TILE, FEAT), F32),
            jax.ShapeDtypeStruct((BANDS // 2, TILE, FEAT), BF16),
        ),
        in_specs=[SMEM_SPEC, VMEM_SPEC] + [ANY_SPEC] * 4,
        out_specs=(VMEM_SPEC,) * 2,
        scratch_shapes=[
            pltpu.VMEM((WINDOW, TILE, FEAT), BF16),
            pltpu.VMEM((BANDS, TILE, FEAT), F32),
            pltpu.SemaphoreType.DMA((4,)),
        ],
        compiler_params=params(),
        name="aggregate_tiles",
    )(meta, tiles, own, odd, skip, far)


def bias_rows(total):
    high = total.astype(BF16).astype(F32)
    return jnp.concatenate([high, total - high, jnp.zeros((8, 128), F32)], axis=0).astype(BF16)


def dense_kernel(core, parts, weight, bias, cot, layer_out, mids, mine, theirs, terms):
    agg = parts[0].astype(F32)
    for i in range(1, BANDS // 2):
        agg = agg + parts[i].astype(F32)
    agg_b = agg.astype(BF16)
    w = weight[...]
    v = jnp.dot(agg_b, w, preferred_element_type=F32) + bias[...]
    v2 = v * v
    t = jnp.tanh(SQRT_2_OVER_PI * (v + 0.044715 * (v2 * v)))
    half = 0.5 * (1.0 + t)
    layer_out[...] = (v * half).astype(BF16)
    slope = half + 0.5 * v * (1.0 - t * t) * (SQRT_2_OVER_PI * (1.0 + 3 * 0.044715 * v2))
    grad_pre = (cot[...].astype(F32) * slope).astype(BF16)
    mid = lax.dot_general(
        grad_pre, w, (((1,), (1,)), ((), ())), preferred_element_type=F32
    ).astype(BF16)
    mids[...] = jnp.broadcast_to(mid[None], mids.shape)
    term = lax.dot_general(agg_b, grad_pre, (((0,), (0,)), ((), ())), preferred_element_type=F32)
    count = mine.shape[0] - 1
    for i in range(2):
        terms[i] = term[:, i * HALF : (i + 1) * HALF].reshape(count, 16, HALF)
    k = core[0]
    mine[0:count] = terms[k]
    theirs[0:count] = terms[1 - k].astype(BF16)
    total = jnp.sum(grad_pre.astype(F32), axis=0, keepdims=True)
    total = jnp.concatenate([total[:, i * 128 : (i + 1) * 128] for i in range(4)], axis=0)
    zeros = jnp.zeros((16, HALF - EXTRA), F32)
    mine[count] = jnp.concatenate([bias_rows(total).astype(F32), zeros], axis=1)
    theirs[count] = jnp.concatenate([bias_rows(total), zeros.astype(BF16)], axis=1)


def dense(core, parts, weight, bias, cot, groups):
    return pl.pallas_call(
        dense_kernel,
        out_shape=(
            jax.ShapeDtypeStruct((TILE, FEAT), BF16),
            jax.ShapeDtypeStruct((BANDS // 2, TILE, FEAT), BF16),
            jax.ShapeDtypeStruct((groups + 1, 16, HALF), F32),
            jax.ShapeDtypeStruct((groups + 1, 16, HALF), BF16),
        ),
        in_specs=[SMEM_SPEC] + [VMEM_SPEC] * 4,
        out_specs=(VMEM_SPEC,) * 4,
        scratch_shapes=[pltpu.VMEM((2, groups, 16, HALF), F32)],
        compiler_params=params(),
        name="dense_layer",
    )(core, parts, weight, bias, cot)


def chip_kernel(mine, theirs, out):
    count = out.shape[0]
    out[:, :, :HALF] = (mine[0:count] + theirs[0:count].astype(F32)).astype(BF16)
    both = mine[count, :, :EXTRA] + theirs[count, :, :EXTRA].astype(F32)
    bias = bias_rows(both[0:4] + both[4:8])
    out[:, :, HALF:] = jnp.broadcast_to(bias[None], (count, 16, EXTRA))


def chip_sum(mine, theirs):
    count = mine.shape[0] - 1
    return pl.pallas_call(
        chip_kernel,
        out_shape=jax.ShapeDtypeStruct((count, 16, HALF + EXTRA), BF16),
        in_specs=[VMEM_SPEC] * 2,
        out_specs=VMEM_SPEC,
        compiler_params=params(),
        name="chip_sum",
    )(mine, theirs)


def backward_kernel(meta, tiles, same, other, own, odd, skip, far, panels, acc, sems):
    copies = copy_in([same, other], [panels.at[0:4], panels.at[4:8]], sems)
    acc[...] = jnp.zeros_like(acc)
    for c in copies:
        c.wait()

    def slot(s, carry):
        acc[meta[SLOTS + s]] += lax.dot_general(
            tiles[s], panels[meta[s]], (((0,), (0,)), ((), ())), preferred_element_type=F32
        )
        return carry

    lax.fori_loop(0, meta[2 * SLOTS], slot, 0)
    own[...] = acc[0:2]
    odd[...] = acc[2:4].astype(BF16)
    skip[...] = acc[4:6].astype(BF16)
    far[...] = acc[6:7].astype(BF16)


def backward(meta, tiles, same, other):
    return pl.pallas_call(
        backward_kernel,
        out_shape=(
            jax.ShapeDtypeStruct((2, TILE, FEAT), F32),
            jax.ShapeDtypeStruct((2, TILE, FEAT), BF16),
            jax.ShapeDtypeStruct((2, TILE, FEAT), BF16),
            jax.ShapeDtypeStruct((1, TILE, FEAT), BF16),
        ),
        in_specs=[SMEM_SPEC, VMEM_SPEC] + [ANY_SPEC] * 2,
        out_specs=(VMEM_SPEC,) * 4,
        scratch_shapes=[
            pltpu.VMEM((BANDS, TILE, FEAT), BF16),
            pltpu.VMEM((WINDOW, TILE, FEAT), F32),
            pltpu.SemaphoreType.DMA((2,)),
        ],
        compiler_params=params(),
        name="backward_tiles",
    )(meta, tiles, same, other)


def pair_kernel(parity, own, odd, skip, mine, sibling):
    p = parity[0]
    mine[...] = own[p] + odd[p].astype(F32) + skip[p].astype(F32)
    q = 1 - p
    sibling[...] = (own[q] + odd[q].astype(F32) + skip[q].astype(F32)).astype(BF16)


def pair_sum(parity, own, odd, skip):
    return pl.pallas_call(
        pair_kernel,
        out_shape=(
            jax.ShapeDtypeStruct((TILE, FEAT), F32),
            jax.ShapeDtypeStruct((TILE, FEAT), BF16),
        ),
        in_specs=[SMEM_SPEC] + [VMEM_SPEC] * 3,
        out_specs=(VMEM_SPEC,) * 2,
        compiler_params=params(),
        name="pair_sum",
    )(parity, own, odd, skip)


def summed(parts):
    total = parts[0].astype(F32)
    for i in range(1, parts.shape[0]):
        total = total + parts[i].astype(F32)
    return total


def middle_kernel(parts, out):
    total = summed(parts)
    bias = bias_rows(total[0:4, HALF:] + total[4:8, HALF:])
    row = jnp.concatenate([total[:, :HALF].astype(BF16), bias], axis=1)
    out[...] = jnp.broadcast_to(row[None], out.shape)


def middle_sum(parts, copies):
    return pl.pallas_call(
        middle_kernel,
        out_shape=jax.ShapeDtypeStruct((copies, 16, HALF + EXTRA), BF16),
        in_specs=[VMEM_SPEC],
        out_specs=VMEM_SPEC,
        compiler_params=params(),
        name="group_sum",
    )(parts)


def last_kernel(parts, out, bias_out):
    total = summed(parts)
    out[...] = jnp.broadcast_to(total[None, :, :HALF].astype(BF16), out.shape)
    bias = total[0:4, HALF:] + total[4:8, HALF:]
    for i in range(4):
        bias_out[:, i * 128 : (i + 1) * 128] = bias[i : i + 1]


def last_sum(parts, copies):
    return pl.pallas_call(
        last_kernel,
        out_shape=(
            jax.ShapeDtypeStruct((copies, 16, HALF), BF16),
            jax.ShapeDtypeStruct((1, FEAT), F32),
        ),
        in_specs=[VMEM_SPEC],
        out_specs=(VMEM_SPEC,) * 2,
        compiler_params=params(),
        name="total_sum",
    )(parts)


def join_kernel(core, mine, other, out):
    for k in range(2):

        @pl.when(core[0] == k)
        def _():
            out[:, k * HALF : (k + 1) * HALF] = mine[...].astype(F32)
            out[:, (1 - k) * HALF : (2 - k) * HALF] = other[...].astype(F32)


def join(core, mine, other):
    return pl.pallas_call(
        join_kernel,
        out_shape=jax.ShapeDtypeStruct((FEAT, FEAT), F32),
        in_specs=[SMEM_SPEC] + [VMEM_SPEC] * 2,
        out_specs=VMEM_SPEC,
        compiler_params=params(),
        name="join_halves",
    )(core, mine, other)


def after(value, other):
    return lax.optimization_barrier((value, other))[0]


def body(features, weight, bias_vec, tile_vals, tile_coords, tile_count, cotangent):
    own_row = lax.axis_index(ROW)
    core = lax.axis_index("core")
    parity = own_row & 1
    pair_row = own_row - parity
    tiles = stage(tile_vals[0, 0])
    coords = tile_coords[0, 0]
    block = coords[:, 0]
    block_at = (block & 1 ^ core) * (BANDS // 2) + (block >> 1)
    rel = coords[:, 1] - pair_row
    below = 2 + 2 * parity
    above = 4 - 2 * parity
    panel_at = jnp.where(
        (rel >= 0) & (rel < 2),
        rel,
        jnp.where(
            (rel >= -2) & (rel < 0),
            below + rel + 2,
            jnp.where((rel >= 2) & (rel < 4), above + rel - 2, 6),
        ),
    )
    meta = jnp.concatenate([block_at, panel_at, tile_count.reshape(1)])

    own = lax.all_gather(features, PAIR, axis=0, tiled=False)
    far = moved(features[None], to_far)
    odd = moved(own, to_odd)
    skip = moved(own, to_skip)
    mine, theirs = forward(meta, tiles, own, odd, skip, far)
    half = (mine + swapped(theirs).astype(F32)).astype(BF16)
    parts = exchange(half, "x")
    groups = lax.axis_size("y") * lax.axis_size("x")
    copies = lax.axis_size("z") * lax.axis_size("pair")
    side = core.reshape(1)
    layer_out, mids, w_mine, w_theirs = dense(
        side, parts, weight, bias_vec.reshape(1, FEAT), cotangent, groups
    )

    same = exchange(mids, "x")
    arrived = exchange(chip_sum(w_mine, swapped(w_theirs)), SPREAD)
    other = swapped(same)
    own_g, odd_g, skip_g, far_g = backward(meta, tiles, same, other)
    arrived = after(arrived, far_g)
    far_in = moved(far_g, to_far)
    odd_in = moved(odd_g, to_odd)
    skip_in = moved(skip_g, from_skip)
    keep, sibling = pair_sum(parity.reshape(1), own_g, odd_in, skip_in)
    sibling_in = moved(sibling, to_sibling)
    grad_features = (keep + far_in[0].astype(F32) + sibling_in.astype(F32)).astype(BF16)

    spread = middle_sum(arrived, copies)
    final, bias_total = last_sum(after(exchange(spread, REST), (odd_in, skip_in, far_in)), groups)
    w_half = exchange(final, SPREAD).reshape(FEAT, HALF)
    grad_weight = join(side, w_half, swapped(w_half))
    return (layer_out, grad_weight, bias_total.reshape(FEAT), grad_features)


def solution(mesh):
    split = Mesh(mesh.devices.reshape(8, 4, 2, 4, 2), ALL)
    return jax.shard_map(
        body,
        mesh=split,
        in_specs=(
            P(ALL, None),
            P(),
            P(),
            P(ROW, COL, None, None, None),
            P(ROW, COL, None, None),
            P(ROW, COL),
            P(ALL, None),
        ),
        out_specs=(P(ALL, None), P(), P(), P(ALL, None)),
        check_vma=False,
    )
```

time: 176 us -> 143 us (0.81)
  blocking collectives: 57.1 us -> 18.6 us
  starting transfers between devices: 75.3 us -> 84.4 us
  waiting for transfers between devices: 30 us -> 25 us
  Pallas kernels: 6.55 us -> 9.42 us
    all_to_all x2 -> x1, blocking collectives: 46 us -> 12.3 us  [exchange(): return lax.all_to_all(chunks, axis, 0, 0, tiled=True)]
    ppermute x13 -> x11, waiting for transfers between devices: 30 us -> 14.8 us  [the longest x7 10.2 us: moved(): lax.ppermute(block, ROW, [(i, target(i) % size) for i in range(size)])]
    all_to_all x2 -> x4, waiting for transfers between devices: 0.01 us -> 10.2 us  [exchange(): return lax.all_to_all(chunks, axis, 0, 0, tiled=True)]
    ppermute x13 -> x11, starting transfers between devices: 59.3 us -> 64.4 us  [the longest x7 43.8 us: moved(): lax.ppermute(block, ROW, [(i, target(i) % size) for i in range(size)])]
    all_gather x1, blocking collectives: 11.1 us -> 6.34 us  [body(): own = lax.all_gather(features, PAIR, axis=0, tiled=False)]
    all_to_all x2 -> x4, starting transfers between devices: 16 us -> 20 us  [exchange(): return lax.all_to_all(chunks, axis, 0, 0, tiled=True)]
    pallas_call x2 -> x6, Pallas kernels: 3.76 us -> 6.62 us  [the longest x1 2.33 us: backward(): pl.pallas_call(backward_kernel, out_shape=(jax.ShapeDtypeStruct((2, TILE,...]
  transfers between devices with their start and end apart: 15 -> 15, of which waited for: 4 -> 9; matrix products, arithmetic and copies ran while one was open for 1% -> 1% of each run, Pallas kernels for 1% -> 3%
where the time goes in v2:
time: 143 us; the launch traced here: 142 us
  starting transfers between devices  84.4 us (59%)
  waiting for transfers between devices  25 us (17%)
  blocking collectives  18.6 us (13%)
  Pallas kernels  9.42 us (7%)
  local copies, waits for them, and re-layouts  2.4 us (2%)
  between operations  1.53 us (1%)
    ppermute x7, starting transfers between devices, moved(): lax.ppermute(block, ROW, [(i, target(i) % size) for i in range(size)])  43.8 us
    ppermute x4, starting transfers between devices, swapped(): return lax.ppermute(block, 'core', [(0, 1), (1, 0)])  20.6 us
    all_to_all x4, starting transfers between devices, exchange(): return lax.all_to_all(chunks, axis, 0, 0, tiled=True)  20 us
    all_to_all x1, blocking collectives, exchange(): return lax.all_to_all(chunks, axis, 0, 0, tiled=True)  12.3 us
    all_to_all x4, waiting for transfers between devices, exchange(): return lax.all_to_all(chunks, axis, 0, 0, tiled=True)  10.2 us
    ppermute x7, waiting for transfers between devices, moved(): lax.ppermute(block, ROW, [(i, target(i) % size) for i in range(size)])  10.2 us
    all_gather x1, blocking collectives, body(): own = lax.all_gather(features, PAIR, axis=0, tiled=False)  6.34 us
    ppermute x4, waiting for transfers between devices, swapped(): return lax.ppermute(block, 'core', [(0, 1), (1, 0)])  4.61 us
  transfers between devices with their start and end apart: 15, of which 9 were waited for; matrix products, arithmetic and copies ran while one was open for 1% of the time, Pallas kernels for 3%

profile of v2, /device:TPU:1, one launch (start us, length us, event | category | flops | bytes accessed | tf_op | source)
XLA Modules:
  0.0 142.4 jit_solution(17503364211132443272)
XLA Ops:
  0.6 6.3 %all-gather = bf16[256,512]{1,0:T(8,128)(2,1)S(1)} all-gather(bf16[128,512]{1,0:T(8,128)(2,1)} %param.7), channel_id=2, replica_groups=mesh['y'=8,'z'=4,'pair'=2,'x'=4,'core'=2] {'pair'}, dimensions={0}, use_global_device_ids=true | all-gather | bytes 393216 | tf_op jit(solution)/shard_map/all_gather | solution.py:363
  7.0 13.4 %collective-permute-start.1 = (bf16[2,128,512]{2,1,0:T(8,128)(2,1)S(1)}, bf16[2,128,512]{2,1,0:T(8,128)(2,1)S(1)}, u32[]{:S(2)}, u32[]{:S(2)}) collective-permute-start(bf16[2,128,512]{2,1,0:T(8,128)(2,1)S(1)} %bitcast.28), channel_id=1, source_target_pairs={{0,496},{8,24},{16,0},{24,40},{32,16},{40,56},{48,32},{56,72},{64,... | collective-permute-start | bytes 786440 | tf_op jit(solution)/shard_map/ppermute | solution.py:39
  20.4 1.9 %collective-permute-start = (bf16[2,128,512]{2,1,0:T(8,128)(2,1)S(1)}, bf16[2,128,512]{2,1,0:T(8,128)(2,1)S(1)}, u32[]{:S(2)}, u32[]{:S(2)}) collective-permute-start(bf16[2,128,512]{2,1,0:T(8,128)(2,1)S(1)} %bitcast.29), channel_id=1, source_target_pairs={{0,504},{8,16},{16,8},{24,32},{32,24},{40,48},{48,40},{56,64},{64,... | collective-permute-start | bytes 786440 | tf_op jit(solution)/shard_map/ppermute | solution.py:39
  22.4 4.0 %collective-permute-start.2 = (bf16[1,128,512]{2,1,0:T(8,128)(2,1)S(1)}, bf16[1,128,512]{2,1,0:T(8,128)(2,1)S(1)}, u32[]{:S(2)}, u32[]{:S(2)}) collective-permute-start(bf16[1,128,512]{2,1,0:T(8,128)(2,1)S(1)} %bitcast.35), channel_id=1, source_target_pairs={{0,488},{8,32},{16,504},{24,48},{32,8},{40,64},{48,24},{56,80},{64... | collective-permute-start | bytes 393224 | tf_op jit(solution)/shard_map/ppermute | solution.py:39
  27.7 1.0 copy-done
  28.9 5.9 %collective-permute-done.2.far = bf16[1,128,512]{2,1,0:T(8,128)(2,1)S(1)} collective-permute-done((bf16[1,128,512]{2,1,0:T(8,128)(2,1)S(1)}, bf16[1,128,512]{2,1,0:T(8,128)(2,1)S(1)}, u32[]{:S(2)}, u32[]{:S(2)}) %collective-permute-start.2) | collective-permute-done | bytes 131104 | tf_op jit(solution)/shard_map/ppermute | solution.py:39
  34.8 2.3 %aggregate_tiles.1 = (f32[4,128,512]{2,1,0:T(8,128)S(1)}, bf16[4,128,512]{2,1,0:T(8,128)(2,1)S(1)}) custom-call(s32[33]{0:T(128)S(1)} %pad_add_fusion.meta, bf16[16,128,128]{2,1,0:T(8,128)(2,1)S(1)} %stage_tiles.1.tiles, bf16[2,128,512]{2,1,0:T(8,128)(2,1)S(1)} %bitcast.30, bf16[2,128,512]{2,1,0:T(8,128)(2,1)S(1)} %collective-permute-done.odd, ...), custom_call_target="tpu_custom_call" | custom-call | tf_op jit(solution)/shard_map/aggregate_tiles/pallas_call | solution.py:117
  37.1 5.4 %collective-permute-start.3 = (bf16[4,128,512]{2,1,0:T(8,128)(2,1)S(1)}, bf16[4,128,512]{2,1,0:T(8,128)(2,1)S(1)}, u32[]{:S(2)}, u32[]{:S(2)}) collective-permute-start(bf16[4,128,512]{2,1,0:T(8,128)(2,1)S(1)} %get-tuple-element.21), channel_id=1, source_target_pairs={{0,1},{1,0},{2,3},{3,2},{4,5},{5,4},{6,7},{7,6},{8,9},{9,8},{10,11... | collective-permute-start | bytes 1572872 | tf_op jit(solution)/shard_map/ppermute | solution.py:63
  42.6 1.5 %collective-permute-done.3 = bf16[4,128,512]{2,1,0:T(8,128)(2,1)S(1)} collective-permute-done((bf16[4,128,512]{2,1,0:T(8,128)(2,1)S(1)}, bf16[4,128,512]{2,1,0:T(8,128)(2,1)S(1)}, u32[]{:S(2)}, u32[]{:S(2)}) %collective-permute-start.3) | collective-permute-done | bytes 524320 | tf_op jit(solution)/shard_map/ppermute | solution.py:63
  44.3 12.3 %all_to_all.25.parts = bf16[4,128,512]{2,1,0:T(8,128)(2,1)S(1)} all-to-all(bf16[4,128,512]{2,1,0:T(8,128)(2,1)S(1)} %add_convert_fusion), channel_id=1, replica_groups=mesh['y'=8,'z'=4,'pair'=2,'x'=4,'core'=2] {'x'}, dimensions={0} | all-to-all | bytes 1048576 | tf_op jit(solution)/shard_map/all_to_all | solution.py:67
  57.2 1.4 dense_layer.1
  58.6 3.5 %all-to-all-start.2 = ((bf16[4,128,512]{2,1,0:T(8,128)(2,1)}), bf16[4,128,512]{2,1,0:T(8,128)(2,1)S(1)}, u32[]{:S(2)}, u32[]{:S(2)}) async-start(bf16[4,128,512]{2,1,0:T(8,128)(2,1)} %get-tuple-element.25), calls=%async_computation.2 | async-start | bytes 1048576 | tf_op jit(solution)/shard_map/all_to_all | solution.py:67
  62.1 3.7 %collective-permute-start.4 = (bf16[33,16,256]{2,1,0:T(8,128)(2,1)S(1)}, bf16[33,16,256]{2,1,0:T(8,128)(2,1)S(1)}, u32[]{:S(2)}, u32[]{:S(2)}) collective-permute-start(bf16[33,16,256]{2,1,0:T(8,128)(2,1)S(1)} %get-tuple-element.24), channel_id=1, source_target_pairs={{0,1},{1,0},{2,3},{3,2},{4,5},{5,4},{6,7},{7,6},{8,9},{9,8},{10,11... | collective-permute-start | bytes 811016 | tf_op jit(solution)/shard_map/ppermute | solution.py:63
  65.8 1.2 collective-permute-done.4.theirs
  67.0 0.8 chip_sum.1
  67.8 1.7 %all-to-all-done.2.same = bf16[4,128,512]{2,1,0:T(8,128)(2,1)S(1)} async-done(((bf16[4,128,512]{2,1,0:T(8,128)(2,1)}), bf16[4,128,512]{2,1,0:T(8,128)(2,1)S(1)}, u32[]{:S(2)}, u32[]{:S(2)}) %all-to-all-start.2) | async-done | bytes 524320 | tf_op jit(solution)/shard_map/all_to_all | solution.py:67
  69.5 5.8 %all-to-all-start.1 = ((bf16[32,16,384]{2,1,0:T(8,128)(2,1)}), bf16[32,16,384]{2,1,0:T(8,128)(2,1)S(1)}, u32[]{:S(2)}, u32[]{:S(2)}) async-start(bf16[32,16,384]{2,1,0:T(8,128)(2,1)} %chip_sum.1), calls=%async_computation.1 | async-start | bytes 786432 | tf_op jit(solution)/shard_map/all_to_all | solution.py:67
  75.2 4.6 %collective-permute-start.5 = (bf16[4,128,512]{2,1,0:T(8,128)(2,1)S(1)}, bf16[4,128,512]{2,1,0:T(8,128)(2,1)S(1)}, u32[]{:S(2)}, u32[]{:S(2)}) collective-permute-start(bf16[4,128,512]{2,1,0:T(8,128)(2,1)S(1)} %all-to-all-done.2.same), channel_id=1, source_target_pairs={{0,1},{1,0},{2,3},{3,2},{4,5},{5,4},{6,7},{7,6},{8,9},{9,8},{10,11... | collective-permute-start | bytes 1572872 | tf_op jit(solution)/shard_map/ppermute | solution.py:63
  79.8 1.5 %collective-permute-done.5.other = bf16[4,128,512]{2,1,0:T(8,128)(2,1)S(1)} collective-permute-done((bf16[4,128,512]{2,1,0:T(8,128)(2,1)S(1)}, bf16[4,128,512]{2,1,0:T(8,128)(2,1)S(1)}, u32[]{:S(2)}, u32[]{:S(2)}) %collective-permute-start.5) | collective-permute-done | bytes 524320 | tf_op jit(solution)/shard_map/ppermute | solution.py:63
  81.3 2.3 %backward_tiles.1 = (f32[2,128,512]{2,1,0:T(8,128)S(1)}, bf16[2,128,512]{2,1,0:T(8,128)(2,1)S(1)}, bf16[2,128,512]{2,1,0:T(8,128)(2,1)S(1)}, bf16[1,128,512]{2,1,0:T(8,128)(2,1)S(1)}) custom-call(s32[33]{0:T(128)S(1)} %pad_add_fusion.meta, bf16[16,128,128]{2,1,0:T(8,128)(2,1)S(1)} %stage_tiles.1.tiles, bf16[4,128,512]{2,1,0:T(8,128)(2,1)S(1)} %all-to-all-done.2.same, ...), custom_call_target="tpu_custom_call" | custom-call | tf_op jit(solution)/shard_map/backward_tiles/pallas_call | solution.py:228
  83.7 9.0 %collective-permute-start.6 = (bf16[2,128,512]{2,1,0:T(8,128)(2,1)S(1)}, bf16[2,128,512]{2,1,0:T(8,128)(2,1)S(1)}, u32[]{:S(2)}, u32[]{:S(2)}) collective-permute-start(bf16[2,128,512]{2,1,0:T(8,128)(2,1)S(1)} %get-tuple-element.28), channel_id=1, source_target_pairs={{0,504},{8,16},{16,8},{24,32},{32,24},{40,48},{48,40},{56,64},{64,... | collective-permute-start | bytes 786440 | tf_op jit(solution)/shard_map/ppermute | solution.py:39
  92.7 1.9 %collective-permute-start.7 = (bf16[2,128,512]{2,1,0:T(8,128)(2,1)S(1)}, bf16[2,128,512]{2,1,0:T(8,128)(2,1)S(1)}, u32[]{:S(2)}, u32[]{:S(2)}) collective-permute-start(bf16[2,128,512]{2,1,0:T(8,128)(2,1)S(1)} %get-tuple-element.29), channel_id=1, source_target_pairs={{0,16},{8,504},{16,32},{24,8},{32,48},{40,24},{48,64},{56,40},{64,... | collective-permute-start | bytes 786440 | tf_op jit(solution)/shard_map/ppermute | solution.py:39
  95.3 3.4 %all-to-all-start.3 = ((bf16[8,16,384]{2,1,0:T(8,128)(2,1)}), bf16[8,16,384]{2,1,0:T(8,128)(2,1)S(1)}, u32[]{:S(2)}, u32[]{:S(2)}) async-start(bf16[8,16,384]{2,1,0:T(8,128)(2,1)} %group_sum.1), calls=%async_computation.3 | async-start | bytes 196608 | tf_op jit(solution)/shard_map/all_to_all | solution.py:67
  98.7 9.9 %collective-permute-start.8 = (bf16[1,128,512]{2,1,0:T(8,128)(2,1)S(1)}, bf16[1,128,512]{2,1,0:T(8,128)(2,1)S(1)}, u32[]{:S(2)}, u32[]{:S(2)}) collective-permute-start(bf16[1,128,512]{2,1,0:T(8,128)(2,1)S(1)} %get-tuple-element.26), channel_id=1, source_target_pairs={{0,488},{8,32},{16,504},{24,48},{32,8},{40,64},{48,24},{56,80},{64... | collective-permute-start | bytes 393224 | tf_op jit(solution)/shard_map/ppermute | solution.py:39
  108.6 4.3 %collective-permute-done.8 = bf16[1,128,512]{2,1,0:T(8,128)(2,1)S(1)} collective-permute-done((bf16[1,128,512]{2,1,0:T(8,128)(2,1)S(1)}, bf16[1,128,512]{2,1,0:T(8,128)(2,1)S(1)}, u32[]{:S(2)}, u32[]{:S(2)}) %collective-permute-start.8) | collective-permute-done | bytes 131104 | tf_op jit(solution)/shard_map/ppermute | solution.py:39
  112.9 1.8 %all-to-all-done.3.parts = bf16[8,16,384]{2,1,0:T(8,128)(2,1)S(1)} async-done(((bf16[8,16,384]{2,1,0:T(8,128)(2,1)}), bf16[8,16,384]{2,1,0:T(8,128)(2,1)S(1)}, u32[]{:S(2)}, u32[]{:S(2)}) %all-to-all-start.3) | async-done | bytes 98336 | tf_op jit(solution)/shard_map/all_to_all | solution.py:67
  114.7 0.7 total_sum.1
  115.5 7.4 %all-to-all-start.4 = ((bf16[32,16,256]{2,1,0:T(8,128)(2,1)}), bf16[32,16,256]{2,1,0:T(8,128)(2,1)S(1)}, u32[]{:S(2)}, u32[]{:S(2)}) async-start(bf16[32,16,256]{2,1,0:T(8,128)(2,1)} %get-tuple-element.31), calls=%async_computation.4 | async-start | bytes 524288 | tf_op jit(solution)/shard_map/all_to_all | solution.py:67
  123.0 3.6 %collective-permute-start.10 = (bf16[128,512]{1,0:T(8,128)(2,1)S(1)}, bf16[128,512]{1,0:T(8,128)(2,1)S(1)}, u32[]{:S(2)}, u32[]{:S(2)}) collective-permute-start(bf16[128,512]{1,0:T(8,128)(2,1)S(1)} %get-tuple-element.35), channel_id=1, source_target_pairs={{0,8},{8,0},{16,24},{24,16},{32,40},{40,32},{48,56},{56,48},{64,72... | collective-permute-start | bytes 393224 | tf_op jit(solution)/shard_map/ppermute | solution.py:39
  126.6 6.7 %all-to-all-done.4 = bf16[32,16,256]{2,1,0:T(8,128)(2,1)S(1)} async-done(((bf16[32,16,256]{2,1,0:T(8,128)(2,1)}), bf16[32,16,256]{2,1,0:T(8,128)(2,1)S(1)}, u32[]{:S(2)}, u32[]{:S(2)}) %all-to-all-start.4) | async-done | bytes 262176 | tf_op jit(solution)/shard_map/all_to_all | solution.py:67
  133.3 6.9 %collective-permute-start.9 = (bf16[512,256]{1,0:T(8,128)(2,1)S(1)}, bf16[512,256]{1,0:T(8,128)(2,1)S(1)}, u32[]{:S(2)}, u32[]{:S(2)}) collective-permute-start(bf16[512,256]{1,0:T(8,128)(2,1)S(1)} %bitcast.31), channel_id=1, source_target_pairs={{0,1},{1,0},{2,3},{3,2},{4,5},{5,4},{6,7},{7,6},{8,9},{9,8},{10,11... | collective-permute-start | bytes 786440 | tf_op jit(solution)/shard_map/ppermute | solution.py:63
  141.3 1.0 join_halves.1
  (26 shorter events, 3.6 us)
Async XLA Ops:
  0.6 21.7 %copy-start.4 = (bf16[128,512]{1,0:T(8,128)(2,1)S(1)}, bf16[128,512]{1,0:T(8,128)(2,1)}, u32[]{:S(2)}) copy-start(bf16[128,512]{1,0:T(8,128)(2,1)} %param.7) | copy-start | bytes 393220
  7.0 27.8 %collective-permute-start.1 = (bf16[2,128,512]{2,1,0:T(8,128)(2,1)S(1)}, bf16[2,128,512]{2,1,0:T(8,128)(2,1)S(1)}, u32[]{:S(2)}, u32[]{:S(2)}) collective-permute-start(bf16[2,128,512]{2,1,0:T(8,128)(2,1)S(1)} %bitcast.28), channel_id=1, source_target_pairs={{0,496},{8,24},{16,0},{24,40},{32,16},{40,56},{48,32},{56,72},{64,... | collective-permute-start | bytes 786440 | tf_op jit(solution)/shard_map/ppermute | solution.py:39
  20.4 14.4 %collective-permute-start = (bf16[2,128,512]{2,1,0:T(8,128)(2,1)S(1)}, bf16[2,128,512]{2,1,0:T(8,128)(2,1)S(1)}, u32[]{:S(2)}, u32[]{:S(2)}) collective-permute-start(bf16[2,128,512]{2,1,0:T(8,128)(2,1)S(1)} %bitcast.29), channel_id=1, source_target_pairs={{0,504},{8,16},{16,8},{24,32},{32,24},{40,48},{48,40},{56,64},{64,... | collective-permute-start | bytes 786440 | tf_op jit(solution)/shard_map/ppermute | solution.py:39
  22.4 12.4 %collective-permute-start.2 = (bf16[1,128,512]{2,1,0:T(8,128)(2,1)S(1)}, bf16[1,128,512]{2,1,0:T(8,128)(2,1)S(1)}, u32[]{:S(2)}, u32[]{:S(2)}) collective-permute-start(bf16[1,128,512]{2,1,0:T(8,128)(2,1)S(1)} %bitcast.35), channel_id=1, source_target_pairs={{0,488},{8,32},{16,504},{24,48},{32,8},{40,64},{48,24},{56,80},{64... | collective-permute-start | bytes 393224 | tf_op jit(solution)/shard_map/ppermute | solution.py:39
  26.4 0.7 copy-start.5
  27.7 1.0 copy-start
  37.1 7.0 %collective-permute-start.3 = (bf16[4,128,512]{2,1,0:T(8,128)(2,1)S(1)}, bf16[4,128,512]{2,1,0:T(8,128)(2,1)S(1)}, u32[]{:S(2)}, u32[]{:S(2)}) collective-permute-start(bf16[4,128,512]{2,1,0:T(8,128)(2,1)S(1)} %get-tuple-element.21), channel_id=1, source_target_pairs={{0,1},{1,0},{2,3},{3,2},{4,5},{5,4},{6,7},{7,6},{8,9},{9,8},{10,11... | collective-permute-start | bytes 1572872 | tf_op jit(solution)/shard_map/ppermute | solution.py:63
  44.2 12.3 %copy-start.1 = (bf16[512,512]{1,0:T(8,128)(2,1)S(1)}, bf16[512,512]{1,0:T(8,128)(2,1)}, u32[]{:S(2)}) copy-start(bf16[512,512]{1,0:T(8,128)(2,1)} %weight.1) | copy-start | bytes 1572868
  44.3 12.3 %copy-start.2 = (bf16[128,512]{1,0:T(8,128)(2,1)S(1)}, bf16[128,512]{1,0:T(8,128)(2,1)}, u32[]{:S(2)}) copy-start(bf16[128,512]{1,0:T(8,128)(2,1)} %cot.1) | copy-start | bytes 393220
  56.6 0.7 copy-start.3
  58.6 10.8 %all-to-all-start.2 = ((bf16[4,128,512]{2,1,0:T(8,128)(2,1)}), bf16[4,128,512]{2,1,0:T(8,128)(2,1)S(1)}, u32[]{:S(2)}, u32[]{:S(2)}) async-start(bf16[4,128,512]{2,1,0:T(8,128)(2,1)} %get-tuple-element.25), calls=%async_computation.2 | async-start | bytes 1048576 | tf_op jit(solution)/shard_map/all_to_all | solution.py:67
  62.1 4.9 %collective-permute-start.4 = (bf16[33,16,256]{2,1,0:T(8,128)(2,1)S(1)}, bf16[33,16,256]{2,1,0:T(8,128)(2,1)S(1)}, u32[]{:S(2)}, u32[]{:S(2)}) collective-permute-start(bf16[33,16,256]{2,1,0:T(8,128)(2,1)S(1)} %get-tuple-element.24), channel_id=1, source_target_pairs={{0,1},{1,0},{2,3},{3,2},{4,5},{5,4},{6,7},{7,6},{8,9},{9,8},{10,11... | collective-permute-start | bytes 811016 | tf_op jit(solution)/shard_map/ppermute | solution.py:63
  69.5 25.2 %all-to-all-start.1 = ((bf16[32,16,384]{2,1,0:T(8,128)(2,1)}), bf16[32,16,384]{2,1,0:T(8,128)(2,1)S(1)}, u32[]{:S(2)}, u32[]{:S(2)}) async-start(bf16[32,16,384]{2,1,0:T(8,128)(2,1)} %chip_sum.1), calls=%async_computation.1 | async-start | bytes 786432 | tf_op jit(solution)/shard_map/all_to_all | solution.py:67
  75.2 6.1 %collective-permute-start.5 = (bf16[4,128,512]{2,1,0:T(8,128)(2,1)S(1)}, bf16[4,128,512]{2,1,0:T(8,128)(2,1)S(1)}, u32[]{:S(2)}, u32[]{:S(2)}) collective-permute-start(bf16[4,128,512]{2,1,0:T(8,128)(2,1)S(1)} %all-to-all-done.2.same), channel_id=1, source_target_pairs={{0,1},{1,0},{2,3},{3,2},{4,5},{5,4},{6,7},{7,6},{8,9},{9,8},{10,11... | collective-permute-start | bytes 1572872 | tf_op jit(solution)/shard_map/ppermute | solution.py:63
  83.7 29.2 %collective-permute-start.6 = (bf16[2,128,512]{2,1,0:T(8,128)(2,1)S(1)}, bf16[2,128,512]{2,1,0:T(8,128)(2,1)S(1)}, u32[]{:S(2)}, u32[]{:S(2)}) collective-permute-start(bf16[2,128,512]{2,1,0:T(8,128)(2,1)S(1)} %get-tuple-element.28), channel_id=1, source_target_pairs={{0,504},{8,16},{16,8},{24,32},{32,24},{40,48},{48,40},{56,64},{64,... | collective-permute-start | bytes 786440 | tf_op jit(solution)/shard_map/ppermute | solution.py:39
  92.7 20.2 %collective-permute-start.7 = (bf16[2,128,512]{2,1,0:T(8,128)(2,1)S(1)}, bf16[2,128,512]{2,1,0:T(8,128)(2,1)S(1)}, u32[]{:S(2)}, u32[]{:S(2)}) collective-permute-start(bf16[2,128,512]{2,1,0:T(8,128)(2,1)S(1)} %get-tuple-element.29), channel_id=1, source_target_pairs={{0,16},{8,504},{16,32},{24,8},{32,48},{40,24},{48,64},{56,40},{64,... | collective-permute-start | bytes 786440 | tf_op jit(solution)/shard_map/ppermute | solution.py:39
  95.3 19.4 %all-to-all-start.3 = ((bf16[8,16,384]{2,1,0:T(8,128)(2,1)}), bf16[8,16,384]{2,1,0:T(8,128)(2,1)S(1)}, u32[]{:S(2)}, u32[]{:S(2)}) async-start(bf16[8,16,384]{2,1,0:T(8,128)(2,1)} %group_sum.1), calls=%async_computation.3 | async-start | bytes 196608 | tf_op jit(solution)/shard_map/all_to_all | solution.py:67
  98.7 14.2 %collective-permute-start.8 = (bf16[1,128,512]{2,1,0:T(8,128)(2,1)S(1)}, bf16[1,128,512]{2,1,0:T(8,128)(2,1)S(1)}, u32[]{:S(2)}, u32[]{:S(2)}) collective-permute-start(bf16[1,128,512]{2,1,0:T(8,128)(2,1)S(1)} %get-tuple-element.26), channel_id=1, source_target_pairs={{0,488},{8,32},{16,504},{24,48},{32,8},{40,64},{48,24},{56,80},{64... | collective-permute-start | bytes 393224 | tf_op jit(solution)/shard_map/ppermute | solution.py:39
  115.5 17.9 %all-to-all-start.4 = ((bf16[32,16,256]{2,1,0:T(8,128)(2,1)}), bf16[32,16,256]{2,1,0:T(8,128)(2,1)S(1)}, u32[]{:S(2)}, u32[]{:S(2)}) async-start(bf16[32,16,256]{2,1,0:T(8,128)(2,1)} %get-tuple-element.31), calls=%async_computation.4 | async-start | bytes 524288 | tf_op jit(solution)/shard_map/all_to_all | solution.py:67
  123.0 17.2 %collective-permute-start.10 = (bf16[128,512]{1,0:T(8,128)(2,1)S(1)}, bf16[128,512]{1,0:T(8,128)(2,1)S(1)}, u32[]{:S(2)}, u32[]{:S(2)}) collective-permute-start(bf16[128,512]{1,0:T(8,128)(2,1)S(1)} %get-tuple-element.35), channel_id=1, source_target_pairs={{0,8},{8,0},{16,24},{24,16},{32,40},{40,32},{48,56},{56,48},{64,72... | collective-permute-start | bytes 393224 | tf_op jit(solution)/shard_map/ppermute | solution.py:39
  133.3 8.0 %collective-permute-start.9 = (bf16[512,256]{1,0:T(8,128)(2,1)S(1)}, bf16[512,256]{1,0:T(8,128)(2,1)S(1)}, u32[]{:S(2)}, u32[]{:S(2)}) collective-permute-start(bf16[512,256]{1,0:T(8,128)(2,1)S(1)} %bitcast.31), channel_id=1, source_target_pairs={{0,1},{1,0},{2,3},{3,2},{4,5},{5,4},{6,7},{7,6},{8,9},{9,8},{10,11... | collective-permute-start | bytes 786440 | tf_op jit(solution)/shard_map/ppermute | solution.py:63

commit v3 on v2

--- a/solution.py
+++ b/solution.py
@@ -94,6 +94,22 @@
     )(tiles)
 
 
+def for_live_slots(count, product, add):
+    def four(g, carry):
+        slots = [4 * g + i for i in range(4)]
+        values = [product(s) for s in slots]
+        for s, v in zip(slots, values):
+            add(s, v)
+        return carry
+
+    def one(s, carry):
+        add(s, product(s))
+        return carry
+
+    lax.fori_loop(0, count >> 2, four, 0)
+    lax.fori_loop(count & ~3, count, one, 0)
+
+
 def forward_kernel(meta, tiles, own, odd, skip, far, mine, theirs, panels, acc, sems):
     copies = copy_in(
         [own, odd, skip, far],
@@ -104,11 +120,13 @@
     for c in copies:
         c.wait()
 
-    def slot(s, carry):
-        acc[meta[s]] += jnp.dot(tiles[s], panels[meta[SLOTS + s]], preferred_element_type=F32)
-        return carry
-
-    lax.fori_loop(0, meta[2 * SLOTS], slot, 0)
+    def product(s):
+        return jnp.dot(tiles[s], panels[meta[SLOTS + s]], preferred_element_type=F32)
+
+    def add(s, value):
+        acc[meta[s]] += value
+
+    for_live_slots(meta[2 * SLOTS], product, add)
     mine[...] = acc[0:4]
     theirs[...] = acc[4:8].astype(BF16)
 
@@ -205,23 +223,25 @@
     )(mine, theirs)
 
 
-def backward_kernel(meta, tiles, same, other, own, odd, skip, far, panels, acc, sems):
+def backward_kernel(meta, tiles, same, other, own, odd, skip, panels, acc, sems):
     copies = copy_in([same, other], [panels.at[0:4], panels.at[4:8]], sems)
     acc[...] = jnp.zeros_like(acc)
     for c in copies:
         c.wait()
 
-    def slot(s, carry):
-        acc[meta[SLOTS + s]] += lax.dot_general(
+    def product(s):
+        return lax.dot_general(
             tiles[s], panels[meta[s]], (((0,), (0,)), ((), ())), preferred_element_type=F32
         )
-        return carry
-
-    lax.fori_loop(0, meta[2 * SLOTS], slot, 0)
+
+    def add(s, value):
+        acc[meta[SLOTS + s]] += value
+
+    for_live_slots(meta[2 * SLOTS], product, add)
     own[...] = acc[0:2]
-    odd[...] = acc[2:4].astype(BF16)
-    skip[...] = acc[4:6].astype(BF16)
-    far[...] = acc[6:7].astype(BF16)
+    odd[0:2] = acc[2:4].astype(BF16)
+    odd[2:3] = acc[6:7].astype(BF16)
+    skip[...] = acc[4:6]
 
 
 def backward(meta, tiles, same, other):
@@ -229,12 +249,11 @@
         backward_kernel,
         out_shape=(
             jax.ShapeDtypeStruct((2, TILE, FEAT), F32),
-            jax.ShapeDtypeStruct((2, TILE, FEAT), BF16),
-            jax.ShapeDtypeStruct((2, TILE, FEAT), BF16),
-            jax.ShapeDtypeStruct((1, TILE, FEAT), BF16),
+            jax.ShapeDtypeStruct((3, TILE, FEAT), BF16),
+            jax.ShapeDtypeStruct((2, TILE, FEAT), F32),
         ),
         in_specs=[SMEM_SPEC, VMEM_SPEC] + [ANY_SPEC] * 2,
-        out_specs=(VMEM_SPEC,) * 4,
+        out_specs=(VMEM_SPEC,) * 3,
         scratch_shapes=[
             pltpu.VMEM((BANDS, TILE, FEAT), BF16),
             pltpu.VMEM((WINDOW, TILE, FEAT), F32),
@@ -243,6 +262,24 @@
         compiler_params=params(),
         name="backward_tiles",
     )(meta, tiles, same, other)
+
+
+def relay_kernel(parity, skip, odd, out):
+    p = parity[0]
+    q = 1 - p
+    out[p] = (skip[p] + odd[2].astype(F32)).astype(BF16)
+    out[q] = skip[q].astype(BF16)
+
+
+def relay_sum(parity, skip, odd):
+    return pl.pallas_call(
+        relay_kernel,
+        out_shape=jax.ShapeDtypeStruct((2, TILE, FEAT), BF16),
+        in_specs=[SMEM_SPEC] + [VMEM_SPEC] * 2,
+        out_specs=VMEM_SPEC,
+        compiler_params=params(),
+        name="relay_sum",
+    )(parity, skip, odd)
 
 
 def pair_kernel(parity, own, odd, skip, mine, sibling):
@@ -377,17 +414,18 @@
     same = exchange(mids, "x")
     arrived = exchange(chip_sum(w_mine, swapped(w_theirs)), SPREAD)
     other = swapped(same)
-    own_g, odd_g, skip_g, far_g = backward(meta, tiles, same, other)
-    arrived = after(arrived, far_g)
-    far_in = moved(far_g, to_far)
+    own_g, odd_g, skip_g = backward(meta, tiles, same, other)
+    arrived = after(arrived, odd_g)
+    side_row = parity.reshape(1)
     odd_in = moved(odd_g, to_odd)
-    skip_in = moved(skip_g, from_skip)
-    keep, sibling = pair_sum(parity.reshape(1), own_g, odd_in, skip_in)
-    sibling_in = moved(sibling, to_sibling)
-    grad_features = (keep + far_in[0].astype(F32) + sibling_in.astype(F32)).astype(BF16)
+    skip_out = relay_sum(side_row, skip_g, odd_in)
+    skip_in = moved(skip_out, from_skip)
+    keep, sibling = pair_sum(side_row, own_g, odd_in, skip_in)
+    grad_features = (keep + moved(sibling, to_sibling).astype(F32)).astype(BF16)
 
     spread = middle_sum(arrived, copies)
-    final, bias_total = last_sum(after(exchange(spread, REST), (odd_in, skip_in, far_in)), groups)
+    summed_in = after(exchange(spread, REST), skip_out)
+    final, bias_total = last_sum(summed_in, groups)
     w_half = exchange(final, SPREAD).reshape(FEAT, HALF)
     grad_weight = join(side, w_half, swapped(w_half))
     return (layer_out, grad_weight, bias_total.reshape(FEAT), grad_features)

time: 143 us -> 137 us (0.958)
  starting transfers between devices: 84.4 us -> 69.5 us
  waiting for transfers between devices: 25 us -> 33.9 us
  Pallas kernels: 9.42 us -> 7.75 us
    ppermute x7 -> x6, waiting for transfers between devices: 10.2 us -> 26.3 us  [moved(): lax.ppermute(block, ROW, [(i, target(i) % size) for i in range(size)])]
    ppermute x7 -> x6, starting transfers between devices: 43.8 us -> 32.4 us  [moved(): lax.ppermute(block, ROW, [(i, target(i) % size) for i in range(size)])]
    all_to_all x4, waiting for transfers between devices: 10.2 us -> 3.43 us  [exchange(): return lax.all_to_all(chunks, axis, 0, 0, tiled=True)]
    ppermute x4, starting transfers between devices: 20.6 us -> 17.1 us  [swapped(): return lax.ppermute(block, 'core', [(0, 1), (1, 0)])]
  transfers between devices with their start and end apart: 15 -> 14, of which waited for: 9 -> 9; matrix products, arithmetic and copies ran while one was open for 1% -> 1% of each run, Pallas kernels for 3% -> 2%
where the time goes in v3:
time: 137 us; the launch traced here: 136 us
  starting transfers between devices  69.5 us (51%)
  waiting for transfers between devices  33.9 us (25%)
  blocking collectives  19.5 us (14%)
  Pallas kernels  7.75 us (6%)
  local copies, waits for them, and re-layouts  2.4 us (2%)
  between operations  1.52 us (1%)
    ppermute x6, starting transfers between devices, moved(): lax.ppermute(block, ROW, [(i, target(i) % size) for i in range(size)])  32.4 us
    ppermute x6, waiting for transfers between devices, moved(): lax.ppermute(block, ROW, [(i, target(i) % size) for i in range(size)])  26.3 us
    all_to_all x4, starting transfers between devices, exchange(): return lax.all_to_all(chunks, axis, 0, 0, tiled=True)  20 us
    ppermute x4, starting transfers between devices, swapped(): return lax.ppermute(block, 'core', [(0, 1), (1, 0)])  17.1 us
    all_to_all x1, blocking collectives, exchange(): return lax.all_to_all(chunks, axis, 0, 0, tiled=True)  13.1 us
    all_gather x1, blocking collectives, body(): own = lax.all_gather(features, PAIR, axis=0, tiled=False)  6.34 us
    ppermute x4, waiting for transfers between devices, swapped(): return lax.ppermute(block, 'core', [(0, 1), (1, 0)])  4.18 us
    all_to_all x4, waiting for transfers between devices, exchange(): return lax.all_to_all(chunks, axis, 0, 0, tiled=True)  3.43 us
  transfers between devices with their start and end apart: 14, of which 9 were waited for; matrix products, arithmetic and copies ran while one was open for 1% of the time, Pallas kernels for 2%

profile of v3, /device:TPU:1, one launch (start us, length us, event | category | flops | bytes accessed | tf_op | source)
XLA Modules:
  0.0 135.5 jit_solution(16189985113805694663)
XLA Ops:
  0.6 6.3 %all-gather = bf16[256,512]{1,0:T(8,128)(2,1)S(1)} all-gather(bf16[128,512]{1,0:T(8,128)(2,1)} %param.7), channel_id=2, replica_groups=mesh['y'=8,'z'=4,'pair'=2,'x'=4,'core'=2] {'pair'}, dimensions={0}, use_global_device_ids=true | all-gather | bytes 393216 | tf_op jit(solution)/shard_map/all_gather | solution.py:400
  7.0 13.4 %collective-permute-start.1 = (bf16[2,128,512]{2,1,0:T(8,128)(2,1)S(1)}, bf16[2,128,512]{2,1,0:T(8,128)(2,1)S(1)}, u32[]{:S(2)}, u32[]{:S(2)}) collective-permute-start(bf16[2,128,512]{2,1,0:T(8,128)(2,1)S(1)} %bitcast.25), channel_id=1, source_target_pairs={{0,496},{8,24},{16,0},{24,40},{32,16},{40,56},{48,32},{56,72},{64,... | collective-permute-start | bytes 786440 | tf_op jit(solution)/shard_map/ppermute | solution.py:39
  20.4 1.9 %collective-permute-start = (bf16[2,128,512]{2,1,0:T(8,128)(2,1)S(1)}, bf16[2,128,512]{2,1,0:T(8,128)(2,1)S(1)}, u32[]{:S(2)}, u32[]{:S(2)}) collective-permute-start(bf16[2,128,512]{2,1,0:T(8,128)(2,1)S(1)} %bitcast.26), channel_id=1, source_target_pairs={{0,504},{8,16},{16,8},{24,32},{32,24},{40,48},{48,40},{56,64},{64,... | collective-permute-start | bytes 786440 | tf_op jit(solution)/shard_map/ppermute | solution.py:39
  22.4 4.0 %collective-permute-start.2 = (bf16[1,128,512]{2,1,0:T(8,128)(2,1)S(1)}, bf16[1,128,512]{2,1,0:T(8,128)(2,1)S(1)}, u32[]{:S(2)}, u32[]{:S(2)}) collective-permute-start(bf16[1,128,512]{2,1,0:T(8,128)(2,1)S(1)} %bitcast.32), channel_id=1, source_target_pairs={{0,488},{8,32},{16,504},{24,48},{32,8},{40,64},{48,24},{56,80},{64... | collective-permute-start | bytes 393224 | tf_op jit(solution)/shard_map/ppermute | solution.py:39
  27.7 1.0 copy-done
  28.9 5.9 %collective-permute-done.2.far = bf16[1,128,512]{2,1,0:T(8,128)(2,1)S(1)} collective-permute-done((bf16[1,128,512]{2,1,0:T(8,128)(2,1)S(1)}, bf16[1,128,512]{2,1,0:T(8,128)(2,1)S(1)}, u32[]{:S(2)}, u32[]{:S(2)}) %collective-permute-start.2) | collective-permute-done | bytes 131104 | tf_op jit(solution)/shard_map/ppermute | solution.py:39
  34.8 1.5 %aggregate_tiles.1 = (f32[4,128,512]{2,1,0:T(8,128)S(1)}, bf16[4,128,512]{2,1,0:T(8,128)(2,1)S(1)}) custom-call(s32[33]{0:T(128)S(1)} %pad_add_fusion.meta, bf16[16,128,128]{2,1,0:T(8,128)(2,1)S(1)} %stage_tiles.1.tiles, bf16[2,128,512]{2,1,0:T(8,128)(2,1)S(1)} %bitcast.27, bf16[2,128,512]{2,1,0:T(8,128)(2,1)S(1)} %collective-permute-done.odd, ...), custom_call_target="tpu_custom_call" | custom-call | tf_op jit(solution)/shard_map/aggregate_tiles/pallas_call | solution.py:135
  36.3 5.9 %collective-permute-start.3 = (bf16[4,128,512]{2,1,0:T(8,128)(2,1)S(1)}, bf16[4,128,512]{2,1,0:T(8,128)(2,1)S(1)}, u32[]{:S(2)}, u32[]{:S(2)}) collective-permute-start(bf16[4,128,512]{2,1,0:T(8,128)(2,1)S(1)} %get-tuple-element.20), channel_id=1, source_target_pairs={{0,1},{1,0},{2,3},{3,2},{4,5},{5,4},{6,7},{7,6},{8,9},{9,8},{10,11... | collective-permute-start | bytes 1572872 | tf_op jit(solution)/shard_map/ppermute | solution.py:63
  42.3 1.5 %collective-permute-done.3 = bf16[4,128,512]{2,1,0:T(8,128)(2,1)S(1)} collective-permute-done((bf16[4,128,512]{2,1,0:T(8,128)(2,1)S(1)}, bf16[4,128,512]{2,1,0:T(8,128)(2,1)S(1)}, u32[]{:S(2)}, u32[]{:S(2)}) %collective-permute-start.3) | collective-permute-done | bytes 524320 | tf_op jit(solution)/shard_map/ppermute | solution.py:63
  44.0 13.1 %all_to_all.25.parts = bf16[4,128,512]{2,1,0:T(8,128)(2,1)S(1)} all-to-all(bf16[4,128,512]{2,1,0:T(8,128)(2,1)S(1)} %add_convert_fusion), channel_id=1, replica_groups=mesh['y'=8,'z'=4,'pair'=2,'x'=4,'core'=2] {'x'}, dimensions={0} | all-to-all | bytes 1048576 | tf_op jit(solution)/shard_map/all_to_all | solution.py:67
  57.8 1.4 %dense_layer.1 = (bf16[128,512]{1,0:T(8,128)(2,1)}, bf16[4,128,512]{2,1,0:T(8,128)(2,1)}, f32[33,16,256]{2,1,0:T(8,128)S(1)}, bf16[33,16,256]{2,1,0:T(8,128)(2,1)S(1)}) custom-call(s32[1]{0:T(128)} %bitcast.core, bf16[4,128,512]{2,1,0:T(8,128)(2,1)S(1)} %all_to_all.25.parts, bf16[512,512]{1,0:T(8,128)(2,1)S(1)} %copy-done.1, f32[1,512]{1,0:T(1,128)S(1)} %bitcast.31, ...), custom_call_target="tpu_custom_call" | custom-call | tf_op jit(solution)/shard_map/dense_layer/pallas_call | solution.py:190
  59.2 3.5 %all-to-all-start.2 = ((bf16[4,128,512]{2,1,0:T(8,128)(2,1)}), bf16[4,128,512]{2,1,0:T(8,128)(2,1)S(1)}, u32[]{:S(2)}, u32[]{:S(2)}) async-start(bf16[4,128,512]{2,1,0:T(8,128)(2,1)} %get-tuple-element.24), calls=%async_computation.2 | async-start | bytes 1048576 | tf_op jit(solution)/shard_map/all_to_all | solution.py:67
  62.7 3.7 %collective-permute-start.4 = (bf16[33,16,256]{2,1,0:T(8,128)(2,1)S(1)}, bf16[33,16,256]{2,1,0:T(8,128)(2,1)S(1)}, u32[]{:S(2)}, u32[]{:S(2)}) collective-permute-start(bf16[33,16,256]{2,1,0:T(8,128)(2,1)S(1)} %get-tuple-element.23), channel_id=1, source_target_pairs={{0,1},{1,0},{2,3},{3,2},{4,5},{5,4},{6,7},{7,6},{8,9},{9,8},{10,11... | collective-permute-start | bytes 811016 | tf_op jit(solution)/shard_map/ppermute | solution.py:63
  66.4 1.2 collective-permute-done.4.theirs
  67.5 0.8 chip_sum.1
  68.4 1.7 %all-to-all-done.2.same = bf16[4,128,512]{2,1,0:T(8,128)(2,1)S(1)} async-done(((bf16[4,128,512]{2,1,0:T(8,128)(2,1)}), bf16[4,128,512]{2,1,0:T(8,128)(2,1)S(1)}, u32[]{:S(2)}, u32[]{:S(2)}) %all-to-all-start.2) | async-done | bytes 524320 | tf_op jit(solution)/shard_map/all_to_all | solution.py:67
  70.0 5.2 %all-to-all-start.1 = ((bf16[32,16,384]{2,1,0:T(8,128)(2,1)}), bf16[32,16,384]{2,1,0:T(8,128)(2,1)S(1)}, u32[]{:S(2)}, u32[]{:S(2)}) async-start(bf16[32,16,384]{2,1,0:T(8,128)(2,1)} %chip_sum.1), calls=%async_computation.1 | async-start | bytes 786432 | tf_op jit(solution)/shard_map/all_to_all | solution.py:67
  75.2 4.6 %collective-permute-start.5 = (bf16[4,128,512]{2,1,0:T(8,128)(2,1)S(1)}, bf16[4,128,512]{2,1,0:T(8,128)(2,1)S(1)}, u32[]{:S(2)}, u32[]{:S(2)}) collective-permute-start(bf16[4,128,512]{2,1,0:T(8,128)(2,1)S(1)} %all-to-all-done.2.same), channel_id=1, source_target_pairs={{0,1},{1,0},{2,3},{3,2},{4,5},{5,4},{6,7},{7,6},{8,9},{9,8},{10,11... | collective-permute-start | bytes 1572872 | tf_op jit(solution)/shard_map/ppermute | solution.py:63
  79.8 1.5 %collective-permute-done.5.other = bf16[4,128,512]{2,1,0:T(8,128)(2,1)S(1)} collective-permute-done((bf16[4,128,512]{2,1,0:T(8,128)(2,1)S(1)}, bf16[4,128,512]{2,1,0:T(8,128)(2,1)S(1)}, u32[]{:S(2)}, u32[]{:S(2)}) %collective-permute-start.5) | collective-permute-done | bytes 524320 | tf_op jit(solution)/shard_map/ppermute | solution.py:63
  81.3 1.4 %backward_tiles.1 = (f32[2,128,512]{2,1,0:T(8,128)S(1)}, bf16[3,128,512]{2,1,0:T(8,128)(2,1)S(1)}, f32[2,128,512]{2,1,0:T(8,128)S(1)}) custom-call(s32[33]{0:T(128)S(1)} %pad_add_fusion.meta, bf16[16,128,128]{2,1,0:T(8,128)(2,1)S(1)} %stage_tiles.1.tiles, bf16[4,128,512]{2,1,0:T(8,128)(2,1)S(1)} %all-to-all-done.2.same, ...), custom_call_target="tpu_custom_call" | custom-call | tf_op jit(solution)/shard_map/backward_tiles/pallas_call | solution.py:248
  82.7 8.1 %collective-permute-start.6 = (bf16[3,128,512]{2,1,0:T(8,128)(2,1)S(1)}, bf16[3,128,512]{2,1,0:T(8,128)(2,1)S(1)}, u32[]{:S(2)}, u32[]{:S(2)}) collective-permute-start(bf16[3,128,512]{2,1,0:T(8,128)(2,1)S(1)} %get-tuple-element.25), channel_id=1, source_target_pairs={{0,504},{8,16},{16,8},{24,32},{32,24},{40,48},{48,40},{56,64},{64,... | collective-permute-start | bytes 1179656 | tf_op jit(solution)/shard_map/ppermute | solution.py:39
  91.5 3.4 %all-to-all-start.3 = ((bf16[8,16,384]{2,1,0:T(8,128)(2,1)}), bf16[8,16,384]{2,1,0:T(8,128)(2,1)S(1)}, u32[]{:S(2)}, u32[]{:S(2)}) async-start(bf16[8,16,384]{2,1,0:T(8,128)(2,1)} %group_sum.1), calls=%async_computation.3 | async-start | bytes 196608 | tf_op jit(solution)/shard_map/all_to_all | solution.py:67
  94.9 5.7 %collective-permute-done.6.odd = bf16[3,128,512]{2,1,0:T(8,128)(2,1)S(1)} collective-permute-done((bf16[3,128,512]{2,1,0:T(8,128)(2,1)S(1)}, bf16[3,128,512]{2,1,0:T(8,128)(2,1)S(1)}, u32[]{:S(2)}, u32[]{:S(2)}) %collective-permute-start.6) | collective-permute-done | bytes 393248 | tf_op jit(solution)/shard_map/ppermute | solution.py:39
  100.6 1.8 %all-to-all-done.3.parts = bf16[8,16,384]{2,1,0:T(8,128)(2,1)S(1)} async-done(((bf16[8,16,384]{2,1,0:T(8,128)(2,1)}), bf16[8,16,384]{2,1,0:T(8,128)(2,1)S(1)}, u32[]{:S(2)}, u32[]{:S(2)}) %all-to-all-start.3) | async-done | bytes 98336 | tf_op jit(solution)/shard_map/all_to_all | solution.py:67
  102.4 0.7 total_sum.1
  103.1 7.9 %all-to-all-start.4 = ((bf16[32,16,256]{2,1,0:T(8,128)(2,1)}), bf16[32,16,256]{2,1,0:T(8,128)(2,1)S(1)}, u32[]{:S(2)}, u32[]{:S(2)}) async-start(bf16[32,16,256]{2,1,0:T(8,128)(2,1)} %get-tuple-element.29), calls=%async_computation.4 | async-start | bytes 524288 | tf_op jit(solution)/shard_map/all_to_all | solution.py:67
  111.1 3.1 %collective-permute-start.8 = (bf16[2,128,512]{2,1,0:T(8,128)(2,1)S(1)}, bf16[2,128,512]{2,1,0:T(8,128)(2,1)S(1)}, u32[]{:S(2)}, u32[]{:S(2)}) collective-permute-start(bf16[2,128,512]{2,1,0:T(8,128)(2,1)S(1)} %relay_sum.1), channel_id=1, source_target_pairs={{0,16},{8,504},{16,32},{24,8},{32,48},{40,24},{48,64},{56,40},{64,... | collective-permute-start | bytes 786440 | tf_op jit(solution)/shard_map/ppermute | solution.py:39
  114.2 13.8 %collective-permute-done.8.skip = bf16[2,128,512]{2,1,0:T(8,128)(2,1)S(1)} collective-permute-done((bf16[2,128,512]{2,1,0:T(8,128)(2,1)S(1)}, bf16[2,128,512]{2,1,0:T(8,128)(2,1)S(1)}, u32[]{:S(2)}, u32[]{:S(2)}) %collective-permute-start.8) | collective-permute-done | bytes 262176 | tf_op jit(solution)/shard_map/ppermute | solution.py:39
  128.1 1.9 %collective-permute-start.9 = (bf16[128,512]{1,0:T(8,128)(2,1)S(1)}, bf16[128,512]{1,0:T(8,128)(2,1)S(1)}, u32[]{:S(2)}, u32[]{:S(2)}) collective-permute-start(bf16[128,512]{1,0:T(8,128)(2,1)S(1)} %get-tuple-element.33), channel_id=1, source_target_pairs={{0,8},{8,0},{16,24},{24,16},{32,40},{40,32},{48,56},{56,48},{64,72... | collective-permute-start | bytes 393224 | tf_op jit(solution)/shard_map/ppermute | solution.py:39
  130.0 2.9 %collective-permute-start.7 = (bf16[512,256]{1,0:T(8,128)(2,1)S(1)}, bf16[512,256]{1,0:T(8,128)(2,1)S(1)}, u32[]{:S(2)}, u32[]{:S(2)}) collective-permute-start(bf16[512,256]{1,0:T(8,128)(2,1)S(1)} %bitcast.28), channel_id=1, source_target_pairs={{0,1},{1,0},{2,3},{3,2},{4,5},{5,4},{6,7},{7,6},{8,9},{9,8},{10,11... | collective-permute-start | bytes 786440 | tf_op jit(solution)/shard_map/ppermute | solution.py:63
  132.9 0.9 collective-permute-done.9
  134.5 1.0 join_halves.1
  (25 shorter events, 3.2 us)
Async XLA Ops:
  0.6 21.7 %copy-start.4 = (bf16[128,512]{1,0:T(8,128)(2,1)S(1)}, bf16[128,512]{1,0:T(8,128)(2,1)}, u32[]{:S(2)}) copy-start(bf16[128,512]{1,0:T(8,128)(2,1)} %param.7) | copy-start | bytes 393220
  7.0 27.8 %collective-permute-start.1 = (bf16[2,128,512]{2,1,0:T(8,128)(2,1)S(1)}, bf16[2,128,512]{2,1,0:T(8,128)(2,1)S(1)}, u32[]{:S(2)}, u32[]{:S(2)}) collective-permute-start(bf16[2,128,512]{2,1,0:T(8,128)(2,1)S(1)} %bitcast.25), channel_id=1, source_target_pairs={{0,496},{8,24},{16,0},{24,40},{32,16},{40,56},{48,32},{56,72},{64,... | collective-permute-start | bytes 786440 | tf_op jit(solution)/shard_map/ppermute | solution.py:39
  20.4 14.4 %collective-permute-start = (bf16[2,128,512]{2,1,0:T(8,128)(2,1)S(1)}, bf16[2,128,512]{2,1,0:T(8,128)(2,1)S(1)}, u32[]{:S(2)}, u32[]{:S(2)}) collective-permute-start(bf16[2,128,512]{2,1,0:T(8,128)(2,1)S(1)} %bitcast.26), channel_id=1, source_target_pairs={{0,504},{8,16},{16,8},{24,32},{32,24},{40,48},{48,40},{56,64},{64,... | collective-permute-start | bytes 786440 | tf_op jit(solution)/shard_map/ppermute | solution.py:39
  22.4 12.4 %collective-permute-start.2 = (bf16[1,128,512]{2,1,0:T(8,128)(2,1)S(1)}, bf16[1,128,512]{2,1,0:T(8,128)(2,1)S(1)}, u32[]{:S(2)}, u32[]{:S(2)}) collective-permute-start(bf16[1,128,512]{2,1,0:T(8,128)(2,1)S(1)} %bitcast.32), channel_id=1, source_target_pairs={{0,488},{8,32},{16,504},{24,48},{32,8},{40,64},{48,24},{56,80},{64... | collective-permute-start | bytes 393224 | tf_op jit(solution)/shard_map/ppermute | solution.py:39
  26.4 0.7 copy-start.5
  27.7 1.0 copy-start
  36.3 7.4 %collective-permute-start.3 = (bf16[4,128,512]{2,1,0:T(8,128)(2,1)S(1)}, bf16[4,128,512]{2,1,0:T(8,128)(2,1)S(1)}, u32[]{:S(2)}, u32[]{:S(2)}) collective-permute-start(bf16[4,128,512]{2,1,0:T(8,128)(2,1)S(1)} %get-tuple-element.20), channel_id=1, source_target_pairs={{0,1},{1,0},{2,3},{3,2},{4,5},{5,4},{6,7},{7,6},{8,9},{9,8},{10,11... | collective-permute-start | bytes 1572872 | tf_op jit(solution)/shard_map/ppermute | solution.py:63
  44.0 13.2 %copy-start.1 = (bf16[512,512]{1,0:T(8,128)(2,1)S(1)}, bf16[512,512]{1,0:T(8,128)(2,1)}, u32[]{:S(2)}) copy-start(bf16[512,512]{1,0:T(8,128)(2,1)} %weight.1) | copy-start | bytes 1572868
  44.0 13.2 %copy-start.2 = (bf16[128,512]{1,0:T(8,128)(2,1)S(1)}, bf16[128,512]{1,0:T(8,128)(2,1)}, u32[]{:S(2)}) copy-start(bf16[128,512]{1,0:T(8,128)(2,1)} %cot.1) | copy-start | bytes 393220
  57.1 0.7 copy-start.3
  59.2 10.8 %all-to-all-start.2 = ((bf16[4,128,512]{2,1,0:T(8,128)(2,1)}), bf16[4,128,512]{2,1,0:T(8,128)(2,1)S(1)}, u32[]{:S(2)}, u32[]{:S(2)}) async-start(bf16[4,128,512]{2,1,0:T(8,128)(2,1)} %get-tuple-element.24), calls=%async_computation.2 | async-start | bytes 1048576 | tf_op jit(solution)/shard_map/all_to_all | solution.py:67
  62.7 4.9 %collective-permute-start.4 = (bf16[33,16,256]{2,1,0:T(8,128)(2,1)S(1)}, bf16[33,16,256]{2,1,0:T(8,128)(2,1)S(1)}, u32[]{:S(2)}, u32[]{:S(2)}) collective-permute-start(bf16[33,16,256]{2,1,0:T(8,128)(2,1)S(1)} %get-tuple-element.23), channel_id=1, source_target_pairs={{0,1},{1,0},{2,3},{3,2},{4,5},{5,4},{6,7},{7,6},{8,9},{9,8},{10,11... | collective-permute-start | bytes 811016 | tf_op jit(solution)/shard_map/ppermute | solution.py:63
  70.0 20.8 %all-to-all-start.1 = ((bf16[32,16,384]{2,1,0:T(8,128)(2,1)}), bf16[32,16,384]{2,1,0:T(8,128)(2,1)S(1)}, u32[]{:S(2)}, u32[]{:S(2)}) async-start(bf16[32,16,384]{2,1,0:T(8,128)(2,1)} %chip_sum.1), calls=%async_computation.1 | async-start | bytes 786432 | tf_op jit(solution)/shard_map/all_to_all | solution.py:67
  75.2 6.1 %collective-permute-start.5 = (bf16[4,128,512]{2,1,0:T(8,128)(2,1)S(1)}, bf16[4,128,512]{2,1,0:T(8,128)(2,1)S(1)}, u32[]{:S(2)}, u32[]{:S(2)}) collective-permute-start(bf16[4,128,512]{2,1,0:T(8,128)(2,1)S(1)} %all-to-all-done.2.same), channel_id=1, source_target_pairs={{0,1},{1,0},{2,3},{3,2},{4,5},{5,4},{6,7},{7,6},{8,9},{9,8},{10,11... | collective-permute-start | bytes 1572872 | tf_op jit(solution)/shard_map/ppermute | solution.py:63
  82.7 17.9 %collective-permute-start.6 = (bf16[3,128,512]{2,1,0:T(8,128)(2,1)S(1)}, bf16[3,128,512]{2,1,0:T(8,128)(2,1)S(1)}, u32[]{:S(2)}, u32[]{:S(2)}) collective-permute-start(bf16[3,128,512]{2,1,0:T(8,128)(2,1)S(1)} %get-tuple-element.25), channel_id=1, source_target_pairs={{0,504},{8,16},{16,8},{24,32},{32,24},{40,48},{48,40},{56,64},{64,... | collective-permute-start | bytes 1179656 | tf_op jit(solution)/shard_map/ppermute | solution.py:39
  91.5 10.9 %all-to-all-start.3 = ((bf16[8,16,384]{2,1,0:T(8,128)(2,1)}), bf16[8,16,384]{2,1,0:T(8,128)(2,1)S(1)}, u32[]{:S(2)}, u32[]{:S(2)}) async-start(bf16[8,16,384]{2,1,0:T(8,128)(2,1)} %group_sum.1), calls=%async_computation.3 | async-start | bytes 196608 | tf_op jit(solution)/shard_map/all_to_all | solution.py:67
  103.1 26.9 %all-to-all-start.4 = ((bf16[32,16,256]{2,1,0:T(8,128)(2,1)}), bf16[32,16,256]{2,1,0:T(8,128)(2,1)S(1)}, u32[]{:S(2)}, u32[]{:S(2)}) async-start(bf16[32,16,256]{2,1,0:T(8,128)(2,1)} %get-tuple-element.29), calls=%async_computation.4 | async-start | bytes 524288 | tf_op jit(solution)/shard_map/all_to_all | solution.py:67
  111.1 16.9 %collective-permute-start.8 = (bf16[2,128,512]{2,1,0:T(8,128)(2,1)S(1)}, bf16[2,128,512]{2,1,0:T(8,128)(2,1)S(1)}, u32[]{:S(2)}, u32[]{:S(2)}) collective-permute-start(bf16[2,128,512]{2,1,0:T(8,128)(2,1)S(1)} %relay_sum.1), channel_id=1, source_target_pairs={{0,16},{8,504},{16,32},{24,8},{32,48},{40,24},{48,64},{56,40},{64,... | collective-permute-start | bytes 786440 | tf_op jit(solution)/shard_map/ppermute | solution.py:39
  128.1 5.7 %collective-permute-start.9 = (bf16[128,512]{1,0:T(8,128)(2,1)S(1)}, bf16[128,512]{1,0:T(8,128)(2,1)S(1)}, u32[]{:S(2)}, u32[]{:S(2)}) collective-permute-start(bf16[128,512]{1,0:T(8,128)(2,1)S(1)} %get-tuple-element.33), channel_id=1, source_target_pairs={{0,8},{8,0},{16,24},{24,16},{32,40},{40,32},{48,56},{56,48},{64,72... | collective-permute-start | bytes 393224 | tf_op jit(solution)/shard_map/ppermute | solution.py:39
  130.0 4.5 %collective-permute-start.7 = (bf16[512,256]{1,0:T(8,128)(2,1)S(1)}, bf16[512,256]{1,0:T(8,128)(2,1)S(1)}, u32[]{:S(2)}, u32[]{:S(2)}) collective-permute-start(bf16[512,256]{1,0:T(8,128)(2,1)S(1)} %bitcast.28), channel_id=1, source_target_pairs={{0,1},{1,0},{2,3},{3,2},{4,5},{5,4},{6,7},{7,6},{8,9},{9,8},{10,11... | collective-permute-start | bytes 786440 | tf_op jit(solution)/shard_map/ppermute | solution.py:63

commit v4 on v3

--- a/solution.py
+++ b/solution.py
@@ -15,8 +15,8 @@
 COL = ("x", "core")
 ALL = ROW + COL
 PAIR = "pair"
-SPREAD = ("y", "x")
-REST = ("z", "pair")
+SPREAD = ("z", "pair", "x")
+REST = ("y",)
 EXTRA = 128
 HALF = 256
 BF16 = jnp.bfloat16
@@ -76,22 +76,24 @@
     return copies
 
 
-def stage_kernel(source, out, sem):
-    copy = pltpu.make_async_copy(source, out, sem)
-    copy.start()
-    copy.wait()
-
-
-def stage(tiles):
+def stage_kernel(tiles, bias, tiles_out, bias_out, sems):
+    for c in copy_in([tiles, bias], [tiles_out, bias_out], sems):
+        c.wait()
+
+
+def stage(tiles, bias):
     return pl.pallas_call(
         stage_kernel,
-        out_shape=jax.ShapeDtypeStruct(tiles.shape, tiles.dtype),
-        in_specs=[HBM_SPEC],
-        out_specs=VMEM_SPEC,
-        scratch_shapes=[pltpu.SemaphoreType.DMA],
+        out_shape=(
+            jax.ShapeDtypeStruct(tiles.shape, tiles.dtype),
+            jax.ShapeDtypeStruct(bias.shape, bias.dtype),
+        ),
+        in_specs=[HBM_SPEC] * 2,
+        out_specs=(VMEM_SPEC,) * 2,
+        scratch_shapes=[pltpu.SemaphoreType.DMA((2,))],
         compiler_params=params(),
         name="stage_tiles",
-    )(tiles)
+    )(tiles, bias)
 
 
 def for_live_slots(count, product, add):
@@ -110,9 +112,25 @@
     lax.fori_loop(count & ~3, count, one, 0)
 
 
-def forward_kernel(meta, tiles, own, odd, skip, far, mine, theirs, panels, acc, sems):
+def bundle_kernel(parity, own, skip, out):
+    out[0:2] = own[...]
+    out[2] = skip[parity[0]]
+
+
+def bundle(parity, own, skip):
+    return pl.pallas_call(
+        bundle_kernel,
+        out_shape=jax.ShapeDtypeStruct((3, TILE, FEAT), BF16),
+        in_specs=[SMEM_SPEC] + [VMEM_SPEC] * 2,
+        out_specs=VMEM_SPEC,
+        compiler_params=params(),
+        name="bundle_panels",
+    )(parity, own, skip)
+
+
+def forward_kernel(meta, tiles, own, odd, skip, mine, theirs, panels, acc, sems):
     copies = copy_in(
-        [own, odd, skip, far],
+        [own, odd.at[0:2], skip, odd.at[2:3]],
         [panels.at[0:2], panels.at[2:4], panels.at[4:6], panels.at[6:7]],
         sems,
     )
@@ -131,14 +149,14 @@
     theirs[...] = acc[4:8].astype(BF16)
 
 
-def forward(meta, tiles, own, odd, skip, far):
+def forward(meta, tiles, own, odd, skip):
     return pl.pallas_call(
         forward_kernel,
         out_shape=(
             jax.ShapeDtypeStruct((BANDS // 2, TILE, FEAT), F32),
             jax.ShapeDtypeStruct((BANDS // 2, TILE, FEAT), BF16),
         ),
-        in_specs=[SMEM_SPEC, VMEM_SPEC] + [ANY_SPEC] * 4,
+        in_specs=[SMEM_SPEC, VMEM_SPEC] + [ANY_SPEC] * 3,
         out_specs=(VMEM_SPEC,) * 2,
         scratch_shapes=[
             pltpu.VMEM((WINDOW, TILE, FEAT), BF16),
@@ -147,7 +165,7 @@
         ],
         compiler_params=params(),
         name="aggregate_tiles",
-    )(meta, tiles, own, odd, skip, far)
+    )(meta, tiles, own, odd, skip)
 
 
 def bias_rows(total):
@@ -379,7 +397,7 @@
     core = lax.axis_index("core")
     parity = own_row & 1
     pair_row = own_row - parity
-    tiles = stage(tile_vals[0, 0])
+    tiles, bias = stage(tile_vals[0, 0], bias_vec.reshape(1, FEAT))
     coords = tile_coords[0, 0]
     block = coords[:, 0]
     block_at = (block & 1 ^ core) * (BANDS // 2) + (block >> 1)
@@ -398,17 +416,17 @@
     meta = jnp.concatenate([block_at, panel_at, tile_count.reshape(1)])
 
     own = lax.all_gather(features, PAIR, axis=0, tiled=False)
-    far = moved(features[None], to_far)
-    odd = moved(own, to_odd)
+    side_row = parity.reshape(1)
     skip = moved(own, to_skip)
-    mine, theirs = forward(meta, tiles, own, odd, skip, far)
+    odd = moved(bundle(side_row, own, skip), to_odd)
+    mine, theirs = forward(meta, tiles, own, odd, skip)
     half = (mine + swapped(theirs).astype(F32)).astype(BF16)
     parts = exchange(half, "x")
-    groups = lax.axis_size("y") * lax.axis_size("x")
-    copies = lax.axis_size("z") * lax.axis_size("pair")
+    groups = lax.axis_size(SPREAD)
+    copies = lax.axis_size(REST)
     side = core.reshape(1)
     layer_out, mids, w_mine, w_theirs = dense(
-        side, parts, weight, bias_vec.reshape(1, FEAT), cotangent, groups
+        side, parts, weight, bias, cotangent, groups
     )
 
     same = exchange(mids, "x")
@@ -416,7 +434,6 @@
     other = swapped(same)
     own_g, odd_g, skip_g = backward(meta, tiles, same, other)
     arrived = after(arrived, odd_g)
-    side_row = parity.reshape(1)
     odd_in = moved(odd_g, to_odd)
     skip_out = relay_sum(side_row, skip_g, odd_in)
     skip_in = moved(skip_out, from_skip)

time: 137 us -> 133 us (0.971)
  local copies, waits for them, and re-layouts: 2.4 us -> 0.69 us
    ppermute x6 -> x5, waiting for transfers between devices: 26.3 us -> 22.7 us  [moved(): lax.ppermute(block, ROW, [(i, target(i) % size) for i in range(size)])]
    all_to_all x4, waiting for transfers between devices: 3.43 us -> 5.95 us  [exchange(): return lax.all_to_all(chunks, axis, 0, 0, tiled=True)]
    all_to_all x4, starting transfers between devices: 20 us -> 17.6 us  [exchange(): return lax.all_to_all(chunks, axis, 0, 0, tiled=True)]
    unnamed x12 -> x10, local copies, waits for them, and re-layouts: 2.4 us -> 0.69 us
    ppermute x6 -> x5, starting transfers between devices: 32.4 us -> 34 us  [moved(): lax.ppermute(block, ROW, [(i, target(i) % size) for i in range(size)])]
    ppermute x4, starting transfers between devices: 17.1 us -> 18.5 us  [swapped(): return lax.ppermute(block, 'core', [(0, 1), (1, 0)])]
  transfers between devices with their start and end apart: 14 -> 13, of which waited for: 9 -> 10; matrix products, arithmetic and copies ran while one was open for 1% -> 1% of each run, Pallas kernels for 2% -> 2%
where the time goes in v4:
time: 133 us
  starting transfers between devices  70.1 us (53%)
  waiting for transfers between devices  33.3 us (25%)
  blocking collectives  18.4 us (14%)
  Pallas kernels  7.56 us (6%)
  between operations  1.52 us (1%)
    ppermute x5, starting transfers between devices, moved(): lax.ppermute(block, ROW, [(i, target(i) % size) for i in range(size)])  34 us
    ppermute x5, waiting for transfers between devices, moved(): lax.ppermute(block, ROW, [(i, target(i) % size) for i in range(size)])  22.7 us
    ppermute x4, starting transfers between devices, swapped(): return lax.ppermute(block, 'core', [(0, 1), (1, 0)])  18.5 us
    all_to_all x4, starting transfers between devices, exchange(): return lax.all_to_all(chunks, axis, 0, 0, tiled=True)  17.6 us
    all_to_all x1, blocking collectives, exchange(): return lax.all_to_all(chunks, axis, 0, 0, tiled=True)  12.2 us
    all_gather x1, blocking collectives, body(): own = lax.all_gather(features, PAIR, axis=0, tiled=False)  6.21 us
    all_to_all x4, waiting for transfers between devices, exchange(): return lax.all_to_all(chunks, axis, 0, 0, tiled=True)  5.95 us
    ppermute x4, waiting for transfers between devices, swapped(): return lax.ppermute(block, 'core', [(0, 1), (1, 0)])  4.63 us
  transfers between devices with their start and end apart: 13, of which 10 were waited for; matrix products, arithmetic and copies ran while one was open for 1% of the time, Pallas kernels for 2%

profile of v4, /device:TPU:1, one launch (start us, length us, event | category | flops | bytes accessed | tf_op | source)
XLA Modules:
  0.0 132.6 jit_solution(2276414758628486210)
XLA Ops:
  0.6 6.2 %all-gather = bf16[256,512]{1,0:T(8,128)(2,1)S(1)} all-gather(bf16[128,512]{1,0:T(8,128)(2,1)} %param.7), channel_id=2, replica_groups=mesh['y'=8,'z'=4,'pair'=2,'x'=4,'core'=2] {'pair'}, dimensions={0}, use_global_device_ids=true | all-gather | bytes 393216 | tf_op jit(solution)/shard_map/all_gather | solution.py:418
  6.8 13.6 %collective-permute-start = (bf16[2,128,512]{2,1,0:T(8,128)(2,1)S(1)}, bf16[2,128,512]{2,1,0:T(8,128)(2,1)S(1)}, u32[]{:S(2)}, u32[]{:S(2)}) collective-permute-start(bf16[2,128,512]{2,1,0:T(8,128)(2,1)S(1)} %bitcast.24), channel_id=1, source_target_pairs={{0,496},{8,24},{16,0},{24,40},{32,16},{40,56},{48,32},{56,72},{64,... | collective-permute-start | bytes 786440 | tf_op jit(solution)/shard_map/ppermute | solution.py:39
  20.4 4.0 %collective-permute-done.skip = bf16[2,128,512]{2,1,0:T(8,128)(2,1)S(1)} collective-permute-done((bf16[2,128,512]{2,1,0:T(8,128)(2,1)S(1)}, bf16[2,128,512]{2,1,0:T(8,128)(2,1)S(1)}, u32[]{:S(2)}, u32[]{:S(2)}) %collective-permute-start) | collective-permute-done | bytes 262176 | tf_op jit(solution)/shard_map/ppermute | solution.py:39
  24.5 5.0 %collective-permute-start.1 = (bf16[3,128,512]{2,1,0:T(8,128)(2,1)S(1)}, bf16[3,128,512]{2,1,0:T(8,128)(2,1)S(1)}, u32[]{:S(2)}, u32[]{:S(2)}) collective-permute-start(bf16[3,128,512]{2,1,0:T(8,128)(2,1)S(1)} %bundle_panels.1), channel_id=1, source_target_pairs={{0,504},{8,16},{16,8},{24,32},{32,24},{40,48},{48,40},{56,64},{64,... | collective-permute-start | bytes 1179656 | tf_op jit(solution)/shard_map/ppermute | solution.py:39
  31.0 6.8 %collective-permute-done.1.odd = bf16[3,128,512]{2,1,0:T(8,128)(2,1)S(1)} collective-permute-done((bf16[3,128,512]{2,1,0:T(8,128)(2,1)S(1)}, bf16[3,128,512]{2,1,0:T(8,128)(2,1)S(1)}, u32[]{:S(2)}, u32[]{:S(2)}) %collective-permute-start.1) | collective-permute-done | bytes 393248 | tf_op jit(solution)/shard_map/ppermute | solution.py:39
  37.8 1.4 %aggregate_tiles.1 = (f32[4,128,512]{2,1,0:T(8,128)S(1)}, bf16[4,128,512]{2,1,0:T(8,128)(2,1)S(1)}) custom-call(s32[33]{0:T(128)S(1)} %pad_add_fusion.meta, bf16[16,128,128]{2,1,0:T(8,128)(2,1)S(1)} %get-tuple-element.21.tiles, bf16[2,128,512]{2,1,0:T(8,128)(2,1)S(1)} %bitcast.26, bf16[3,128,512]{2,1,0:T(8,128)(2,1)S(1)} %collective-permute-done.1.odd, ...), custom_call_target="tpu_custom_call" | custom-call | tf_op jit(solution)/shard_map/aggregate_tiles/pallas_call | solution.py:153
  39.3 5.6 %collective-permute-start.2 = (bf16[4,128,512]{2,1,0:T(8,128)(2,1)S(1)}, bf16[4,128,512]{2,1,0:T(8,128)(2,1)S(1)}, u32[]{:S(2)}, u32[]{:S(2)}) collective-permute-start(bf16[4,128,512]{2,1,0:T(8,128)(2,1)S(1)} %get-tuple-element.23), channel_id=1, source_target_pairs={{0,1},{1,0},{2,3},{3,2},{4,5},{5,4},{6,7},{7,6},{8,9},{9,8},{10,11... | collective-permute-start | bytes 1572872 | tf_op jit(solution)/shard_map/ppermute | solution.py:63
  44.8 1.5 %collective-permute-done.2 = bf16[4,128,512]{2,1,0:T(8,128)(2,1)S(1)} collective-permute-done((bf16[4,128,512]{2,1,0:T(8,128)(2,1)S(1)}, bf16[4,128,512]{2,1,0:T(8,128)(2,1)S(1)}, u32[]{:S(2)}, u32[]{:S(2)}) %collective-permute-start.2) | collective-permute-done | bytes 524320 | tf_op jit(solution)/shard_map/ppermute | solution.py:63
  46.6 12.2 %all_to_all.25.parts = bf16[4,128,512]{2,1,0:T(8,128)(2,1)S(1)} all-to-all(bf16[4,128,512]{2,1,0:T(8,128)(2,1)S(1)} %add_convert_fusion), channel_id=1, replica_groups=mesh['y'=8,'z'=4,'pair'=2,'x'=4,'core'=2] {'x'}, dimensions={0} | all-to-all | bytes 1048576 | tf_op jit(solution)/shard_map/all_to_all | solution.py:67
  58.8 1.4 %dense_layer.1 = (bf16[128,512]{1,0:T(8,128)(2,1)}, bf16[4,128,512]{2,1,0:T(8,128)(2,1)}, f32[33,16,256]{2,1,0:T(8,128)S(1)}, bf16[33,16,256]{2,1,0:T(8,128)(2,1)S(1)}) custom-call(s32[1]{0:T(128)} %bitcast.core, bf16[4,128,512]{2,1,0:T(8,128)(2,1)S(1)} %all_to_all.25.parts, bf16[512,512]{1,0:T(8,128)(2,1)S(1)} %copy-done.1, ...), custom_call_target="tpu_custom_call" | custom-call | tf_op jit(solution)/shard_map/dense_layer/pallas_call | solution.py:208
  60.2 3.5 %all-to-all-start.2 = ((bf16[4,128,512]{2,1,0:T(8,128)(2,1)}), bf16[4,128,512]{2,1,0:T(8,128)(2,1)S(1)}, u32[]{:S(2)}, u32[]{:S(2)}) async-start(bf16[4,128,512]{2,1,0:T(8,128)(2,1)} %get-tuple-element.28), calls=%async_computation.2 | async-start | bytes 1048576 | tf_op jit(solution)/shard_map/all_to_all | solution.py:67
  63.7 3.7 %collective-permute-start.3 = (bf16[33,16,256]{2,1,0:T(8,128)(2,1)S(1)}, bf16[33,16,256]{2,1,0:T(8,128)(2,1)S(1)}, u32[]{:S(2)}, u32[]{:S(2)}) collective-permute-start(bf16[33,16,256]{2,1,0:T(8,128)(2,1)S(1)} %get-tuple-element.27), channel_id=1, source_target_pairs={{0,1},{1,0},{2,3},{3,2},{4,5},{5,4},{6,7},{7,6},{8,9},{9,8},{10,11... | collective-permute-start | bytes 811016 | tf_op jit(solution)/shard_map/ppermute | solution.py:63
  67.4 1.2 collective-permute-done.3.theirs
  68.6 0.8 chip_sum.1
  69.4 1.7 %all-to-all-done.2.same = bf16[4,128,512]{2,1,0:T(8,128)(2,1)S(1)} async-done(((bf16[4,128,512]{2,1,0:T(8,128)(2,1)}), bf16[4,128,512]{2,1,0:T(8,128)(2,1)S(1)}, u32[]{:S(2)}, u32[]{:S(2)}) %all-to-all-start.2) | async-done | bytes 524320 | tf_op jit(solution)/shard_map/all_to_all | solution.py:67
  71.0 3.9 %all-to-all-start.1 = ((bf16[32,16,384]{2,1,0:T(8,128)(2,1)}), bf16[32,16,384]{2,1,0:T(8,128)(2,1)S(1)}, u32[]{:S(2)}, u32[]{:S(2)}) async-start(bf16[32,16,384]{2,1,0:T(8,128)(2,1)} %chip_sum.1), calls=%async_computation.1 | async-start | bytes 786432 | tf_op jit(solution)/shard_map/all_to_all | solution.py:67
  74.9 4.9 %collective-permute-start.4 = (bf16[4,128,512]{2,1,0:T(8,128)(2,1)S(1)}, bf16[4,128,512]{2,1,0:T(8,128)(2,1)S(1)}, u32[]{:S(2)}, u32[]{:S(2)}) collective-permute-start(bf16[4,128,512]{2,1,0:T(8,128)(2,1)S(1)} %all-to-all-done.2.same), channel_id=1, source_target_pairs={{0,1},{1,0},{2,3},{3,2},{4,5},{5,4},{6,7},{7,6},{8,9},{9,8},{10,11... | collective-permute-start | bytes 1572872 | tf_op jit(solution)/shard_map/ppermute | solution.py:63
  79.9 1.5 %collective-permute-done.4.other = bf16[4,128,512]{2,1,0:T(8,128)(2,1)S(1)} collective-permute-done((bf16[4,128,512]{2,1,0:T(8,128)(2,1)S(1)}, bf16[4,128,512]{2,1,0:T(8,128)(2,1)S(1)}, u32[]{:S(2)}, u32[]{:S(2)}) %collective-permute-start.4) | collective-permute-done | bytes 524320 | tf_op jit(solution)/shard_map/ppermute | solution.py:63
  81.4 1.3 backward_tiles.1
  82.7 7.2 %collective-permute-start.5 = (bf16[3,128,512]{2,1,0:T(8,128)(2,1)S(1)}, bf16[3,128,512]{2,1,0:T(8,128)(2,1)S(1)}, u32[]{:S(2)}, u32[]{:S(2)}) collective-permute-start(bf16[3,128,512]{2,1,0:T(8,128)(2,1)S(1)} %get-tuple-element.29), channel_id=1, source_target_pairs={{0,504},{8,16},{16,8},{24,32},{32,24},{40,48},{48,40},{56,64},{64,... | collective-permute-start | bytes 1179656 | tf_op jit(solution)/shard_map/ppermute | solution.py:39
  89.9 0.7 group_sum.1
  90.6 4.2 %all-to-all-start.3 = ((bf16[8,16,384]{2,1,0:T(8,128)(2,1)}), bf16[8,16,384]{2,1,0:T(8,128)(2,1)S(1)}, u32[]{:S(2)}, u32[]{:S(2)}) async-start(bf16[8,16,384]{2,1,0:T(8,128)(2,1)} %group_sum.1), calls=%async_computation.3 | async-start | bytes 196608 | tf_op jit(solution)/shard_map/all_to_all | solution.py:67
  94.8 3.4 %collective-permute-done.5.odd = bf16[3,128,512]{2,1,0:T(8,128)(2,1)S(1)} collective-permute-done((bf16[3,128,512]{2,1,0:T(8,128)(2,1)S(1)}, bf16[3,128,512]{2,1,0:T(8,128)(2,1)S(1)}, u32[]{:S(2)}, u32[]{:S(2)}) %collective-permute-start.5) | collective-permute-done | bytes 393248 | tf_op jit(solution)/shard_map/ppermute | solution.py:39
  98.2 4.3 %all-to-all-done.3.parts = bf16[8,16,384]{2,1,0:T(8,128)(2,1)S(1)} async-done(((bf16[8,16,384]{2,1,0:T(8,128)(2,1)}), bf16[8,16,384]{2,1,0:T(8,128)(2,1)S(1)}, u32[]{:S(2)}, u32[]{:S(2)}) %all-to-all-start.3) | async-done | bytes 98336 | tf_op jit(solution)/shard_map/all_to_all | solution.py:67
  102.5 0.7 total_sum.1
  103.2 6.0 %all-to-all-start.4 = ((bf16[32,16,256]{2,1,0:T(8,128)(2,1)}), bf16[32,16,256]{2,1,0:T(8,128)(2,1)S(1)}, u32[]{:S(2)}, u32[]{:S(2)}) async-start(bf16[32,16,256]{2,1,0:T(8,128)(2,1)} %get-tuple-element.33), calls=%async_computation.4 | async-start | bytes 524288 | tf_op jit(solution)/shard_map/all_to_all | solution.py:67
  109.2 4.0 %collective-permute-start.7 = (bf16[2,128,512]{2,1,0:T(8,128)(2,1)S(1)}, bf16[2,128,512]{2,1,0:T(8,128)(2,1)S(1)}, u32[]{:S(2)}, u32[]{:S(2)}) collective-permute-start(bf16[2,128,512]{2,1,0:T(8,128)(2,1)S(1)} %relay_sum.1), channel_id=1, source_target_pairs={{0,16},{8,504},{16,32},{24,8},{32,48},{40,24},{48,64},{56,40},{64,... | collective-permute-start | bytes 786440 | tf_op jit(solution)/shard_map/ppermute | solution.py:39
  113.3 8.5 %collective-permute-done.7.skip = bf16[2,128,512]{2,1,0:T(8,128)(2,1)S(1)} collective-permute-done((bf16[2,128,512]{2,1,0:T(8,128)(2,1)S(1)}, bf16[2,128,512]{2,1,0:T(8,128)(2,1)S(1)}, u32[]{:S(2)}, u32[]{:S(2)}) %collective-permute-start.7) | collective-permute-done | bytes 262176 | tf_op jit(solution)/shard_map/ppermute | solution.py:39
  121.9 4.2 %collective-permute-start.8 = (bf16[128,512]{1,0:T(8,128)(2,1)S(1)}, bf16[128,512]{1,0:T(8,128)(2,1)S(1)}, u32[]{:S(2)}, u32[]{:S(2)}) collective-permute-start(bf16[128,512]{1,0:T(8,128)(2,1)S(1)} %get-tuple-element.37), channel_id=1, source_target_pairs={{0,8},{8,0},{16,24},{24,16},{32,40},{40,32},{48,56},{56,48},{64,72... | collective-permute-start | bytes 393224 | tf_op jit(solution)/shard_map/ppermute | solution.py:39
  126.1 4.2 %collective-permute-start.6 = (bf16[512,256]{1,0:T(8,128)(2,1)S(1)}, bf16[512,256]{1,0:T(8,128)(2,1)S(1)}, u32[]{:S(2)}, u32[]{:S(2)}) collective-permute-start(bf16[512,256]{1,0:T(8,128)(2,1)S(1)} %bitcast.27), channel_id=1, source_target_pairs={{0,1},{1,0},{2,3},{3,2},{4,5},{5,4},{6,7},{7,6},{8,9},{9,8},{10,11... | collective-permute-start | bytes 786440 | tf_op jit(solution)/shard_map/ppermute | solution.py:63
  130.4 0.7 add_convert_fusion.1
  131.5 1.0 join_halves.1
  (22 shorter events, 1.6 us)
Async XLA Ops:
  6.8 23.4 %copy-start = (bf16[1,1,16,128,128]{4,3,2,1,0:T(8,128)(2,1)S(1)}, bf16[1,1,16,128,128]{4,3,2,1,0:T(8,128)(2,1)}, u32[]{:S(2)}) copy-start(bf16[1,1,16,128,128]{4,3,2,1,0:T(8,128)(2,1)} %param.10) | copy-start | bytes 1572868
  6.8 17.6 %collective-permute-start = (bf16[2,128,512]{2,1,0:T(8,128)(2,1)S(1)}, bf16[2,128,512]{2,1,0:T(8,128)(2,1)S(1)}, u32[]{:S(2)}, u32[]{:S(2)}) collective-permute-start(bf16[2,128,512]{2,1,0:T(8,128)(2,1)S(1)} %bitcast.24), channel_id=1, source_target_pairs={{0,496},{8,24},{16,0},{24,40},{32,16},{40,56},{48,32},{56,72},{64,... | collective-permute-start | bytes 786440 | tf_op jit(solution)/shard_map/ppermute | solution.py:39
  24.5 5.0 %copy-start.4 = (s32[1,1,16,2]{2,3,1,0:T(2,128)S(1)}, s32[1,1,16,2]{2,3,1,0:T(2,128)}, u32[]{:S(2)}) copy-start(s32[1,1,16,2]{2,3,1,0:T(2,128)} %param.11) | copy-start | bytes 388
  24.5 13.4 %collective-permute-start.1 = (bf16[3,128,512]{2,1,0:T(8,128)(2,1)S(1)}, bf16[3,128,512]{2,1,0:T(8,128)(2,1)S(1)}, u32[]{:S(2)}, u32[]{:S(2)}) collective-permute-start(bf16[3,128,512]{2,1,0:T(8,128)(2,1)S(1)} %bundle_panels.1), channel_id=1, source_target_pairs={{0,504},{8,16},{16,8},{24,32},{32,24},{40,48},{48,40},{56,64},{64,... | collective-permute-start | bytes 1179656 | tf_op jit(solution)/shard_map/ppermute | solution.py:39
  30.2 0.7 copy-start.3
  39.3 7.1 %collective-permute-start.2 = (bf16[4,128,512]{2,1,0:T(8,128)(2,1)S(1)}, bf16[4,128,512]{2,1,0:T(8,128)(2,1)S(1)}, u32[]{:S(2)}, u32[]{:S(2)}) collective-permute-start(bf16[4,128,512]{2,1,0:T(8,128)(2,1)S(1)} %get-tuple-element.23), channel_id=1, source_target_pairs={{0,1},{1,0},{2,3},{3,2},{4,5},{5,4},{6,7},{7,6},{8,9},{9,8},{10,11... | collective-permute-start | bytes 1572872 | tf_op jit(solution)/shard_map/ppermute | solution.py:63
  46.6 12.2 %copy-start.1 = (bf16[512,512]{1,0:T(8,128)(2,1)S(1)}, bf16[512,512]{1,0:T(8,128)(2,1)}, u32[]{:S(2)}) copy-start(bf16[512,512]{1,0:T(8,128)(2,1)} %weight.1) | copy-start | bytes 1572868
  46.6 12.2 %copy-start.2 = (bf16[128,512]{1,0:T(8,128)(2,1)S(1)}, bf16[128,512]{1,0:T(8,128)(2,1)}, u32[]{:S(2)}) copy-start(bf16[128,512]{1,0:T(8,128)(2,1)} %cot.1) | copy-start | bytes 393220
  60.2 10.8 %all-to-all-start.2 = ((bf16[4,128,512]{2,1,0:T(8,128)(2,1)}), bf16[4,128,512]{2,1,0:T(8,128)(2,1)S(1)}, u32[]{:S(2)}, u32[]{:S(2)}) async-start(bf16[4,128,512]{2,1,0:T(8,128)(2,1)} %get-tuple-element.28), calls=%async_computation.2 | async-start | bytes 1048576 | tf_op jit(solution)/shard_map/all_to_all | solution.py:67
  63.7 4.9 %collective-permute-start.3 = (bf16[33,16,256]{2,1,0:T(8,128)(2,1)S(1)}, bf16[33,16,256]{2,1,0:T(8,128)(2,1)S(1)}, u32[]{:S(2)}, u32[]{:S(2)}) collective-permute-start(bf16[33,16,256]{2,1,0:T(8,128)(2,1)S(1)} %get-tuple-element.27), channel_id=1, source_target_pairs={{0,1},{1,0},{2,3},{3,2},{4,5},{5,4},{6,7},{7,6},{8,9},{9,8},{10,11... | collective-permute-start | bytes 811016 | tf_op jit(solution)/shard_map/ppermute | solution.py:63
  71.0 18.9 %all-to-all-start.1 = ((bf16[32,16,384]{2,1,0:T(8,128)(2,1)}), bf16[32,16,384]{2,1,0:T(8,128)(2,1)S(1)}, u32[]{:S(2)}, u32[]{:S(2)}) async-start(bf16[32,16,384]{2,1,0:T(8,128)(2,1)} %chip_sum.1), calls=%async_computation.1 | async-start | bytes 786432 | tf_op jit(solution)/shard_map/all_to_all | solution.py:67
  74.9 6.5 %collective-permute-start.4 = (bf16[4,128,512]{2,1,0:T(8,128)(2,1)S(1)}, bf16[4,128,512]{2,1,0:T(8,128)(2,1)S(1)}, u32[]{:S(2)}, u32[]{:S(2)}) collective-permute-start(bf16[4,128,512]{2,1,0:T(8,128)(2,1)S(1)} %all-to-all-done.2.same), channel_id=1, source_target_pairs={{0,1},{1,0},{2,3},{3,2},{4,5},{5,4},{6,7},{7,6},{8,9},{9,8},{10,11... | collective-permute-start | bytes 1572872 | tf_op jit(solution)/shard_map/ppermute | solution.py:63
  82.7 15.5 %collective-permute-start.5 = (bf16[3,128,512]{2,1,0:T(8,128)(2,1)S(1)}, bf16[3,128,512]{2,1,0:T(8,128)(2,1)S(1)}, u32[]{:S(2)}, u32[]{:S(2)}) collective-permute-start(bf16[3,128,512]{2,1,0:T(8,128)(2,1)S(1)} %get-tuple-element.29), channel_id=1, source_target_pairs={{0,504},{8,16},{16,8},{24,32},{32,24},{40,48},{48,40},{56,64},{64,... | collective-permute-start | bytes 1179656 | tf_op jit(solution)/shard_map/ppermute | solution.py:39
  90.6 11.9 %all-to-all-start.3 = ((bf16[8,16,384]{2,1,0:T(8,128)(2,1)}), bf16[8,16,384]{2,1,0:T(8,128)(2,1)S(1)}, u32[]{:S(2)}, u32[]{:S(2)}) async-start(bf16[8,16,384]{2,1,0:T(8,128)(2,1)} %group_sum.1), calls=%async_computation.3 | async-start | bytes 196608 | tf_op jit(solution)/shard_map/all_to_all | solution.py:67
  103.2 22.9 %all-to-all-start.4 = ((bf16[32,16,256]{2,1,0:T(8,128)(2,1)}), bf16[32,16,256]{2,1,0:T(8,128)(2,1)S(1)}, u32[]{:S(2)}, u32[]{:S(2)}) async-start(bf16[32,16,256]{2,1,0:T(8,128)(2,1)} %get-tuple-element.33), calls=%async_computation.4 | async-start | bytes 524288 | tf_op jit(solution)/shard_map/all_to_all | solution.py:67
  109.2 12.6 %collective-permute-start.7 = (bf16[2,128,512]{2,1,0:T(8,128)(2,1)S(1)}, bf16[2,128,512]{2,1,0:T(8,128)(2,1)S(1)}, u32[]{:S(2)}, u32[]{:S(2)}) collective-permute-start(bf16[2,128,512]{2,1,0:T(8,128)(2,1)S(1)} %relay_sum.1), channel_id=1, source_target_pairs={{0,16},{8,504},{16,32},{24,8},{32,48},{40,24},{48,64},{56,40},{64,... | collective-permute-start | bytes 786440 | tf_op jit(solution)/shard_map/ppermute | solution.py:39
  121.9 8.5 %collective-permute-start.8 = (bf16[128,512]{1,0:T(8,128)(2,1)S(1)}, bf16[128,512]{1,0:T(8,128)(2,1)S(1)}, u32[]{:S(2)}, u32[]{:S(2)}) collective-permute-start(bf16[128,512]{1,0:T(8,128)(2,1)S(1)} %get-tuple-element.37), channel_id=1, source_target_pairs={{0,8},{8,0},{16,24},{24,16},{32,40},{40,32},{48,56},{56,48},{64,72... | collective-permute-start | bytes 393224 | tf_op jit(solution)/shard_map/ppermute | solution.py:39
  126.1 5.4 %collective-permute-start.6 = (bf16[512,256]{1,0:T(8,128)(2,1)S(1)}, bf16[512,256]{1,0:T(8,128)(2,1)S(1)}, u32[]{:S(2)}, u32[]{:S(2)}) collective-permute-start(bf16[512,256]{1,0:T(8,128)(2,1)S(1)} %bitcast.27), channel_id=1, source_target_pairs={{0,1},{1,0},{2,3},{3,2},{4,5},{5,4},{6,7},{7,6},{8,9},{9,8},{10,11... | collective-permute-start | bytes 786440 | tf_op jit(solution)/shard_map/ppermute | solution.py:63

commit v5 on v4

--- a/solution.py
+++ b/solution.py
@@ -112,25 +112,24 @@
     lax.fori_loop(count & ~3, count, one, 0)
 
 
-def bundle_kernel(parity, own, skip, out):
-    out[0:2] = own[...]
-    out[2] = skip[parity[0]]
-
-
-def bundle(parity, own, skip):
-    return pl.pallas_call(
-        bundle_kernel,
-        out_shape=jax.ShapeDtypeStruct((3, TILE, FEAT), BF16),
-        in_specs=[SMEM_SPEC] + [VMEM_SPEC] * 2,
+def pick_kernel(parity, skip, out):
+    out[0] = skip[parity[0]]
+
+
+def pick(parity, skip):
+    return pl.pallas_call(
+        pick_kernel,
+        out_shape=jax.ShapeDtypeStruct((1, TILE, FEAT), BF16),
+        in_specs=[SMEM_SPEC, VMEM_SPEC],
         out_specs=VMEM_SPEC,
         compiler_params=params(),
-        name="bundle_panels",
-    )(parity, own, skip)
-
-
-def forward_kernel(meta, tiles, own, odd, skip, mine, theirs, panels, acc, sems):
+        name="pick_panel",
+    )(parity, skip)
+
+
+def forward_kernel(meta, tiles, own, odd, skip, far, mine, theirs, panels, acc, sems):
     copies = copy_in(
-        [own, odd.at[0:2], skip, odd.at[2:3]],
+        [own, odd, skip, far],
         [panels.at[0:2], panels.at[2:4], panels.at[4:6], panels.at[6:7]],
         sems,
     )
@@ -149,14 +148,14 @@
     theirs[...] = acc[4:8].astype(BF16)
 
 
-def forward(meta, tiles, own, odd, skip):
+def forward(meta, tiles, own, odd, skip, far):
     return pl.pallas_call(
         forward_kernel,
         out_shape=(
             jax.ShapeDtypeStruct((BANDS // 2, TILE, FEAT), F32),
             jax.ShapeDtypeStruct((BANDS // 2, TILE, FEAT), BF16),
         ),
-        in_specs=[SMEM_SPEC, VMEM_SPEC] + [ANY_SPEC] * 3,
+        in_specs=[SMEM_SPEC, VMEM_SPEC] + [ANY_SPEC] * 4,
         out_specs=(VMEM_SPEC,) * 2,
         scratch_shapes=[
             pltpu.VMEM((WINDOW, TILE, FEAT), BF16),
@@ -165,7 +164,7 @@
         ],
         compiler_params=params(),
         name="aggregate_tiles",
-    )(meta, tiles, own, odd, skip)
+    )(meta, tiles, own, odd, skip, far)
 
 
 def bias_rows(total):
@@ -418,8 +417,9 @@
     own = lax.all_gather(features, PAIR, axis=0, tiled=False)
     side_row = parity.reshape(1)
     skip = moved(own, to_skip)
-    odd = moved(bundle(side_row, own, skip), to_odd)
-    mine, theirs = forward(meta, tiles, own, odd, skip)
+    odd = moved(own, to_odd)
+    far = moved(pick(side_row, skip), to_odd)
+    mine, theirs = forward(meta, tiles, own, odd, skip, far)
     half = (mine + swapped(theirs).astype(F32)).astype(BF16)
     parts = exchange(half, "x")
     groups = lax.axis_size(SPREAD)
@@ -441,7 +441,7 @@
     grad_features = (keep + moved(sibling, to_sibling).astype(F32)).astype(BF16)
 
     spread = middle_sum(arrived, copies)
-    summed_in = after(exchange(spread, REST), skip_out)
+    summed_in = after(exchange(spread, REST), odd_in)
     final, bias_total = last_sum(summed_in, groups)
     w_half = exchange(final, SPREAD).reshape(FEAT, HALF)
     grad_weight = join(side, w_half, swapped(w_half))

time: 133 us -> 130 us (0.977)
  waiting for transfers between devices: 33.3 us -> 20 us
  blocking collectives: 18.4 us -> 30.6 us
  starting transfers between devices: 70.1 us -> 67.7 us
    all_to_all x1 -> x2, blocking collectives: 12.2 us -> 24.3 us  [exchange(): return lax.all_to_all(chunks, axis, 0, 0, tiled=True)]
    ppermute x5 -> x6, waiting for transfers between devices: 22.7 us -> 13.7 us  [moved(): lax.ppermute(block, ROW, [(i, target(i) % size) for i in range(size)])]
    all_to_all x4 -> x3, waiting for transfers between devices: 5.95 us -> 1.68 us  [exchange(): return lax.all_to_all(chunks, axis, 0, 0, tiled=True)]
    all_to_all x4 -> x3, starting transfers between devices: 17.6 us -> 13.4 us  [exchange(): return lax.all_to_all(chunks, axis, 0, 0, tiled=True)]
    ppermute x5 -> x6, starting transfers between devices: 34 us -> 35.6 us  [moved(): lax.ppermute(block, ROW, [(i, target(i) % size) for i in range(size)])]
  transfers between devices with their start and end apart: 13 -> 13, of which waited for: 10 -> 9; matrix products, arithmetic and copies ran while one was open for 1% -> 1% of each run, Pallas kernels for 2% -> 2%
where the time goes in v5:
time: 130 us
  starting transfers between devices  67.7 us (52%)
  blocking collectives  30.6 us (24%)
  waiting for transfers between devices  20 us (15%)
  Pallas kernels  7.36 us (6%)
  other arithmetic  1.66 us (1%)
  between operations  1.53 us (1%)
    ppermute x6, starting transfers between devices, moved(): lax.ppermute(block, ROW, [(i, target(i) % size) for i in range(size)])  35.6 us
    all_to_all x2, blocking collectives, exchange(): return lax.all_to_all(chunks, axis, 0, 0, tiled=True)  24.3 us
    ppermute x4, starting transfers between devices, swapped(): return lax.ppermute(block, 'core', [(0, 1), (1, 0)])  18.7 us
    ppermute x6, waiting for transfers between devices, moved(): lax.ppermute(block, ROW, [(i, target(i) % size) for i in range(size)])  13.7 us
    all_to_all x3, starting transfers between devices, exchange(): return lax.all_to_all(chunks, axis, 0, 0, tiled=True)  13.4 us
    all_gather x1, blocking collectives, body(): own = lax.all_gather(features, PAIR, axis=0, tiled=False)  6.34 us
    ppermute x4, waiting for transfers between devices, swapped(): return lax.ppermute(block, 'core', [(0, 1), (1, 0)])  4.63 us
  transfers between devices with their start and end apart: 13, of which 9 were waited for; matrix products, arithmetic and copies ran while one was open for 1% of the time, Pallas kernels for 2%

profile of v5, /device:TPU:1, one launch (start us, length us, event | category | flops | bytes accessed | tf_op | source)
XLA Modules:
  0.0 129.6 jit_solution(5638757498391979718)
XLA Ops:
  0.6 6.3 %all-gather = bf16[256,512]{1,0:T(8,128)(2,1)S(1)} all-gather(bf16[128,512]{1,0:T(8,128)(2,1)} %param.7), channel_id=2, replica_groups=mesh['y'=8,'z'=4,'pair'=2,'x'=4,'core'=2] {'pair'}, dimensions={0}, use_global_device_ids=true | all-gather | bytes 393216 | tf_op jit(solution)/shard_map/all_gather | solution.py:417
  7.0 13.4 %collective-permute-start.1 = (bf16[2,128,512]{2,1,0:T(8,128)(2,1)S(1)}, bf16[2,128,512]{2,1,0:T(8,128)(2,1)S(1)}, u32[]{:S(2)}, u32[]{:S(2)}) collective-permute-start(bf16[2,128,512]{2,1,0:T(8,128)(2,1)S(1)} %bitcast.24), channel_id=1, source_target_pairs={{0,496},{8,24},{16,0},{24,40},{32,16},{40,56},{48,32},{56,72},{64,... | collective-permute-start | bytes 786440 | tf_op jit(solution)/shard_map/ppermute | solution.py:39
  20.4 1.9 %collective-permute-start = (bf16[2,128,512]{2,1,0:T(8,128)(2,1)S(1)}, bf16[2,128,512]{2,1,0:T(8,128)(2,1)S(1)}, u32[]{:S(2)}, u32[]{:S(2)}) collective-permute-start(bf16[2,128,512]{2,1,0:T(8,128)(2,1)S(1)} %bitcast.25), channel_id=1, source_target_pairs={{0,504},{8,16},{16,8},{24,32},{32,24},{40,48},{48,40},{56,64},{64,... | collective-permute-start | bytes 786440 | tf_op jit(solution)/shard_map/ppermute | solution.py:39
  22.4 0.7 add_bitcast_fusion
  23.1 1.4 %collective-permute-done.1.skip = bf16[2,128,512]{2,1,0:T(8,128)(2,1)S(1)} collective-permute-done((bf16[2,128,512]{2,1,0:T(8,128)(2,1)S(1)}, bf16[2,128,512]{2,1,0:T(8,128)(2,1)S(1)}, u32[]{:S(2)}, u32[]{:S(2)}) %collective-permute-start.1) | collective-permute-done | bytes 262176 | tf_op jit(solution)/shard_map/ppermute | solution.py:39
  24.5 5.3 %collective-permute-start.2 = (bf16[1,128,512]{2,1,0:T(8,128)(2,1)S(1)}, bf16[1,128,512]{2,1,0:T(8,128)(2,1)S(1)}, u32[]{:S(2)}, u32[]{:S(2)}) collective-permute-start(bf16[1,128,512]{2,1,0:T(8,128)(2,1)S(1)} %pick_panel.1), channel_id=1, source_target_pairs={{0,504},{8,16},{16,8},{24,32},{32,24},{40,48},{48,40},{56,64},{64,... | collective-permute-start | bytes 393224 | tf_op jit(solution)/shard_map/ppermute | solution.py:39
  30.5 0.7 copy-done.3
  31.6 3.7 %collective-permute-done.2.far = bf16[1,128,512]{2,1,0:T(8,128)(2,1)S(1)} collective-permute-done((bf16[1,128,512]{2,1,0:T(8,128)(2,1)S(1)}, bf16[1,128,512]{2,1,0:T(8,128)(2,1)S(1)}, u32[]{:S(2)}, u32[]{:S(2)}) %collective-permute-start.2) | collective-permute-done | bytes 131104 | tf_op jit(solution)/shard_map/ppermute | solution.py:39
  35.3 1.6 %aggregate_tiles.1 = (f32[4,128,512]{2,1,0:T(8,128)S(1)}, bf16[4,128,512]{2,1,0:T(8,128)(2,1)S(1)}) custom-call(s32[33]{0:T(128)S(1)} %pad_add_fusion.meta, bf16[16,128,128]{2,1,0:T(8,128)(2,1)S(1)} %get-tuple-element.21.tiles, bf16[2,128,512]{2,1,0:T(8,128)(2,1)S(1)} %bitcast.26, bf16[2,128,512]{2,1,0:T(8,128)(2,1)S(1)} %collective-permute-done.odd, ...), custom_call_target="tpu_custom_call" | custom-call | tf_op jit(solution)/shard_map/aggregate_tiles/pallas_call | solution.py:152
  36.9 5.8 %collective-permute-start.3 = (bf16[4,128,512]{2,1,0:T(8,128)(2,1)S(1)}, bf16[4,128,512]{2,1,0:T(8,128)(2,1)S(1)}, u32[]{:S(2)}, u32[]{:S(2)}) collective-permute-start(bf16[4,128,512]{2,1,0:T(8,128)(2,1)S(1)} %get-tuple-element.23), channel_id=1, source_target_pairs={{0,1},{1,0},{2,3},{3,2},{4,5},{5,4},{6,7},{7,6},{8,9},{9,8},{10,11... | collective-permute-start | bytes 1572872 | tf_op jit(solution)/shard_map/ppermute | solution.py:63
  42.7 1.5 %collective-permute-done.3 = bf16[4,128,512]{2,1,0:T(8,128)(2,1)S(1)} collective-permute-done((bf16[4,128,512]{2,1,0:T(8,128)(2,1)S(1)}, bf16[4,128,512]{2,1,0:T(8,128)(2,1)S(1)}, u32[]{:S(2)}, u32[]{:S(2)}) %collective-permute-start.3) | collective-permute-done | bytes 524320 | tf_op jit(solution)/shard_map/ppermute | solution.py:63
  44.4 12.6 %all_to_all.25.parts = bf16[4,128,512]{2,1,0:T(8,128)(2,1)S(1)} all-to-all(bf16[4,128,512]{2,1,0:T(8,128)(2,1)S(1)} %add_convert_fusion), channel_id=1, replica_groups=mesh['y'=8,'z'=4,'pair'=2,'x'=4,'core'=2] {'x'}, dimensions={0} | all-to-all | bytes 1048576 | tf_op jit(solution)/shard_map/all_to_all | solution.py:67
  57.0 1.4 %dense_layer.1 = (bf16[128,512]{1,0:T(8,128)(2,1)}, bf16[4,128,512]{2,1,0:T(8,128)(2,1)}, f32[33,16,256]{2,1,0:T(8,128)S(1)}, bf16[33,16,256]{2,1,0:T(8,128)(2,1)S(1)}) custom-call(s32[1]{0:T(128)} %bitcast.core, bf16[4,128,512]{2,1,0:T(8,128)(2,1)S(1)} %all_to_all.25.parts, bf16[512,512]{1,0:T(8,128)(2,1)S(1)} %copy-done.1, ...), custom_call_target="tpu_custom_call" | custom-call | tf_op jit(solution)/shard_map/dense_layer/pallas_call | solution.py:207
  58.4 3.5 %all-to-all-start.2 = ((bf16[4,128,512]{2,1,0:T(8,128)(2,1)}), bf16[4,128,512]{2,1,0:T(8,128)(2,1)S(1)}, u32[]{:S(2)}, u32[]{:S(2)}) async-start(bf16[4,128,512]{2,1,0:T(8,128)(2,1)} %get-tuple-element.28), calls=%async_computation.2 | async-start | bytes 1048576 | tf_op jit(solution)/shard_map/all_to_all | solution.py:67
  61.9 3.7 %collective-permute-start.4 = (bf16[33,16,256]{2,1,0:T(8,128)(2,1)S(1)}, bf16[33,16,256]{2,1,0:T(8,128)(2,1)S(1)}, u32[]{:S(2)}, u32[]{:S(2)}) collective-permute-start(bf16[33,16,256]{2,1,0:T(8,128)(2,1)S(1)} %get-tuple-element.27), channel_id=1, source_target_pairs={{0,1},{1,0},{2,3},{3,2},{4,5},{5,4},{6,7},{7,6},{8,9},{9,8},{10,11... | collective-permute-start | bytes 811016 | tf_op jit(solution)/shard_map/ppermute | solution.py:63
  65.6 1.2 collective-permute-done.4.theirs
  66.8 0.8 chip_sum.1
  67.6 1.7 %all-to-all-done.2.same = bf16[4,128,512]{2,1,0:T(8,128)(2,1)S(1)} async-done(((bf16[4,128,512]{2,1,0:T(8,128)(2,1)}), bf16[4,128,512]{2,1,0:T(8,128)(2,1)S(1)}, u32[]{:S(2)}, u32[]{:S(2)}) %all-to-all-start.2) | async-done | bytes 524320 | tf_op jit(solution)/shard_map/all_to_all | solution.py:67
  69.2 3.9 %all-to-all-start.1 = ((bf16[32,16,384]{2,1,0:T(8,128)(2,1)}), bf16[32,16,384]{2,1,0:T(8,128)(2,1)S(1)}, u32[]{:S(2)}, u32[]{:S(2)}) async-start(bf16[32,16,384]{2,1,0:T(8,128)(2,1)} %chip_sum.1), calls=%async_computation.1 | async-start | bytes 786432 | tf_op jit(solution)/shard_map/all_to_all | solution.py:67
  73.1 4.9 %collective-permute-start.5 = (bf16[4,128,512]{2,1,0:T(8,128)(2,1)S(1)}, bf16[4,128,512]{2,1,0:T(8,128)(2,1)S(1)}, u32[]{:S(2)}, u32[]{:S(2)}) collective-permute-start(bf16[4,128,512]{2,1,0:T(8,128)(2,1)S(1)} %all-to-all-done.2.same), channel_id=1, source_target_pairs={{0,1},{1,0},{2,3},{3,2},{4,5},{5,4},{6,7},{7,6},{8,9},{9,8},{10,11... | collective-permute-start | bytes 1572872 | tf_op jit(solution)/shard_map/ppermute | solution.py:63
  78.1 1.5 %collective-permute-done.5.other = bf16[4,128,512]{2,1,0:T(8,128)(2,1)S(1)} collective-permute-done((bf16[4,128,512]{2,1,0:T(8,128)(2,1)S(1)}, bf16[4,128,512]{2,1,0:T(8,128)(2,1)S(1)}, u32[]{:S(2)}, u32[]{:S(2)}) %collective-permute-start.5) | collective-permute-done | bytes 524320 | tf_op jit(solution)/shard_map/ppermute | solution.py:63
  79.6 1.5 %backward_tiles.1 = (f32[2,128,512]{2,1,0:T(8,128)S(1)}, bf16[3,128,512]{2,1,0:T(8,128)(2,1)S(1)}, f32[2,128,512]{2,1,0:T(8,128)S(1)}) custom-call(s32[33]{0:T(128)S(1)} %pad_add_fusion.meta, bf16[16,128,128]{2,1,0:T(8,128)(2,1)S(1)} %get-tuple-element.21.tiles, bf16[4,128,512]{2,1,0:T(8,128)(2,1)S(1)} %all-to-all-done.2.same, ...), custom_call_target="tpu_custom_call" | custom-call | tf_op jit(solution)/shard_map/backward_tiles/pallas_call | solution.py:265
  81.1 6.5 %collective-permute-start.6 = (bf16[3,128,512]{2,1,0:T(8,128)(2,1)S(1)}, bf16[3,128,512]{2,1,0:T(8,128)(2,1)S(1)}, u32[]{:S(2)}, u32[]{:S(2)}) collective-permute-start(bf16[3,128,512]{2,1,0:T(8,128)(2,1)S(1)} %get-tuple-element.29), channel_id=1, source_target_pairs={{0,504},{8,16},{16,8},{24,32},{32,24},{40,48},{48,40},{56,64},{64,... | collective-permute-start | bytes 1179656 | tf_op jit(solution)/shard_map/ppermute | solution.py:39
  87.7 11.7 %all_to_all.26.parts = bf16[8,16,384]{2,1,0:T(8,128)(2,1)S(1)} all-to-all(bf16[8,16,384]{2,1,0:T(8,128)(2,1)S(1)} %group_sum.1), channel_id=1, replica_groups=mesh['y'=8,'z'=4,'pair'=2,'x'=4,'core'=2] {'y'}, dimensions={0} | all-to-all | bytes 196608 | tf_op jit(solution)/shard_map/all_to_all | solution.py:67
  99.4 0.7 total_sum.1
  100.1 6.0 %all-to-all-start.4 = ((bf16[32,16,256]{2,1,0:T(8,128)(2,1)}), bf16[32,16,256]{2,1,0:T(8,128)(2,1)S(1)}, u32[]{:S(2)}, u32[]{:S(2)}) async-start(bf16[32,16,256]{2,1,0:T(8,128)(2,1)} %get-tuple-element.32), calls=%async_computation.4 | async-start | bytes 524288 | tf_op jit(solution)/shard_map/all_to_all | solution.py:67
  106.2 4.0 %collective-permute-start.8 = (bf16[2,128,512]{2,1,0:T(8,128)(2,1)S(1)}, bf16[2,128,512]{2,1,0:T(8,128)(2,1)S(1)}, u32[]{:S(2)}, u32[]{:S(2)}) collective-permute-start(bf16[2,128,512]{2,1,0:T(8,128)(2,1)S(1)} %relay_sum.1), channel_id=1, source_target_pairs={{0,16},{8,504},{16,32},{24,8},{32,48},{40,24},{48,64},{56,40},{64,... | collective-permute-start | bytes 786440 | tf_op jit(solution)/shard_map/ppermute | solution.py:39
  110.3 8.3 %collective-permute-done.8.skip = bf16[2,128,512]{2,1,0:T(8,128)(2,1)S(1)} collective-permute-done((bf16[2,128,512]{2,1,0:T(8,128)(2,1)S(1)}, bf16[2,128,512]{2,1,0:T(8,128)(2,1)S(1)}, u32[]{:S(2)}, u32[]{:S(2)}) %collective-permute-start.8) | collective-permute-done | bytes 262176 | tf_op jit(solution)/shard_map/ppermute | solution.py:39
  118.7 4.4 %collective-permute-start.9 = (bf16[128,512]{1,0:T(8,128)(2,1)S(1)}, bf16[128,512]{1,0:T(8,128)(2,1)S(1)}, u32[]{:S(2)}, u32[]{:S(2)}) collective-permute-start(bf16[128,512]{1,0:T(8,128)(2,1)S(1)} %get-tuple-element.37), channel_id=1, source_target_pairs={{0,8},{8,0},{16,24},{24,16},{32,40},{40,32},{48,56},{56,48},{64,72... | collective-permute-start | bytes 393224 | tf_op jit(solution)/shard_map/ppermute | solution.py:39
  123.1 4.3 %collective-permute-start.7 = (bf16[512,256]{1,0:T(8,128)(2,1)S(1)}, bf16[512,256]{1,0:T(8,128)(2,1)S(1)}, u32[]{:S(2)}, u32[]{:S(2)}) collective-permute-start(bf16[512,256]{1,0:T(8,128)(2,1)S(1)} %bitcast.27), channel_id=1, source_target_pairs={{0,1},{1,0},{2,3},{3,2},{4,5},{5,4},{6,7},{7,6},{8,9},{9,8},{10,11... | collective-permute-start | bytes 786440 | tf_op jit(solution)/shard_map/ppermute | solution.py:63
  127.4 0.7 add_convert_fusion.1
  128.5 1.0 join_halves.1
  (23 shorter events, 1.4 us)
Async XLA Ops:
  0.6 29.8 %copy-start = (bf16[1,1,16,128,128]{4,3,2,1,0:T(8,128)(2,1)S(1)}, bf16[1,1,16,128,128]{4,3,2,1,0:T(8,128)(2,1)}, u32[]{:S(2)}) copy-start(bf16[1,1,16,128,128]{4,3,2,1,0:T(8,128)(2,1)} %param.10) | copy-start | bytes 1572868
  7.0 17.5 %collective-permute-start.1 = (bf16[2,128,512]{2,1,0:T(8,128)(2,1)S(1)}, bf16[2,128,512]{2,1,0:T(8,128)(2,1)S(1)}, u32[]{:S(2)}, u32[]{:S(2)}) collective-permute-start(bf16[2,128,512]{2,1,0:T(8,128)(2,1)S(1)} %bitcast.24), channel_id=1, source_target_pairs={{0,496},{8,24},{16,0},{24,40},{32,16},{40,56},{48,32},{56,72},{64,... | collective-permute-start | bytes 786440 | tf_op jit(solution)/shard_map/ppermute | solution.py:39
  20.4 11.2 %collective-permute-start = (bf16[2,128,512]{2,1,0:T(8,128)(2,1)S(1)}, bf16[2,128,512]{2,1,0:T(8,128)(2,1)S(1)}, u32[]{:S(2)}, u32[]{:S(2)}) collective-permute-start(bf16[2,128,512]{2,1,0:T(8,128)(2,1)S(1)} %bitcast.25), channel_id=1, source_target_pairs={{0,504},{8,16},{16,8},{24,32},{32,24},{40,48},{48,40},{56,64},{64,... | collective-permute-start | bytes 786440 | tf_op jit(solution)/shard_map/ppermute | solution.py:39
  24.4 5.3 %copy-start.4 = (s32[1,1,16,2]{2,3,1,0:T(2,128)S(1)}, s32[1,1,16,2]{2,3,1,0:T(2,128)}, u32[]{:S(2)}) copy-start(s32[1,1,16,2]{2,3,1,0:T(2,128)} %param.11) | copy-start | bytes 388
  24.5 10.8 %collective-permute-start.2 = (bf16[1,128,512]{2,1,0:T(8,128)(2,1)S(1)}, bf16[1,128,512]{2,1,0:T(8,128)(2,1)S(1)}, u32[]{:S(2)}, u32[]{:S(2)}) collective-permute-start(bf16[1,128,512]{2,1,0:T(8,128)(2,1)S(1)} %pick_panel.1), channel_id=1, source_target_pairs={{0,504},{8,16},{16,8},{24,32},{32,24},{40,48},{48,40},{56,64},{64,... | collective-permute-start | bytes 393224 | tf_op jit(solution)/shard_map/ppermute | solution.py:39
  30.4 0.7 copy-start.3
  36.9 7.3 %collective-permute-start.3 = (bf16[4,128,512]{2,1,0:T(8,128)(2,1)S(1)}, bf16[4,128,512]{2,1,0:T(8,128)(2,1)S(1)}, u32[]{:S(2)}, u32[]{:S(2)}) collective-permute-start(bf16[4,128,512]{2,1,0:T(8,128)(2,1)S(1)} %get-tuple-element.23), channel_id=1, source_target_pairs={{0,1},{1,0},{2,3},{3,2},{4,5},{5,4},{6,7},{7,6},{8,9},{9,8},{10,11... | collective-permute-start | bytes 1572872 | tf_op jit(solution)/shard_map/ppermute | solution.py:63
  44.4 12.6 %copy-start.1 = (bf16[512,512]{1,0:T(8,128)(2,1)S(1)}, bf16[512,512]{1,0:T(8,128)(2,1)}, u32[]{:S(2)}) copy-start(bf16[512,512]{1,0:T(8,128)(2,1)} %weight.1) | copy-start | bytes 1572868
  44.4 12.6 %copy-start.2 = (bf16[128,512]{1,0:T(8,128)(2,1)S(1)}, bf16[128,512]{1,0:T(8,128)(2,1)}, u32[]{:S(2)}) copy-start(bf16[128,512]{1,0:T(8,128)(2,1)} %cot.1) | copy-start | bytes 393220
  58.4 10.8 %all-to-all-start.2 = ((bf16[4,128,512]{2,1,0:T(8,128)(2,1)}), bf16[4,128,512]{2,1,0:T(8,128)(2,1)S(1)}, u32[]{:S(2)}, u32[]{:S(2)}) async-start(bf16[4,128,512]{2,1,0:T(8,128)(2,1)} %get-tuple-element.28), calls=%async_computation.2 | async-start | bytes 1048576 | tf_op jit(solution)/shard_map/all_to_all | solution.py:67
  61.9 4.9 %collective-permute-start.4 = (bf16[33,16,256]{2,1,0:T(8,128)(2,1)S(1)}, bf16[33,16,256]{2,1,0:T(8,128)(2,1)S(1)}, u32[]{:S(2)}, u32[]{:S(2)}) collective-permute-start(bf16[33,16,256]{2,1,0:T(8,128)(2,1)S(1)} %get-tuple-element.27), channel_id=1, source_target_pairs={{0,1},{1,0},{2,3},{3,2},{4,5},{5,4},{6,7},{7,6},{8,9},{9,8},{10,11... | collective-permute-start | bytes 811016 | tf_op jit(solution)/shard_map/ppermute | solution.py:63
  69.2 18.4 %all-to-all-start.1 = ((bf16[32,16,384]{2,1,0:T(8,128)(2,1)}), bf16[32,16,384]{2,1,0:T(8,128)(2,1)S(1)}, u32[]{:S(2)}, u32[]{:S(2)}) async-start(bf16[32,16,384]{2,1,0:T(8,128)(2,1)} %chip_sum.1), calls=%async_computation.1 | async-start | bytes 786432 | tf_op jit(solution)/shard_map/all_to_all | solution.py:67
  73.1 6.5 %collective-permute-start.5 = (bf16[4,128,512]{2,1,0:T(8,128)(2,1)S(1)}, bf16[4,128,512]{2,1,0:T(8,128)(2,1)S(1)}, u32[]{:S(2)}, u32[]{:S(2)}) collective-permute-start(bf16[4,128,512]{2,1,0:T(8,128)(2,1)S(1)} %all-to-all-done.2.same), channel_id=1, source_target_pairs={{0,1},{1,0},{2,3},{3,2},{4,5},{5,4},{6,7},{7,6},{8,9},{9,8},{10,11... | collective-permute-start | bytes 1572872 | tf_op jit(solution)/shard_map/ppermute | solution.py:63
  81.1 18.3 %collective-permute-start.6 = (bf16[3,128,512]{2,1,0:T(8,128)(2,1)S(1)}, bf16[3,128,512]{2,1,0:T(8,128)(2,1)S(1)}, u32[]{:S(2)}, u32[]{:S(2)}) collective-permute-start(bf16[3,128,512]{2,1,0:T(8,128)(2,1)S(1)} %get-tuple-element.29), channel_id=1, source_target_pairs={{0,504},{8,16},{16,8},{24,32},{32,24},{40,48},{48,40},{56,64},{64,... | collective-permute-start | bytes 1179656 | tf_op jit(solution)/shard_map/ppermute | solution.py:39
  100.1 22.9 %all-to-all-start.4 = ((bf16[32,16,256]{2,1,0:T(8,128)(2,1)}), bf16[32,16,256]{2,1,0:T(8,128)(2,1)S(1)}, u32[]{:S(2)}, u32[]{:S(2)}) async-start(bf16[32,16,256]{2,1,0:T(8,128)(2,1)} %get-tuple-element.32), calls=%async_computation.4 | async-start | bytes 524288 | tf_op jit(solution)/shard_map/all_to_all | solution.py:67
  106.2 12.4 %collective-permute-start.8 = (bf16[2,128,512]{2,1,0:T(8,128)(2,1)S(1)}, bf16[2,128,512]{2,1,0:T(8,128)(2,1)S(1)}, u32[]{:S(2)}, u32[]{:S(2)}) collective-permute-start(bf16[2,128,512]{2,1,0:T(8,128)(2,1)S(1)} %relay_sum.1), channel_id=1, source_target_pairs={{0,16},{8,504},{16,32},{24,8},{32,48},{40,24},{48,64},{56,40},{64,... | collective-permute-start | bytes 786440 | tf_op jit(solution)/shard_map/ppermute | solution.py:39
  118.7 8.7 %collective-permute-start.9 = (bf16[128,512]{1,0:T(8,128)(2,1)S(1)}, bf16[128,512]{1,0:T(8,128)(2,1)S(1)}, u32[]{:S(2)}, u32[]{:S(2)}) collective-permute-start(bf16[128,512]{1,0:T(8,128)(2,1)S(1)} %get-tuple-element.37), channel_id=1, source_target_pairs={{0,8},{8,0},{16,24},{24,16},{32,40},{40,32},{48,56},{56,48},{64,72... | collective-permute-start | bytes 393224 | tf_op jit(solution)/shard_map/ppermute | solution.py:39
  123.1 5.4 %collective-permute-start.7 = (bf16[512,256]{1,0:T(8,128)(2,1)S(1)}, bf16[512,256]{1,0:T(8,128)(2,1)S(1)}, u32[]{:S(2)}, u32[]{:S(2)}) collective-permute-start(bf16[512,256]{1,0:T(8,128)(2,1)S(1)} %bitcast.27), channel_id=1, source_target_pairs={{0,1},{1,0},{2,3},{3,2},{4,5},{5,4},{6,7},{7,6},{8,9},{9,8},{10,11... | collective-permute-start | bytes 786440 | tf_op jit(solution)/shard_map/ppermute | solution.py:63

commit v6 on v5

--- a/solution.py
+++ b/solution.py
@@ -172,11 +172,12 @@
     return jnp.concatenate([high, total - high, jnp.zeros((8, 128), F32)], axis=0).astype(BF16)
 
 
-def dense_kernel(core, parts, weight, bias, cot, layer_out, mids, mine, theirs, terms):
+def dense_kernel(parts, weight, bias, cot, layer_out, mids, agg_out, pre_out):
     agg = parts[0].astype(F32)
     for i in range(1, BANDS // 2):
         agg = agg + parts[i].astype(F32)
     agg_b = agg.astype(BF16)
+    agg_out[...] = agg_b
     w = weight[...]
     v = jnp.dot(agg_b, w, preferred_element_type=F32) + bias[...]
     v2 = v * v
@@ -185,39 +186,59 @@
     layer_out[...] = (v * half).astype(BF16)
     slope = half + 0.5 * v * (1.0 - t * t) * (SQRT_2_OVER_PI * (1.0 + 3 * 0.044715 * v2))
     grad_pre = (cot[...].astype(F32) * slope).astype(BF16)
+    pre_out[...] = grad_pre
     mid = lax.dot_general(
         grad_pre, w, (((1,), (1,)), ((), ())), preferred_element_type=F32
     ).astype(BF16)
     mids[...] = jnp.broadcast_to(mid[None], mids.shape)
-    term = lax.dot_general(agg_b, grad_pre, (((0,), (0,)), ((), ())), preferred_element_type=F32)
+
+
+def dense(parts, weight, bias, cot):
+    return pl.pallas_call(
+        dense_kernel,
+        out_shape=(
+            jax.ShapeDtypeStruct((TILE, FEAT), BF16),
+            jax.ShapeDtypeStruct((BANDS // 2, TILE, FEAT), BF16),
+            jax.ShapeDtypeStruct((TILE, FEAT), BF16),
+            jax.ShapeDtypeStruct((TILE, FEAT), BF16),
+        ),
+        in_specs=[VMEM_SPEC] * 4,
+        out_specs=(VMEM_SPEC,) * 4,
+        compiler_params=params(),
+        name="dense_layer",
+    )(parts, weight, bias, cot)
+
+
+def term_kernel(core, agg_b, grad_pre, mine, theirs, terms):
+    term = lax.dot_general(
+        agg_b[...], grad_pre[...], (((0,), (0,)), ((), ())), preferred_element_type=F32
+    )
     count = mine.shape[0] - 1
     for i in range(2):
         terms[i] = term[:, i * HALF : (i + 1) * HALF].reshape(count, 16, HALF)
     k = core[0]
     mine[0:count] = terms[k]
     theirs[0:count] = terms[1 - k].astype(BF16)
-    total = jnp.sum(grad_pre.astype(F32), axis=0, keepdims=True)
+    total = jnp.sum(grad_pre[...].astype(F32), axis=0, keepdims=True)
     total = jnp.concatenate([total[:, i * 128 : (i + 1) * 128] for i in range(4)], axis=0)
     zeros = jnp.zeros((16, HALF - EXTRA), F32)
     mine[count] = jnp.concatenate([bias_rows(total).astype(F32), zeros], axis=1)
     theirs[count] = jnp.concatenate([bias_rows(total), zeros.astype(BF16)], axis=1)
 
 
-def dense(core, parts, weight, bias, cot, groups):
-    return pl.pallas_call(
-        dense_kernel,
-        out_shape=(
-            jax.ShapeDtypeStruct((TILE, FEAT), BF16),
-            jax.ShapeDtypeStruct((BANDS // 2, TILE, FEAT), BF16),
+def weight_term(core, agg_b, grad_pre, groups):
+    return pl.pallas_call(
+        term_kernel,
+        out_shape=(
             jax.ShapeDtypeStruct((groups + 1, 16, HALF), F32),
             jax.ShapeDtypeStruct((groups + 1, 16, HALF), BF16),
         ),
-        in_specs=[SMEM_SPEC] + [VMEM_SPEC] * 4,
-        out_specs=(VMEM_SPEC,) * 4,
+        in_specs=[SMEM_SPEC] + [VMEM_SPEC] * 2,
+        out_specs=(VMEM_SPEC,) * 2,
         scratch_shapes=[pltpu.VMEM((2, groups, 16, HALF), F32)],
         compiler_params=params(),
-        name="dense_layer",
-    )(core, parts, weight, bias, cot)
+        name="weight_term",
+    )(core, agg_b, grad_pre)
 
 
 def chip_kernel(mine, theirs, out):
@@ -240,15 +261,14 @@
     )(mine, theirs)
 
 
-def backward_kernel(meta, tiles, same, other, own, odd, skip, panels, acc, sems):
-    copies = copy_in([same, other], [panels.at[0:4], panels.at[4:8]], sems)
+def backward_kernel(meta, tiles, same, other, own, odd, skip, acc):
     acc[...] = jnp.zeros_like(acc)
-    for c in copies:
-        c.wait()
 
     def product(s):
+        b = meta[s]
+        panel = lax.select(b < BANDS // 2, same[b & 3], other[b & 3])
         return lax.dot_general(
-            tiles[s], panels[meta[s]], (((0,), (0,)), ((), ())), preferred_element_type=F32
+            tiles[s], panel, (((0,), (0,)), ((), ())), preferred_element_type=F32
         )
 
     def add(s, value):
@@ -269,12 +289,10 @@
             jax.ShapeDtypeStruct((3, TILE, FEAT), BF16),
             jax.ShapeDtypeStruct((2, TILE, FEAT), F32),
         ),
-        in_specs=[SMEM_SPEC, VMEM_SPEC] + [ANY_SPEC] * 2,
+        in_specs=[SMEM_SPEC] + [VMEM_SPEC] * 3,
         out_specs=(VMEM_SPEC,) * 3,
         scratch_shapes=[
-            pltpu.VMEM((BANDS, TILE, FEAT), BF16),
             pltpu.VMEM((WINDOW, TILE, FEAT), F32),
-            pltpu.SemaphoreType.DMA((2,)),
         ],
         compiler_params=params(),
         name="backward_tiles",
@@ -425,9 +443,8 @@
     groups = lax.axis_size(SPREAD)
     copies = lax.axis_size(REST)
     side = core.reshape(1)
-    layer_out, mids, w_mine, w_theirs = dense(
-        side, parts, weight, bias, cotangent, groups
-    )
+    layer_out, mids, agg_b, grad_pre = dense(parts, weight, bias, cotangent)
+    w_mine, w_theirs = weight_term(side, agg_b, grad_pre, groups)
 
     same = exchange(mids, "x")
     arrived = exchange(chip_sum(w_mine, swapped(w_theirs)), SPREAD)

time: 130 us -> 131 us (level)
  starting transfers between devices: 67.7 us -> 69.1 us
    all_to_all x3, starting transfers between devices: 13.4 us -> 15 us  [exchange(): return lax.all_to_all(chunks, axis, 0, 0, tiled=True)]
where the time goes in v6:
time: 131 us; the launch traced here: 130 us
  starting transfers between devices  69.1 us (53%)
  blocking collectives  30.1 us (23%)
  waiting for transfers between devices  19.6 us (15%)
  Pallas kernels  7.38 us (6%)
  other arithmetic  1.66 us (1%)
  between operations  1.54 us (1%)
    ppermute x6, starting transfers between devices, moved(): lax.ppermute(block, ROW, [(i, target(i) % size) for i in range(size)])  35.3 us
    all_to_all x2, blocking collectives, exchange(): return lax.all_to_all(chunks, axis, 0, 0, tiled=True)  23.8 us
    ppermute x4, starting transfers between devices, swapped(): return lax.ppermute(block, 'core', [(0, 1), (1, 0)])  18.8 us
    all_to_all x3, starting transfers between devices, exchange(): return lax.all_to_all(chunks, axis, 0, 0, tiled=True)  15 us
    ppermute x6, waiting for transfers between devices, moved(): lax.ppermute(block, ROW, [(i, target(i) % size) for i in range(size)])  13.7 us
    all_gather x1, blocking collectives, body(): own = lax.all_gather(features, PAIR, axis=0, tiled=False)  6.34 us
    ppermute x4, waiting for transfers between devices, swapped(): return lax.ppermute(block, 'core', [(0, 1), (1, 0)])  4.63 us
  transfers between devices with their start and end apart: 13, of which 9 were waited for; matrix products, arithmetic and copies ran while one was open for 1% of the time, Pallas kernels for 2%

profile of v6, /device:TPU:1, one launch (start us, length us, event | category | flops | bytes accessed | tf_op | source)
XLA Modules:
  0.0 130.1 jit_solution(1135978596659646444)
XLA Ops:
  0.6 6.3 %all-gather = bf16[256,512]{1,0:T(8,128)(2,1)S(1)} all-gather(bf16[128,512]{1,0:T(8,128)(2,1)} %param.7), channel_id=2, replica_groups=mesh['y'=8,'z'=4,'pair'=2,'x'=4,'core'=2] {'pair'}, dimensions={0}, use_global_device_ids=true | all-gather | bytes 393216 | tf_op jit(solution)/shard_map/all_gather | solution.py:435
  7.0 13.4 %collective-permute-start.1 = (bf16[2,128,512]{2,1,0:T(8,128)(2,1)S(1)}, bf16[2,128,512]{2,1,0:T(8,128)(2,1)S(1)}, u32[]{:S(2)}, u32[]{:S(2)}) collective-permute-start(bf16[2,128,512]{2,1,0:T(8,128)(2,1)S(1)} %bitcast.24), channel_id=1, source_target_pairs={{0,496},{8,24},{16,0},{24,40},{32,16},{40,56},{48,32},{56,72},{64,... | collective-permute-start | bytes 786440 | tf_op jit(solution)/shard_map/ppermute | solution.py:39
  20.4 1.9 %collective-permute-start = (bf16[2,128,512]{2,1,0:T(8,128)(2,1)S(1)}, bf16[2,128,512]{2,1,0:T(8,128)(2,1)S(1)}, u32[]{:S(2)}, u32[]{:S(2)}) collective-permute-start(bf16[2,128,512]{2,1,0:T(8,128)(2,1)S(1)} %bitcast.25), channel_id=1, source_target_pairs={{0,504},{8,16},{16,8},{24,32},{32,24},{40,48},{48,40},{56,64},{64,... | collective-permute-start | bytes 786440 | tf_op jit(solution)/shard_map/ppermute | solution.py:39
  22.4 0.7 add_bitcast_fusion
  23.1 1.4 %collective-permute-done.1.skip = bf16[2,128,512]{2,1,0:T(8,128)(2,1)S(1)} collective-permute-done((bf16[2,128,512]{2,1,0:T(8,128)(2,1)S(1)}, bf16[2,128,512]{2,1,0:T(8,128)(2,1)S(1)}, u32[]{:S(2)}, u32[]{:S(2)}) %collective-permute-start.1) | collective-permute-done | bytes 262176 | tf_op jit(solution)/shard_map/ppermute | solution.py:39
  24.5 5.3 %collective-permute-start.2 = (bf16[1,128,512]{2,1,0:T(8,128)(2,1)S(1)}, bf16[1,128,512]{2,1,0:T(8,128)(2,1)S(1)}, u32[]{:S(2)}, u32[]{:S(2)}) collective-permute-start(bf16[1,128,512]{2,1,0:T(8,128)(2,1)S(1)} %pick_panel.1), channel_id=1, source_target_pairs={{0,504},{8,16},{16,8},{24,32},{32,24},{40,48},{48,40},{56,64},{64,... | collective-permute-start | bytes 393224 | tf_op jit(solution)/shard_map/ppermute | solution.py:39
  30.5 0.7 copy-done.3
  31.6 3.7 %collective-permute-done.2.far = bf16[1,128,512]{2,1,0:T(8,128)(2,1)S(1)} collective-permute-done((bf16[1,128,512]{2,1,0:T(8,128)(2,1)S(1)}, bf16[1,128,512]{2,1,0:T(8,128)(2,1)S(1)}, u32[]{:S(2)}, u32[]{:S(2)}) %collective-permute-start.2) | collective-permute-done | bytes 131104 | tf_op jit(solution)/shard_map/ppermute | solution.py:39
  35.3 1.5 %aggregate_tiles.1 = (f32[4,128,512]{2,1,0:T(8,128)S(1)}, bf16[4,128,512]{2,1,0:T(8,128)(2,1)S(1)}) custom-call(s32[33]{0:T(128)S(1)} %pad_add_fusion.meta, bf16[16,128,128]{2,1,0:T(8,128)(2,1)S(1)} %get-tuple-element.23.tiles, bf16[2,128,512]{2,1,0:T(8,128)(2,1)S(1)} %bitcast.26, bf16[2,128,512]{2,1,0:T(8,128)(2,1)S(1)} %collective-permute-done.odd, ...), custom_call_target="tpu_custom_call" | custom-call | tf_op jit(solution)/shard_map/aggregate_tiles/pallas_call | solution.py:152
  36.8 5.8 %collective-permute-start.3 = (bf16[4,128,512]{2,1,0:T(8,128)(2,1)S(1)}, bf16[4,128,512]{2,1,0:T(8,128)(2,1)S(1)}, u32[]{:S(2)}, u32[]{:S(2)}) collective-permute-start(bf16[4,128,512]{2,1,0:T(8,128)(2,1)S(1)} %get-tuple-element.25), channel_id=1, source_target_pairs={{0,1},{1,0},{2,3},{3,2},{4,5},{5,4},{6,7},{7,6},{8,9},{9,8},{10,11... | collective-permute-start | bytes 1572872 | tf_op jit(solution)/shard_map/ppermute | solution.py:63
  42.6 1.5 %collective-permute-done.3 = bf16[4,128,512]{2,1,0:T(8,128)(2,1)S(1)} collective-permute-done((bf16[4,128,512]{2,1,0:T(8,128)(2,1)S(1)}, bf16[4,128,512]{2,1,0:T(8,128)(2,1)S(1)}, u32[]{:S(2)}, u32[]{:S(2)}) %collective-permute-start.3) | collective-permute-done | bytes 524320 | tf_op jit(solution)/shard_map/ppermute | solution.py:63
  44.4 13.0 %all_to_all.25.parts = bf16[4,128,512]{2,1,0:T(8,128)(2,1)S(1)} all-to-all(bf16[4,128,512]{2,1,0:T(8,128)(2,1)S(1)} %add_convert_fusion), channel_id=1, replica_groups=mesh['y'=8,'z'=4,'pair'=2,'x'=4,'core'=2] {'x'}, dimensions={0} | all-to-all | bytes 1048576 | tf_op jit(solution)/shard_map/all_to_all | solution.py:67
  57.4 1.3 %dense_layer.1 = (bf16[128,512]{1,0:T(8,128)(2,1)}, bf16[4,128,512]{2,1,0:T(8,128)(2,1)}, bf16[128,512]{1,0:T(8,128)(2,1)S(1)}, bf16[128,512]{1,0:T(8,128)(2,1)S(1)}) custom-call(bf16[4,128,512]{2,1,0:T(8,128)(2,1)S(1)} %all_to_all.25.parts, bf16[512,512]{1,0:T(8,128)(2,1)S(1)} %copy-done.1, f32[1,512]{1,0:T(1,128)S(1)} %get-tuple-element.26.bias, ...), custom_call_target="tpu_custom_call" | custom-call | tf_op jit(solution)/shard_map/dense_layer/pallas_call | solution.py:197
  58.7 3.5 %all-to-all-start.2 = ((bf16[4,128,512]{2,1,0:T(8,128)(2,1)}), bf16[4,128,512]{2,1,0:T(8,128)(2,1)S(1)}, u32[]{:S(2)}, u32[]{:S(2)}) async-start(bf16[4,128,512]{2,1,0:T(8,128)(2,1)} %get-tuple-element.32), calls=%async_computation.2 | async-start | bytes 1048576 | tf_op jit(solution)/shard_map/all_to_all | solution.py:67
  62.6 3.7 %collective-permute-start.4 = (bf16[33,16,256]{2,1,0:T(8,128)(2,1)S(1)}, bf16[33,16,256]{2,1,0:T(8,128)(2,1)S(1)}, u32[]{:S(2)}, u32[]{:S(2)}) collective-permute-start(bf16[33,16,256]{2,1,0:T(8,128)(2,1)S(1)} %get-tuple-element.31), channel_id=1, source_target_pairs={{0,1},{1,0},{2,3},{3,2},{4,5},{5,4},{6,7},{7,6},{8,9},{9,8},{10,11... | collective-permute-start | bytes 811016 | tf_op jit(solution)/shard_map/ppermute | solution.py:63
  66.3 1.2 collective-permute-done.4.theirs
  67.4 0.8 chip_sum.1
  68.3 1.3 all-to-all-done.2.same
  69.5 3.9 %all-to-all-start.1 = ((bf16[32,16,384]{2,1,0:T(8,128)(2,1)}), bf16[32,16,384]{2,1,0:T(8,128)(2,1)S(1)}, u32[]{:S(2)}, u32[]{:S(2)}) async-start(bf16[32,16,384]{2,1,0:T(8,128)(2,1)} %chip_sum.1), calls=%async_computation.1 | async-start | bytes 786432 | tf_op jit(solution)/shard_map/all_to_all | solution.py:67
  73.4 4.9 %collective-permute-start.5 = (bf16[4,128,512]{2,1,0:T(8,128)(2,1)S(1)}, bf16[4,128,512]{2,1,0:T(8,128)(2,1)S(1)}, u32[]{:S(2)}, u32[]{:S(2)}) collective-permute-start(bf16[4,128,512]{2,1,0:T(8,128)(2,1)S(1)} %all-to-all-done.2.same), channel_id=1, source_target_pairs={{0,1},{1,0},{2,3},{3,2},{4,5},{5,4},{6,7},{7,6},{8,9},{9,8},{10,11... | collective-permute-start | bytes 1572872 | tf_op jit(solution)/shard_map/ppermute | solution.py:63
  78.4 1.5 %collective-permute-done.5.other = bf16[4,128,512]{2,1,0:T(8,128)(2,1)S(1)} collective-permute-done((bf16[4,128,512]{2,1,0:T(8,128)(2,1)S(1)}, bf16[4,128,512]{2,1,0:T(8,128)(2,1)S(1)}, u32[]{:S(2)}, u32[]{:S(2)}) %collective-permute-start.5) | collective-permute-done | bytes 524320 | tf_op jit(solution)/shard_map/ppermute | solution.py:63
  79.9 1.3 backward_tiles.1
  81.2 6.2 %collective-permute-start.6 = (bf16[3,128,512]{2,1,0:T(8,128)(2,1)S(1)}, bf16[3,128,512]{2,1,0:T(8,128)(2,1)S(1)}, u32[]{:S(2)}, u32[]{:S(2)}) collective-permute-start(bf16[3,128,512]{2,1,0:T(8,128)(2,1)S(1)} %get-tuple-element.33), channel_id=1, source_target_pairs={{0,504},{8,16},{16,8},{24,32},{32,24},{40,48},{48,40},{56,64},{64,... | collective-permute-start | bytes 1179656 | tf_op jit(solution)/shard_map/ppermute | solution.py:39
  87.5 10.8 %all_to_all.26.parts = bf16[8,16,384]{2,1,0:T(8,128)(2,1)S(1)} all-to-all(bf16[8,16,384]{2,1,0:T(8,128)(2,1)S(1)} %group_sum.1), channel_id=1, replica_groups=mesh['y'=8,'z'=4,'pair'=2,'x'=4,'core'=2] {'y'}, dimensions={0} | all-to-all | bytes 196608 | tf_op jit(solution)/shard_map/all_to_all | solution.py:67
  98.3 0.7 total_sum.1
  99.1 7.6 %all-to-all-start.4 = ((bf16[32,16,256]{2,1,0:T(8,128)(2,1)}), bf16[32,16,256]{2,1,0:T(8,128)(2,1)S(1)}, u32[]{:S(2)}, u32[]{:S(2)}) async-start(bf16[32,16,256]{2,1,0:T(8,128)(2,1)} %get-tuple-element.36), calls=%async_computation.4 | async-start | bytes 524288 | tf_op jit(solution)/shard_map/all_to_all | solution.py:67
  106.7 4.0 %collective-permute-start.8 = (bf16[2,128,512]{2,1,0:T(8,128)(2,1)S(1)}, bf16[2,128,512]{2,1,0:T(8,128)(2,1)S(1)}, u32[]{:S(2)}, u32[]{:S(2)}) collective-permute-start(bf16[2,128,512]{2,1,0:T(8,128)(2,1)S(1)} %relay_sum.1), channel_id=1, source_target_pairs={{0,16},{8,504},{16,32},{24,8},{32,48},{40,24},{48,64},{56,40},{64,... | collective-permute-start | bytes 786440 | tf_op jit(solution)/shard_map/ppermute | solution.py:39
  110.8 8.3 %collective-permute-done.8.skip = bf16[2,128,512]{2,1,0:T(8,128)(2,1)S(1)} collective-permute-done((bf16[2,128,512]{2,1,0:T(8,128)(2,1)S(1)}, bf16[2,128,512]{2,1,0:T(8,128)(2,1)S(1)}, u32[]{:S(2)}, u32[]{:S(2)}) %collective-permute-start.8) | collective-permute-done | bytes 262176 | tf_op jit(solution)/shard_map/ppermute | solution.py:39
  119.2 4.4 %collective-permute-start.9 = (bf16[128,512]{1,0:T(8,128)(2,1)S(1)}, bf16[128,512]{1,0:T(8,128)(2,1)S(1)}, u32[]{:S(2)}, u32[]{:S(2)}) collective-permute-start(bf16[128,512]{1,0:T(8,128)(2,1)S(1)} %get-tuple-element.41), channel_id=1, source_target_pairs={{0,8},{8,0},{16,24},{24,16},{32,40},{40,32},{48,56},{56,48},{64,72... | collective-permute-start | bytes 393224 | tf_op jit(solution)/shard_map/ppermute | solution.py:39
  123.6 4.3 %collective-permute-start.7 = (bf16[512,256]{1,0:T(8,128)(2,1)S(1)}, bf16[512,256]{1,0:T(8,128)(2,1)S(1)}, u32[]{:S(2)}, u32[]{:S(2)}) collective-permute-start(bf16[512,256]{1,0:T(8,128)(2,1)S(1)} %bitcast.27), channel_id=1, source_target_pairs={{0,1},{1,0},{2,3},{3,2},{4,5},{5,4},{6,7},{7,6},{8,9},{9,8},{10,11... | collective-permute-start | bytes 786440 | tf_op jit(solution)/shard_map/ppermute | solution.py:63
  127.9 0.7 add_convert_fusion.1
  129.1 1.0 join_halves.1
  (24 shorter events, 1.7 us)
Async XLA Ops:
  0.6 29.8 %copy-start = (bf16[1,1,16,128,128]{4,3,2,1,0:T(8,128)(2,1)S(1)}, bf16[1,1,16,128,128]{4,3,2,1,0:T(8,128)(2,1)}, u32[]{:S(2)}) copy-start(bf16[1,1,16,128,128]{4,3,2,1,0:T(8,128)(2,1)} %param.10) | copy-start | bytes 1572868
  7.0 17.5 %collective-permute-start.1 = (bf16[2,128,512]{2,1,0:T(8,128)(2,1)S(1)}, bf16[2,128,512]{2,1,0:T(8,128)(2,1)S(1)}, u32[]{:S(2)}, u32[]{:S(2)}) collective-permute-start(bf16[2,128,512]{2,1,0:T(8,128)(2,1)S(1)} %bitcast.24), channel_id=1, source_target_pairs={{0,496},{8,24},{16,0},{24,40},{32,16},{40,56},{48,32},{56,72},{64,... | collective-permute-start | bytes 786440 | tf_op jit(solution)/shard_map/ppermute | solution.py:39
  20.4 11.2 %collective-permute-start = (bf16[2,128,512]{2,1,0:T(8,128)(2,1)S(1)}, bf16[2,128,512]{2,1,0:T(8,128)(2,1)S(1)}, u32[]{:S(2)}, u32[]{:S(2)}) collective-permute-start(bf16[2,128,512]{2,1,0:T(8,128)(2,1)S(1)} %bitcast.25), channel_id=1, source_target_pairs={{0,504},{8,16},{16,8},{24,32},{32,24},{40,48},{48,40},{56,64},{64,... | collective-permute-start | bytes 786440 | tf_op jit(solution)/shard_map/ppermute | solution.py:39
  24.4 5.3 %copy-start.4 = (s32[1,1,16,2]{2,3,1,0:T(2,128)S(1)}, s32[1,1,16,2]{2,3,1,0:T(2,128)}, u32[]{:S(2)}) copy-start(s32[1,1,16,2]{2,3,1,0:T(2,128)} %param.11) | copy-start | bytes 388
  24.5 10.8 %collective-permute-start.2 = (bf16[1,128,512]{2,1,0:T(8,128)(2,1)S(1)}, bf16[1,128,512]{2,1,0:T(8,128)(2,1)S(1)}, u32[]{:S(2)}, u32[]{:S(2)}) collective-permute-start(bf16[1,128,512]{2,1,0:T(8,128)(2,1)S(1)} %pick_panel.1), channel_id=1, source_target_pairs={{0,504},{8,16},{16,8},{24,32},{32,24},{40,48},{48,40},{56,64},{64,... | collective-permute-start | bytes 393224 | tf_op jit(solution)/shard_map/ppermute | solution.py:39
  30.4 0.7 copy-start.3
  36.8 7.4 %collective-permute-start.3 = (bf16[4,128,512]{2,1,0:T(8,128)(2,1)S(1)}, bf16[4,128,512]{2,1,0:T(8,128)(2,1)S(1)}, u32[]{:S(2)}, u32[]{:S(2)}) collective-permute-start(bf16[4,128,512]{2,1,0:T(8,128)(2,1)S(1)} %get-tuple-element.25), channel_id=1, source_target_pairs={{0,1},{1,0},{2,3},{3,2},{4,5},{5,4},{6,7},{7,6},{8,9},{9,8},{10,11... | collective-permute-start | bytes 1572872 | tf_op jit(solution)/shard_map/ppermute | solution.py:63
  44.3 13.0 %copy-start.1 = (bf16[512,512]{1,0:T(8,128)(2,1)S(1)}, bf16[512,512]{1,0:T(8,128)(2,1)}, u32[]{:S(2)}) copy-start(bf16[512,512]{1,0:T(8,128)(2,1)} %weight.1) | copy-start | bytes 1572868
  44.4 13.0 %copy-start.2 = (bf16[128,512]{1,0:T(8,128)(2,1)S(1)}, bf16[128,512]{1,0:T(8,128)(2,1)}, u32[]{:S(2)}) copy-start(bf16[128,512]{1,0:T(8,128)(2,1)} %cot.1) | copy-start | bytes 393220
  58.7 10.8 %all-to-all-start.2 = ((bf16[4,128,512]{2,1,0:T(8,128)(2,1)}), bf16[4,128,512]{2,1,0:T(8,128)(2,1)S(1)}, u32[]{:S(2)}, u32[]{:S(2)}) async-start(bf16[4,128,512]{2,1,0:T(8,128)(2,1)} %get-tuple-element.32), calls=%async_computation.2 | async-start | bytes 1048576 | tf_op jit(solution)/shard_map/all_to_all | solution.py:67
  62.6 4.9 %collective-permute-start.4 = (bf16[33,16,256]{2,1,0:T(8,128)(2,1)S(1)}, bf16[33,16,256]{2,1,0:T(8,128)(2,1)S(1)}, u32[]{:S(2)}, u32[]{:S(2)}) collective-permute-start(bf16[33,16,256]{2,1,0:T(8,128)(2,1)S(1)} %get-tuple-element.31), channel_id=1, source_target_pairs={{0,1},{1,0},{2,3},{3,2},{4,5},{5,4},{6,7},{7,6},{8,9},{9,8},{10,11... | collective-permute-start | bytes 811016 | tf_op jit(solution)/shard_map/ppermute | solution.py:63
  69.5 17.9 %all-to-all-start.1 = ((bf16[32,16,384]{2,1,0:T(8,128)(2,1)}), bf16[32,16,384]{2,1,0:T(8,128)(2,1)S(1)}, u32[]{:S(2)}, u32[]{:S(2)}) async-start(bf16[32,16,384]{2,1,0:T(8,128)(2,1)} %chip_sum.1), calls=%async_computation.1 | async-start | bytes 786432 | tf_op jit(solution)/shard_map/all_to_all | solution.py:67
  73.4 6.5 %collective-permute-start.5 = (bf16[4,128,512]{2,1,0:T(8,128)(2,1)S(1)}, bf16[4,128,512]{2,1,0:T(8,128)(2,1)S(1)}, u32[]{:S(2)}, u32[]{:S(2)}) collective-permute-start(bf16[4,128,512]{2,1,0:T(8,128)(2,1)S(1)} %all-to-all-done.2.same), channel_id=1, source_target_pairs={{0,1},{1,0},{2,3},{3,2},{4,5},{5,4},{6,7},{7,6},{8,9},{9,8},{10,11... | collective-permute-start | bytes 1572872 | tf_op jit(solution)/shard_map/ppermute | solution.py:63
  81.2 17.1 %collective-permute-start.6 = (bf16[3,128,512]{2,1,0:T(8,128)(2,1)S(1)}, bf16[3,128,512]{2,1,0:T(8,128)(2,1)S(1)}, u32[]{:S(2)}, u32[]{:S(2)}) collective-permute-start(bf16[3,128,512]{2,1,0:T(8,128)(2,1)S(1)} %get-tuple-element.33), channel_id=1, source_target_pairs={{0,504},{8,16},{16,8},{24,32},{32,24},{40,48},{48,40},{56,64},{64,... | collective-permute-start | bytes 1179656 | tf_op jit(solution)/shard_map/ppermute | solution.py:39
  99.1 24.5 %all-to-all-start.4 = ((bf16[32,16,256]{2,1,0:T(8,128)(2,1)}), bf16[32,16,256]{2,1,0:T(8,128)(2,1)S(1)}, u32[]{:S(2)}, u32[]{:S(2)}) async-start(bf16[32,16,256]{2,1,0:T(8,128)(2,1)} %get-tuple-element.36), calls=%async_computation.4 | async-start | bytes 524288 | tf_op jit(solution)/shard_map/all_to_all | solution.py:67
  106.7 12.4 %collective-permute-start.8 = (bf16[2,128,512]{2,1,0:T(8,128)(2,1)S(1)}, bf16[2,128,512]{2,1,0:T(8,128)(2,1)S(1)}, u32[]{:S(2)}, u32[]{:S(2)}) collective-permute-start(bf16[2,128,512]{2,1,0:T(8,128)(2,1)S(1)} %relay_sum.1), channel_id=1, source_target_pairs={{0,16},{8,504},{16,32},{24,8},{32,48},{40,24},{48,64},{56,40},{64,... | collective-permute-start | bytes 786440 | tf_op jit(solution)/shard_map/ppermute | solution.py:39
  119.2 8.7 %collective-permute-start.9 = (bf16[128,512]{1,0:T(8,128)(2,1)S(1)}, bf16[128,512]{1,0:T(8,128)(2,1)S(1)}, u32[]{:S(2)}, u32[]{:S(2)}) collective-permute-start(bf16[128,512]{1,0:T(8,128)(2,1)S(1)} %get-tuple-element.41), channel_id=1, source_target_pairs={{0,8},{8,0},{16,24},{24,16},{32,40},{40,32},{48,56},{56,48},{64,72... | collective-permute-start | bytes 393224 | tf_op jit(solution)/shard_map/ppermute | solution.py:39
  123.6 5.5 %collective-permute-start.7 = (bf16[512,256]{1,0:T(8,128)(2,1)S(1)}, bf16[512,256]{1,0:T(8,128)(2,1)S(1)}, u32[]{:S(2)}, u32[]{:S(2)}) collective-permute-start(bf16[512,256]{1,0:T(8,128)(2,1)S(1)} %bitcast.27), channel_id=1, source_target_pairs={{0,1},{1,0},{2,3},{3,2},{4,5},{5,4},{6,7},{7,6},{8,9},{9,8},{10,11... | collective-permute-start | bytes 786440 | tf_op jit(solution)/shard_map/ppermute | solution.py:63

commit v7 on v5

--- a/solution.py
+++ b/solution.py
@@ -240,15 +240,14 @@
     )(mine, theirs)
 
 
-def backward_kernel(meta, tiles, same, other, own, odd, skip, panels, acc, sems):
-    copies = copy_in([same, other], [panels.at[0:4], panels.at[4:8]], sems)
+def backward_kernel(meta, tiles, same, other, own, odd, skip, acc):
     acc[...] = jnp.zeros_like(acc)
-    for c in copies:
-        c.wait()
 
     def product(s):
+        b = meta[s]
+        panel = lax.select(b < BANDS // 2, same[b & 3], other[b & 3])
         return lax.dot_general(
-            tiles[s], panels[meta[s]], (((0,), (0,)), ((), ())), preferred_element_type=F32
+            tiles[s], panel, (((0,), (0,)), ((), ())), preferred_element_type=F32
         )
 
     def add(s, value):
@@ -269,12 +268,10 @@
             jax.ShapeDtypeStruct((3, TILE, FEAT), BF16),
             jax.ShapeDtypeStruct((2, TILE, FEAT), F32),
         ),
-        in_specs=[SMEM_SPEC, VMEM_SPEC] + [ANY_SPEC] * 2,
+        in_specs=[SMEM_SPEC] + [VMEM_SPEC] * 3,
         out_specs=(VMEM_SPEC,) * 3,
         scratch_shapes=[
-            pltpu.VMEM((BANDS, TILE, FEAT), BF16),
             pltpu.VMEM((WINDOW, TILE, FEAT), F32),
-            pltpu.SemaphoreType.DMA((2,)),
         ],
         compiler_params=params(),
         name="backward_tiles",

time: 130 us -> 131 us (level)
    ppermute x6, starting transfers between devices: 35.6 us -> 34.3 us  [moved(): lax.ppermute(block, ROW, [(i, target(i) % size) for i in range(size)])]
where the time goes in v7:
time: 131 us; the launch traced here: 130 us
  starting transfers between devices  66.8 us (51%)
  blocking collectives  31.7 us (24%)
  waiting for transfers between devices  20.4 us (16%)
  Pallas kernels  7.26 us (6%)
  other arithmetic  1.66 us (1%)
  between operations  1.53 us (1%)
    ppermute x6, starting transfers between devices, moved(): lax.ppermute(block, ROW, [(i, target(i) % size) for i in range(size)])  34.3 us
    all_to_all x2, blocking collectives, exchange(): return lax.all_to_all(chunks, axis, 0, 0, tiled=True)  25.4 us
    ppermute x4, starting transfers between devices, swapped(): return lax.ppermute(block, 'core', [(0, 1), (1, 0)])  18.4 us
    all_to_all x3, starting transfers between devices, exchange(): return lax.all_to_all(chunks, axis, 0, 0, tiled=True)  14.1 us
    ppermute x6, waiting for transfers between devices, moved(): lax.ppermute(block, ROW, [(i, target(i) % size) for i in range(size)])  14.1 us
    all_gather x1, blocking collectives, body(): own = lax.all_gather(features, PAIR, axis=0, tiled=False)  6.34 us
    ppermute x4, waiting for transfers between devices, swapped(): return lax.ppermute(block, 'core', [(0, 1), (1, 0)])  4.63 us
  transfers between devices with their start and end apart: 13, of which 9 were waited for; matrix products, arithmetic and copies ran while one was open for 1% of the time, Pallas kernels for 2%

profile of v7, /device:TPU:1, one launch (start us, length us, event | category | flops | bytes accessed | tf_op | source)
XLA Modules:
  0.0 130.0 jit_solution(7564165667880102367)
XLA Ops:
  0.6 6.3 %all-gather = bf16[256,512]{1,0:T(8,128)(2,1)S(1)} all-gather(bf16[128,512]{1,0:T(8,128)(2,1)} %param.7), channel_id=2, replica_groups=mesh['y'=8,'z'=4,'pair'=2,'x'=4,'core'=2] {'pair'}, dimensions={0}, use_global_device_ids=true | all-gather | bytes 393216 | tf_op jit(solution)/shard_map/all_gather | solution.py:414
  7.0 13.4 %collective-permute-start.1 = (bf16[2,128,512]{2,1,0:T(8,128)(2,1)S(1)}, bf16[2,128,512]{2,1,0:T(8,128)(2,1)S(1)}, u32[]{:S(2)}, u32[]{:S(2)}) collective-permute-start(bf16[2,128,512]{2,1,0:T(8,128)(2,1)S(1)} %bitcast.24), channel_id=1, source_target_pairs={{0,496},{8,24},{16,0},{24,40},{32,16},{40,56},{48,32},{56,72},{64,... | collective-permute-start | bytes 786440 | tf_op jit(solution)/shard_map/ppermute | solution.py:39
  20.4 1.9 %collective-permute-start = (bf16[2,128,512]{2,1,0:T(8,128)(2,1)S(1)}, bf16[2,128,512]{2,1,0:T(8,128)(2,1)S(1)}, u32[]{:S(2)}, u32[]{:S(2)}) collective-permute-start(bf16[2,128,512]{2,1,0:T(8,128)(2,1)S(1)} %bitcast.25), channel_id=1, source_target_pairs={{0,504},{8,16},{16,8},{24,32},{32,24},{40,48},{48,40},{56,64},{64,... | collective-permute-start | bytes 786440 | tf_op jit(solution)/shard_map/ppermute | solution.py:39
  22.4 0.7 add_bitcast_fusion
  23.1 1.4 %collective-permute-done.1.skip = bf16[2,128,512]{2,1,0:T(8,128)(2,1)S(1)} collective-permute-done((bf16[2,128,512]{2,1,0:T(8,128)(2,1)S(1)}, bf16[2,128,512]{2,1,0:T(8,128)(2,1)S(1)}, u32[]{:S(2)}, u32[]{:S(2)}) %collective-permute-start.1) | collective-permute-done | bytes 262176 | tf_op jit(solution)/shard_map/ppermute | solution.py:39
  24.5 5.3 %collective-permute-start.2 = (bf16[1,128,512]{2,1,0:T(8,128)(2,1)S(1)}, bf16[1,128,512]{2,1,0:T(8,128)(2,1)S(1)}, u32[]{:S(2)}, u32[]{:S(2)}) collective-permute-start(bf16[1,128,512]{2,1,0:T(8,128)(2,1)S(1)} %pick_panel.1), channel_id=1, source_target_pairs={{0,504},{8,16},{16,8},{24,32},{32,24},{40,48},{48,40},{56,64},{64,... | collective-permute-start | bytes 393224 | tf_op jit(solution)/shard_map/ppermute | solution.py:39
  30.5 0.7 copy-done.3
  31.6 3.7 %collective-permute-done.2.far = bf16[1,128,512]{2,1,0:T(8,128)(2,1)S(1)} collective-permute-done((bf16[1,128,512]{2,1,0:T(8,128)(2,1)S(1)}, bf16[1,128,512]{2,1,0:T(8,128)(2,1)S(1)}, u32[]{:S(2)}, u32[]{:S(2)}) %collective-permute-start.2) | collective-permute-done | bytes 131104 | tf_op jit(solution)/shard_map/ppermute | solution.py:39
  35.3 1.6 %aggregate_tiles.1 = (f32[4,128,512]{2,1,0:T(8,128)S(1)}, bf16[4,128,512]{2,1,0:T(8,128)(2,1)S(1)}) custom-call(s32[33]{0:T(128)S(1)} %pad_add_fusion.meta, bf16[16,128,128]{2,1,0:T(8,128)(2,1)S(1)} %get-tuple-element.21.tiles, bf16[2,128,512]{2,1,0:T(8,128)(2,1)S(1)} %bitcast.26, bf16[2,128,512]{2,1,0:T(8,128)(2,1)S(1)} %collective-permute-done.odd, ...), custom_call_target="tpu_custom_call" | custom-call | tf_op jit(solution)/shard_map/aggregate_tiles/pallas_call | solution.py:152
  36.9 5.5 %collective-permute-start.3 = (bf16[4,128,512]{2,1,0:T(8,128)(2,1)S(1)}, bf16[4,128,512]{2,1,0:T(8,128)(2,1)S(1)}, u32[]{:S(2)}, u32[]{:S(2)}) collective-permute-start(bf16[4,128,512]{2,1,0:T(8,128)(2,1)S(1)} %get-tuple-element.23), channel_id=1, source_target_pairs={{0,1},{1,0},{2,3},{3,2},{4,5},{5,4},{6,7},{7,6},{8,9},{9,8},{10,11... | collective-permute-start | bytes 1572872 | tf_op jit(solution)/shard_map/ppermute | solution.py:63
  42.5 1.5 %collective-permute-done.3 = bf16[4,128,512]{2,1,0:T(8,128)(2,1)S(1)} collective-permute-done((bf16[4,128,512]{2,1,0:T(8,128)(2,1)S(1)}, bf16[4,128,512]{2,1,0:T(8,128)(2,1)S(1)}, u32[]{:S(2)}, u32[]{:S(2)}) %collective-permute-start.3) | collective-permute-done | bytes 524320 | tf_op jit(solution)/shard_map/ppermute | solution.py:63
  44.2 13.4 %all_to_all.25.parts = bf16[4,128,512]{2,1,0:T(8,128)(2,1)S(1)} all-to-all(bf16[4,128,512]{2,1,0:T(8,128)(2,1)S(1)} %add_convert_fusion), channel_id=1, replica_groups=mesh['y'=8,'z'=4,'pair'=2,'x'=4,'core'=2] {'x'}, dimensions={0} | all-to-all | bytes 1048576 | tf_op jit(solution)/shard_map/all_to_all | solution.py:67
  57.6 1.4 %dense_layer.1 = (bf16[128,512]{1,0:T(8,128)(2,1)}, bf16[4,128,512]{2,1,0:T(8,128)(2,1)}, f32[33,16,256]{2,1,0:T(8,128)S(1)}, bf16[33,16,256]{2,1,0:T(8,128)(2,1)S(1)}) custom-call(s32[1]{0:T(128)} %bitcast.core, bf16[4,128,512]{2,1,0:T(8,128)(2,1)S(1)} %all_to_all.25.parts, bf16[512,512]{1,0:T(8,128)(2,1)S(1)} %copy-done.1, ...), custom_call_target="tpu_custom_call" | custom-call | tf_op jit(solution)/shard_map/dense_layer/pallas_call | solution.py:207
  59.0 3.5 %all-to-all-start.2 = ((bf16[4,128,512]{2,1,0:T(8,128)(2,1)}), bf16[4,128,512]{2,1,0:T(8,128)(2,1)S(1)}, u32[]{:S(2)}, u32[]{:S(2)}) async-start(bf16[4,128,512]{2,1,0:T(8,128)(2,1)} %get-tuple-element.28), calls=%async_computation.2 | async-start | bytes 1048576 | tf_op jit(solution)/shard_map/all_to_all | solution.py:67
  62.5 3.7 %collective-permute-start.4 = (bf16[33,16,256]{2,1,0:T(8,128)(2,1)S(1)}, bf16[33,16,256]{2,1,0:T(8,128)(2,1)S(1)}, u32[]{:S(2)}, u32[]{:S(2)}) collective-permute-start(bf16[33,16,256]{2,1,0:T(8,128)(2,1)S(1)} %get-tuple-element.27), channel_id=1, source_target_pairs={{0,1},{1,0},{2,3},{3,2},{4,5},{5,4},{6,7},{7,6},{8,9},{9,8},{10,11... | collective-permute-start | bytes 811016 | tf_op jit(solution)/shard_map/ppermute | solution.py:63
  66.2 1.2 collective-permute-done.4.theirs
  67.4 0.8 chip_sum.1
  68.2 1.7 %all-to-all-done.2.same = bf16[4,128,512]{2,1,0:T(8,128)(2,1)S(1)} async-done(((bf16[4,128,512]{2,1,0:T(8,128)(2,1)}), bf16[4,128,512]{2,1,0:T(8,128)(2,1)S(1)}, u32[]{:S(2)}, u32[]{:S(2)}) %all-to-all-start.2) | async-done | bytes 524320 | tf_op jit(solution)/shard_map/all_to_all | solution.py:67
  69.8 3.9 %all-to-all-start.1 = ((bf16[32,16,384]{2,1,0:T(8,128)(2,1)}), bf16[32,16,384]{2,1,0:T(8,128)(2,1)S(1)}, u32[]{:S(2)}, u32[]{:S(2)}) async-start(bf16[32,16,384]{2,1,0:T(8,128)(2,1)} %chip_sum.1), calls=%async_computation.1 | async-start | bytes 786432 | tf_op jit(solution)/shard_map/all_to_all | solution.py:67
  73.7 4.9 %collective-permute-start.5 = (bf16[4,128,512]{2,1,0:T(8,128)(2,1)S(1)}, bf16[4,128,512]{2,1,0:T(8,128)(2,1)S(1)}, u32[]{:S(2)}, u32[]{:S(2)}) collective-permute-start(bf16[4,128,512]{2,1,0:T(8,128)(2,1)S(1)} %all-to-all-done.2.same), channel_id=1, source_target_pairs={{0,1},{1,0},{2,3},{3,2},{4,5},{5,4},{6,7},{7,6},{8,9},{9,8},{10,11... | collective-permute-start | bytes 1572872 | tf_op jit(solution)/shard_map/ppermute | solution.py:63
  78.7 1.5 %collective-permute-done.5.other = bf16[4,128,512]{2,1,0:T(8,128)(2,1)S(1)} collective-permute-done((bf16[4,128,512]{2,1,0:T(8,128)(2,1)S(1)}, bf16[4,128,512]{2,1,0:T(8,128)(2,1)S(1)}, u32[]{:S(2)}, u32[]{:S(2)}) %collective-permute-start.5) | collective-permute-done | bytes 524320 | tf_op jit(solution)/shard_map/ppermute | solution.py:63
  80.2 1.4 %backward_tiles.1 = (f32[2,128,512]{2,1,0:T(8,128)S(1)}, bf16[3,128,512]{2,1,0:T(8,128)(2,1)S(1)}, f32[2,128,512]{2,1,0:T(8,128)S(1)}) custom-call(s32[33]{0:T(128)S(1)} %pad_add_fusion.meta, bf16[16,128,128]{2,1,0:T(8,128)(2,1)S(1)} %get-tuple-element.21.tiles, bf16[4,128,512]{2,1,0:T(8,128)(2,1)S(1)} %all-to-all-done.2.same, ...), custom_call_target="tpu_custom_call" | custom-call | tf_op jit(solution)/shard_map/backward_tiles/pallas_call | solution.py:264
  81.6 5.5 %collective-permute-start.6 = (bf16[3,128,512]{2,1,0:T(8,128)(2,1)S(1)}, bf16[3,128,512]{2,1,0:T(8,128)(2,1)S(1)}, u32[]{:S(2)}, u32[]{:S(2)}) collective-permute-start(bf16[3,128,512]{2,1,0:T(8,128)(2,1)S(1)} %get-tuple-element.29), channel_id=1, source_target_pairs={{0,504},{8,16},{16,8},{24,32},{32,24},{40,48},{48,40},{56,64},{64,... | collective-permute-start | bytes 1179656 | tf_op jit(solution)/shard_map/ppermute | solution.py:39
  87.2 11.9 %all_to_all.26.parts = bf16[8,16,384]{2,1,0:T(8,128)(2,1)S(1)} all-to-all(bf16[8,16,384]{2,1,0:T(8,128)(2,1)S(1)} %group_sum.1), channel_id=1, replica_groups=mesh['y'=8,'z'=4,'pair'=2,'x'=4,'core'=2] {'y'}, dimensions={0} | all-to-all | bytes 196608 | tf_op jit(solution)/shard_map/all_to_all | solution.py:67
  99.1 0.7 total_sum.1
  99.8 6.8 %all-to-all-start.4 = ((bf16[32,16,256]{2,1,0:T(8,128)(2,1)}), bf16[32,16,256]{2,1,0:T(8,128)(2,1)S(1)}, u32[]{:S(2)}, u32[]{:S(2)}) async-start(bf16[32,16,256]{2,1,0:T(8,128)(2,1)} %get-tuple-element.32), calls=%async_computation.4 | async-start | bytes 524288 | tf_op jit(solution)/shard_map/all_to_all | solution.py:67
  106.6 4.0 %collective-permute-start.8 = (bf16[2,128,512]{2,1,0:T(8,128)(2,1)S(1)}, bf16[2,128,512]{2,1,0:T(8,128)(2,1)S(1)}, u32[]{:S(2)}, u32[]{:S(2)}) collective-permute-start(bf16[2,128,512]{2,1,0:T(8,128)(2,1)S(1)} %relay_sum.1), channel_id=1, source_target_pairs={{0,16},{8,504},{16,32},{24,8},{32,48},{40,24},{48,64},{56,40},{64,... | collective-permute-start | bytes 786440 | tf_op jit(solution)/shard_map/ppermute | solution.py:39
  110.7 8.7 %collective-permute-done.8.skip = bf16[2,128,512]{2,1,0:T(8,128)(2,1)S(1)} collective-permute-done((bf16[2,128,512]{2,1,0:T(8,128)(2,1)S(1)}, bf16[2,128,512]{2,1,0:T(8,128)(2,1)S(1)}, u32[]{:S(2)}, u32[]{:S(2)}) %collective-permute-start.8) | collective-permute-done | bytes 262176 | tf_op jit(solution)/shard_map/ppermute | solution.py:39
  119.5 4.1 %collective-permute-start.9 = (bf16[128,512]{1,0:T(8,128)(2,1)S(1)}, bf16[128,512]{1,0:T(8,128)(2,1)S(1)}, u32[]{:S(2)}, u32[]{:S(2)}) collective-permute-start(bf16[128,512]{1,0:T(8,128)(2,1)S(1)} %get-tuple-element.37), channel_id=1, source_target_pairs={{0,8},{8,0},{16,24},{24,16},{32,40},{40,32},{48,56},{56,48},{64,72... | collective-permute-start | bytes 393224 | tf_op jit(solution)/shard_map/ppermute | solution.py:39
  123.6 4.2 %collective-permute-start.7 = (bf16[512,256]{1,0:T(8,128)(2,1)S(1)}, bf16[512,256]{1,0:T(8,128)(2,1)S(1)}, u32[]{:S(2)}, u32[]{:S(2)}) collective-permute-start(bf16[512,256]{1,0:T(8,128)(2,1)S(1)} %bitcast.27), channel_id=1, source_target_pairs={{0,1},{1,0},{2,3},{3,2},{4,5},{5,4},{6,7},{7,6},{8,9},{9,8},{10,11... | collective-permute-start | bytes 786440 | tf_op jit(solution)/shard_map/ppermute | solution.py:63
  127.8 0.7 add_convert_fusion.1
  128.9 1.0 join_halves.1
  (23 shorter events, 1.4 us)
Async XLA Ops:
  0.6 29.8 %copy-start = (bf16[1,1,16,128,128]{4,3,2,1,0:T(8,128)(2,1)S(1)}, bf16[1,1,16,128,128]{4,3,2,1,0:T(8,128)(2,1)}, u32[]{:S(2)}) copy-start(bf16[1,1,16,128,128]{4,3,2,1,0:T(8,128)(2,1)} %param.10) | copy-start | bytes 1572868
  7.0 17.5 %collective-permute-start.1 = (bf16[2,128,512]{2,1,0:T(8,128)(2,1)S(1)}, bf16[2,128,512]{2,1,0:T(8,128)(2,1)S(1)}, u32[]{:S(2)}, u32[]{:S(2)}) collective-permute-start(bf16[2,128,512]{2,1,0:T(8,128)(2,1)S(1)} %bitcast.24), channel_id=1, source_target_pairs={{0,496},{8,24},{16,0},{24,40},{32,16},{40,56},{48,32},{56,72},{64,... | collective-permute-start | bytes 786440 | tf_op jit(solution)/shard_map/ppermute | solution.py:39
  20.4 11.2 %collective-permute-start = (bf16[2,128,512]{2,1,0:T(8,128)(2,1)S(1)}, bf16[2,128,512]{2,1,0:T(8,128)(2,1)S(1)}, u32[]{:S(2)}, u32[]{:S(2)}) collective-permute-start(bf16[2,128,512]{2,1,0:T(8,128)(2,1)S(1)} %bitcast.25), channel_id=1, source_target_pairs={{0,504},{8,16},{16,8},{24,32},{32,24},{40,48},{48,40},{56,64},{64,... | collective-permute-start | bytes 786440 | tf_op jit(solution)/shard_map/ppermute | solution.py:39
  24.4 5.3 %copy-start.4 = (s32[1,1,16,2]{2,3,1,0:T(2,128)S(1)}, s32[1,1,16,2]{2,3,1,0:T(2,128)}, u32[]{:S(2)}) copy-start(s32[1,1,16,2]{2,3,1,0:T(2,128)} %param.11) | copy-start | bytes 388
  24.5 10.8 %collective-permute-start.2 = (bf16[1,128,512]{2,1,0:T(8,128)(2,1)S(1)}, bf16[1,128,512]{2,1,0:T(8,128)(2,1)S(1)}, u32[]{:S(2)}, u32[]{:S(2)}) collective-permute-start(bf16[1,128,512]{2,1,0:T(8,128)(2,1)S(1)} %pick_panel.1), channel_id=1, source_target_pairs={{0,504},{8,16},{16,8},{24,32},{32,24},{40,48},{48,40},{56,64},{64,... | collective-permute-start | bytes 393224 | tf_op jit(solution)/shard_map/ppermute | solution.py:39
  30.4 0.7 copy-start.3
  36.9 7.1 %collective-permute-start.3 = (bf16[4,128,512]{2,1,0:T(8,128)(2,1)S(1)}, bf16[4,128,512]{2,1,0:T(8,128)(2,1)S(1)}, u32[]{:S(2)}, u32[]{:S(2)}) collective-permute-start(bf16[4,128,512]{2,1,0:T(8,128)(2,1)S(1)} %get-tuple-element.23), channel_id=1, source_target_pairs={{0,1},{1,0},{2,3},{3,2},{4,5},{5,4},{6,7},{7,6},{8,9},{9,8},{10,11... | collective-permute-start | bytes 1572872 | tf_op jit(solution)/shard_map/ppermute | solution.py:63
  44.2 13.5 %copy-start.1 = (bf16[512,512]{1,0:T(8,128)(2,1)S(1)}, bf16[512,512]{1,0:T(8,128)(2,1)}, u32[]{:S(2)}) copy-start(bf16[512,512]{1,0:T(8,128)(2,1)} %weight.1) | copy-start | bytes 1572868
  44.2 13.4 %copy-start.2 = (bf16[128,512]{1,0:T(8,128)(2,1)S(1)}, bf16[128,512]{1,0:T(8,128)(2,1)}, u32[]{:S(2)}) copy-start(bf16[128,512]{1,0:T(8,128)(2,1)} %cot.1) | copy-start | bytes 393220
  59.0 10.8 %all-to-all-start.2 = ((bf16[4,128,512]{2,1,0:T(8,128)(2,1)}), bf16[4,128,512]{2,1,0:T(8,128)(2,1)S(1)}, u32[]{:S(2)}, u32[]{:S(2)}) async-start(bf16[4,128,512]{2,1,0:T(8,128)(2,1)} %get-tuple-element.28), calls=%async_computation.2 | async-start | bytes 1048576 | tf_op jit(solution)/shard_map/all_to_all | solution.py:67
  62.5 4.9 %collective-permute-start.4 = (bf16[33,16,256]{2,1,0:T(8,128)(2,1)S(1)}, bf16[33,16,256]{2,1,0:T(8,128)(2,1)S(1)}, u32[]{:S(2)}, u32[]{:S(2)}) collective-permute-start(bf16[33,16,256]{2,1,0:T(8,128)(2,1)S(1)} %get-tuple-element.27), channel_id=1, source_target_pairs={{0,1},{1,0},{2,3},{3,2},{4,5},{5,4},{6,7},{7,6},{8,9},{9,8},{10,11... | collective-permute-start | bytes 811016 | tf_op jit(solution)/shard_map/ppermute | solution.py:63
  69.8 17.3 %all-to-all-start.1 = ((bf16[32,16,384]{2,1,0:T(8,128)(2,1)}), bf16[32,16,384]{2,1,0:T(8,128)(2,1)S(1)}, u32[]{:S(2)}, u32[]{:S(2)}) async-start(bf16[32,16,384]{2,1,0:T(8,128)(2,1)} %chip_sum.1), calls=%async_computation.1 | async-start | bytes 786432 | tf_op jit(solution)/shard_map/all_to_all | solution.py:67
  73.7 6.5 %collective-permute-start.5 = (bf16[4,128,512]{2,1,0:T(8,128)(2,1)S(1)}, bf16[4,128,512]{2,1,0:T(8,128)(2,1)S(1)}, u32[]{:S(2)}, u32[]{:S(2)}) collective-permute-start(bf16[4,128,512]{2,1,0:T(8,128)(2,1)S(1)} %all-to-all-done.2.same), channel_id=1, source_target_pairs={{0,1},{1,0},{2,3},{3,2},{4,5},{5,4},{6,7},{7,6},{8,9},{9,8},{10,11... | collective-permute-start | bytes 1572872 | tf_op jit(solution)/shard_map/ppermute | solution.py:63
  81.6 17.5 %collective-permute-start.6 = (bf16[3,128,512]{2,1,0:T(8,128)(2,1)S(1)}, bf16[3,128,512]{2,1,0:T(8,128)(2,1)S(1)}, u32[]{:S(2)}, u32[]{:S(2)}) collective-permute-start(bf16[3,128,512]{2,1,0:T(8,128)(2,1)S(1)} %get-tuple-element.29), channel_id=1, source_target_pairs={{0,504},{8,16},{16,8},{24,32},{32,24},{40,48},{48,40},{56,64},{64,... | collective-permute-start | bytes 1179656 | tf_op jit(solution)/shard_map/ppermute | solution.py:39
  99.8 23.8 %all-to-all-start.4 = ((bf16[32,16,256]{2,1,0:T(8,128)(2,1)}), bf16[32,16,256]{2,1,0:T(8,128)(2,1)S(1)}, u32[]{:S(2)}, u32[]{:S(2)}) async-start(bf16[32,16,256]{2,1,0:T(8,128)(2,1)} %get-tuple-element.32), calls=%async_computation.4 | async-start | bytes 524288 | tf_op jit(solution)/shard_map/all_to_all | solution.py:67
  106.6 12.7 %collective-permute-start.8 = (bf16[2,128,512]{2,1,0:T(8,128)(2,1)S(1)}, bf16[2,128,512]{2,1,0:T(8,128)(2,1)S(1)}, u32[]{:S(2)}, u32[]{:S(2)}) collective-permute-start(bf16[2,128,512]{2,1,0:T(8,128)(2,1)S(1)} %relay_sum.1), channel_id=1, source_target_pairs={{0,16},{8,504},{16,32},{24,8},{32,48},{40,24},{48,64},{56,40},{64,... | collective-permute-start | bytes 786440 | tf_op jit(solution)/shard_map/ppermute | solution.py:39
  119.5 8.3 %collective-permute-start.9 = (bf16[128,512]{1,0:T(8,128)(2,1)S(1)}, bf16[128,512]{1,0:T(8,128)(2,1)S(1)}, u32[]{:S(2)}, u32[]{:S(2)}) collective-permute-start(bf16[128,512]{1,0:T(8,128)(2,1)S(1)} %get-tuple-element.37), channel_id=1, source_target_pairs={{0,8},{8,0},{16,24},{24,16},{32,40},{40,32},{48,56},{56,48},{64,72... | collective-permute-start | bytes 393224 | tf_op jit(solution)/shard_map/ppermute | solution.py:39
  123.6 5.3 %collective-permute-start.7 = (bf16[512,256]{1,0:T(8,128)(2,1)S(1)}, bf16[512,256]{1,0:T(8,128)(2,1)S(1)}, u32[]{:S(2)}, u32[]{:S(2)}) collective-permute-start(bf16[512,256]{1,0:T(8,128)(2,1)S(1)} %bitcast.27), channel_id=1, source_target_pairs={{0,1},{1,0},{2,3},{3,2},{4,5},{5,4},{6,7},{7,6},{8,9},{9,8},{10,11... | collective-permute-start | bytes 786440 | tf_op jit(solution)/shard_map/ppermute | solution.py:63
